TPU v7x, 512 devices: a whole 4x8x8 slice. The times are simulated.
512 devices in a mesh: front: 4 (over x), helper: 128 (over y, z, core).
Axes of the slice: x: 4, y: 8, z: 8, core: 2. Of those that a mesh axis runs over, the one named last changes fastest.
Arguments:
- lower_panel: bfloat16 [8192, 2048], P(('front', 'helper')), parts along dimension 0, may hold values from -0.125 to 0.125
- pivot_inverse: bfloat16 [64, 128, 128], P('front'), parts along dimension 0
- lower_rows: bfloat16 [131072, 2048], P(('front', 'helper')), parts along dimension 0, may hold values from -1 to 1
- window_block: bfloat16 [131072, 512], P(('front', 'helper')), parts along dimension 0, may hold values from -6 to 6
- block_count: int32 [512], P(('front', 'helper')), parts along dimension 0, may hold values from 1 to 2, as said below
- parent_slot: int32 [131072], P(('front', 'helper')), parts along dimension 0, may hold values from 0 to 16383, as said below
Outputs:
- factor_rows: bfloat16 [131072, 2048], P(('front', 'helper')), parts along dimension 0
- parent_block: float32 [65536, 512], P(('front', 'helper')), parts along dimension 0
There are 4 independent parts, one for each index of `front`. A program takes and returns all parts, laid end to end along the dimension named above; each array names one. Nothing has to cross between parts.
Inputs may be any that keep to these rules, and one draw needn't show every extreme that they name: `block_count`: each helper holds 1 to 2 blocks; some helper holds 2. Owner is parent_slot // 128. The 256 slots of one helper name each owner at most 2 times; in every draw one owner is named by the first 2 slots of every helper.
All inputs are finite; a program needn't handle non-finite values.
Results may differ from a plain program's by a relative error of at most 0.0062.
Values may be sent and summed in bfloat16 or wider, within the bound.
No kernel may reach another device: no remote copies, remote signals or barrier semaphores. Data moves between devices by JAX's collectives and lax.ppermute only.
A program may use at most 64 MiB of HBM per device.

v0:
```python
import jax
import jax.numpy as jnp
from jax import lax
from jax.sharding import PartitionSpec as P

UNIT = 128
SR = 4
PROWS = 128


def solve_rows(row_block, pivot_panel, inverse):
    count_blocks = inverse.shape[0]
    block_width = inverse.shape[1]
    pieces = []
    for block_index in range(count_blocks):
        column_start = block_index * block_width
        current = row_block[:, column_start : column_start + block_width].astype(jnp.float32)
        if block_index > 0:
            earlier = jnp.concatenate(pieces, axis=1)
            current = current - lax.dot_general(
                earlier,
                pivot_panel[column_start : column_start + block_width, :column_start],
                (((1,), (1,)), ((), ())),
                preferred_element_type=jnp.float32,
            )
        pieces.append(current.astype(jnp.bfloat16))
    solved = jnp.concatenate(pieces, axis=1)
    shaped = solved.reshape(solved.shape[0], count_blocks, block_width)
    factor = jnp.einsum("rkb,kbc->rkc", shaped, inverse, preferred_element_type=jnp.float32)
    return (solved, factor.reshape(solved.shape).astype(jnp.bfloat16))


def per_device(lower_panel, pivot_inverse, lower_rows, window_block, block_count, parent_slot):
    pivot_panel = lax.all_gather(lower_panel, "helper", axis=0, tiled=True)
    row_total = lower_rows.shape[0]
    live_rows = jnp.arange(row_total) < UNIT * block_count[0]
    solved, factor = solve_rows(lower_rows, pivot_panel, pivot_inverse)
    window_rows = lax.all_gather(factor[:SR], "helper", axis=0, tiled=True)
    factor = jnp.where(live_rows[:, None], factor, jnp.zeros_like(factor))
    product = lax.dot_general(
        solved, window_rows, (((1,), (1,)), ((), ())), preferred_element_type=jnp.float32
    )
    contribution = (window_block.astype(jnp.float32) - product).astype(jnp.bfloat16)
    helpers = lax.axis_size("helper")
    capacity = max(2, (row_total + helpers - 1) // helpers)
    owner_id = parent_slot // PROWS
    local_row = parent_slot % PROWS
    owner_hot = ((owner_id[:, None] == jnp.arange(helpers)[None, :]) & live_rows[:, None]).astype(
        jnp.int32
    )
    before = jnp.cumsum(owner_hot, axis=0) - owner_hot
    slot_rank = jnp.sum(before * owner_hot, axis=1)
    target = jnp.where(live_rows, owner_id * capacity + slot_rank, helpers * capacity)
    send_rows = (
        jnp.zeros((helpers * capacity, contribution.shape[1]), jnp.bfloat16)
        .at[target]
        .set(contribution, mode="drop")
    )
    send_local = (
        jnp.full((helpers * capacity,), -1, jnp.int32).at[target].set(local_row, mode="drop")
    )
    got_rows, got_local = (
        lax.all_to_all(
            send_rows.reshape(helpers, capacity, contribution.shape[1]),
            "helper",
            split_axis=0,
            concat_axis=0,
            tiled=True,
        ),
        lax.all_to_all(
            send_local.reshape(helpers, capacity), "helper", split_axis=0, concat_axis=0, tiled=True
        ),
    )
    flat_rows = got_rows.reshape(helpers * capacity, contribution.shape[1])
    flat_local = got_local.reshape(helpers * capacity)
    chooser = (jnp.arange(PROWS)[:, None] == flat_local[None, :]).astype(jnp.bfloat16)
    parent_block = jnp.dot(chooser, flat_rows, preferred_element_type=jnp.float32)
    return (factor, parent_block)


def solution(mesh):
    return jax.shard_map(
        per_device,
        mesh=mesh,
        in_specs=(
            P(("front", "helper"), None),
            P("front", None, None),
            P(("front", "helper"), None),
            P(("front", "helper"), None),
            P(("front", "helper")),
            P(("front", "helper")),
        ),
        out_specs=(P(("front", "helper"), None), P(("front", "helper"), None)),
        check_vma=False,
    )
```

profile of v0, /device:TPU:6, one launch (start us, length us, event | category | flops | bytes accessed | tf_op | source)
XLA Modules:
  0.0 255.6 jit_solution(3178389487960829072)
XLA Ops:
  7.2 0.0 copy-start
  7.2 0.0 all-gather.4.cloned.1.call-start
  7.2 0.7 all-gather.4.cloned.1.call-update
  7.9 0.0 all-gather.6.cloned.1.call-start
  8.0 1.4 fusion.65
  9.3 0.1 copy.69
  9.5 0.7 copy.70
  10.2 0.7 copy.71
  10.9 0.7 copy.72
  11.7 0.7 copy.73
  12.4 0.7 copy.74
  13.1 0.7 copy.75
  13.9 0.7 copy.76
  14.6 0.7 copy.77
  15.3 0.7 copy.78
  16.1 0.7 copy.79
  16.8 0.7 copy.80
  17.5 0.7 copy.81
  18.2 0.7 copy.82
  19.0 0.7 copy.83
  19.7 0.7 copy.84
  20.4 0.9 constant_dynamic-update-slice_fusion.109
  21.3 82.6 %all-gather.4.cloned.1.call-done = bf16[2048,2048]{1,0:T(8,128)(2,1)} async-done(((bf16[16,2048]{1,0:T(8,128)(2,1)}), bf16[2048,2048]{1,0:T(8,128)(2,1)}) %all-gather.4.cloned.1.call-update) | async-done | bytes 8388624 | tf_op jit(solution)/shard_map/all_gather | solution.py:34
  103.9 2.0 constant_dynamic-update-slice_fusion.108
  105.9 1.9 constant_dynamic-update-slice_fusion.107
  107.8 1.9 constant_dynamic-update-slice_fusion.106
  109.7 2.0 constant_dynamic-update-slice_fusion.105
  111.7 2.0 constant_dynamic-update-slice_fusion.104
  113.7 2.1 constant_dynamic-update-slice_fusion.103
  115.8 2.1 constant_dynamic-update-slice_fusion.102
  117.9 2.1 constant_dynamic-update-slice_fusion.101
  119.9 2.1 constant_dynamic-update-slice_fusion.100
  122.1 0.0 copy-done.6
  122.1 2.1 constant_dynamic-update-slice_fusion.99
  124.2 2.1 constant_dynamic-update-slice_fusion.98
  126.3 2.2 constant_dynamic-update-slice_fusion.97
  128.5 1.6 constant_dynamic-update-slice_fusion.96
  130.1 1.3 constant_dynamic-update-slice_fusion.95
  131.4 1.3 fusion.8
  132.8 0.5 fusion
  133.3 0.6 slice_bitcast_fusion
  133.9 0.0 all-gather.6.cloned.1.call-update
  133.9 0.1 copy.64
  134.7 0.3 fusion.41
  135.2 0.2 fusion.47
  135.4 1.4 scatter_custom_fusion
  136.8 0.8 all_to_all.9
  137.6 9.9 %all-to-all-start = ((s32[128,1,2]{2,1,0:T(1,128)}), s32[128,1,2]{2,1,0:T(1,128)S(1)}, u32[]{:S(2)}, u32[]{:S(2)}) async-start(s32[128,1,2]{2,1,0:T(1,128)} %bitcast.8), calls=%async_computation | async-start | bytes 131072 | tf_op jit(solution)/shard_map/all_to_all | solution.py:70
  147.5 66.3 %all-gather.6.cloned.1.call-done = bf16[128,4,2048]{2,1,0:T(4,128)(2,1)} async-done(((bf16[1,4,2048]{2,1,0:T(4,128)(2,1)}), bf16[128,4,2048]{2,1,0:T(4,128)(2,1)}) %all-gather.6.cloned.1.call-update) | async-done | bytes 2097168 | tf_op jit(solution)/shard_map/all_gather | solution.py:38
  213.8 3.9 %reshape.73 = bf16[512,2048]{1,0:T(8,128)(2,1)} reshape(bf16[128,4,2048]{2,1,0:T(4,128)(2,1)} %all-gather.6.cloned.1.call-done) | data formatting | bytes 4194304
  217.8 2.3 fusion.1
  220.1 1.6 scatter_custom_fusion.1
  221.7 0.8 reshape.52
  222.5 0.0 all-to-all-done
  222.5 10.2 %all-to-all-start.1 = ((bf16[128,2,512]{2,1,0:T(2,128)(2,1)}), bf16[128,2,512]{2,1,0:T(2,128)(2,1)S(1)}, u32[]{:S(2)}, u32[]{:S(2)}) async-start(bf16[128,2,512]{2,1,0:T(2,128)(2,1)} %reshape.52), calls=%async_computation.1 | async-start | bytes 524288 | tf_op jit(solution)/shard_map/all_to_all | solution.py:63
  232.7 0.5 broadcast.68
  233.2 0.8 reduce.3
  234.0 0.1 eq.48
  234.1 0.5 copy.63
  234.7 0.1 bitcast_select_fusion
  234.8 1.4 copy.67
  236.2 11.5 %all-to-all-done.1 = bf16[128,2,512]{2,1,0:T(2,128)(2,1)S(1)} async-done(((bf16[128,2,512]{2,1,0:T(2,128)(2,1)}), bf16[128,2,512]{2,1,0:T(2,128)(2,1)S(1)}, u32[]{:S(2)}, u32[]{:S(2)}) %all-to-all-start.1) | async-done | bytes 262176 | tf_op jit(solution)/shard_map/all_to_all | solution.py:63
  247.8 0.1 reshape.53
  247.9 0.9 fusion.51
  (28 shorter events, 0.2 us)
Async XLA Ops:
  7.2 125.6 %copy-start = (bf16[16,128,128]{2,1,0:T(8,128)(2,1)S(1)}, bf16[16,128,128]{2,1,0:T(8,128)(2,1)}, u32[]{:S(2)}) copy-start(bf16[16,128,128]{2,1,0:T(8,128)(2,1)} %param.7) | copy-start | bytes 1572868
  7.2 96.7 %all-gather.4.cloned.1.call-start = ((), (), s32[]{:S(2)}) async-start(), calls=%async_computation.2 | async-start | bytes 8454144 | tf_op jit(solution)/shard_map/all_gather | solution.py:34
  7.9 205.9 %all-gather.6.cloned.1.call-start = ((), (), s32[]{:S(2)}) async-start(), calls=%async_computation.3 | async-start | bytes 2113536 | tf_op jit(solution)/shard_map/all_gather | solution.py:38
  103.9 14.0 %copy-start.8 = (bf16[256,128]{0,1:T(8,128)(2,1)S(1)}, bf16[256,128]{0,1:T(8,128)(2,1)}, u32[]{:S(2)}) copy-start(bf16[256,128]{0,1:T(8,128)(2,1)} %copy.77) | copy-start | bytes 196612
  103.9 16.1 %copy-start.7 = (bf16[256,128]{0,1:T(8,128)(2,1)S(1)}, bf16[256,128]{0,1:T(8,128)(2,1)}, u32[]{:S(2)}) copy-start(bf16[256,128]{0,1:T(8,128)(2,1)} %copy.78) | copy-start | bytes 196612
  103.9 18.2 %copy-start.6 = (bf16[256,128]{0,1:T(8,128)(2,1)S(1)}, bf16[256,128]{0,1:T(8,128)(2,1)}, u32[]{:S(2)}) copy-start(bf16[256,128]{0,1:T(8,128)(2,1)} %copy.79) | copy-start | bytes 196612
  103.9 20.3 %copy-start.5 = (bf16[256,128]{0,1:T(8,128)(2,1)S(1)}, bf16[256,128]{0,1:T(8,128)(2,1)}, u32[]{:S(2)}) copy-start(bf16[256,128]{0,1:T(8,128)(2,1)} %copy.80) | copy-start | bytes 196612
  103.9 22.4 %copy-start.4 = (bf16[256,128]{0,1:T(8,128)(2,1)S(1)}, bf16[256,128]{0,1:T(8,128)(2,1)}, u32[]{:S(2)}) copy-start(bf16[256,128]{0,1:T(8,128)(2,1)} %copy.81) | copy-start | bytes 196612
  103.9 24.6 %copy-start.3 = (bf16[256,128]{0,1:T(8,128)(2,1)S(1)}, bf16[256,128]{0,1:T(8,128)(2,1)}, u32[]{:S(2)}) copy-start(bf16[256,128]{0,1:T(8,128)(2,1)} %copy.82) | copy-start | bytes 196612
  105.9 24.2 %copy-start.2 = (bf16[256,128]{0,1:T(8,128)(2,1)S(1)}, bf16[256,128]{0,1:T(8,128)(2,1)}, u32[]{:S(2)}) copy-start(bf16[256,128]{0,1:T(8,128)(2,1)} %copy.83) | copy-start | bytes 196612
  109.7 21.7 %copy-start.1 = (bf16[256,128]{0,1:T(8,128)(2,1)S(1)}, bf16[256,128]{0,1:T(8,128)(2,1)}, u32[]{:S(2)}) copy-start(bf16[256,128]{0,1:T(8,128)(2,1)} %copy.84) | copy-start | bytes 196612
  113.7 20.2 %copy-start.9 = (s32[256]{0:T(256)S(1)}, s32[256]{0:T(256)}, u32[]{:S(2)}) copy-start(s32[256]{0:T(256)} %param.11) | copy-start | bytes 3076
  137.6 84.9 %all-to-all-start = ((s32[128,1,2]{2,1,0:T(1,128)}), s32[128,1,2]{2,1,0:T(1,128)S(1)}, u32[]{:S(2)}, u32[]{:S(2)}) async-start(s32[128,1,2]{2,1,0:T(1,128)} %bitcast.8), calls=%async_computation | async-start | bytes 131072 | tf_op jit(solution)/shard_map/all_to_all | solution.py:70
  222.5 25.3 %all-to-all-start.1 = ((bf16[128,2,512]{2,1,0:T(2,128)(2,1)}), bf16[128,2,512]{2,1,0:T(2,128)(2,1)S(1)}, u32[]{:S(2)}, u32[]{:S(2)}) async-start(bf16[128,2,512]{2,1,0:T(2,128)(2,1)} %reshape.52), calls=%async_computation.1 | async-start | bytes 524288 | tf_op jit(solution)/shard_map/all_to_all | solution.py:63
Sparse Core Ops, SparseCore 0:
  11.1 92.6 all-gather.3
  134.0 79.7 all-gather.5
where the time goes:
time: 257 us; the launch traced here: 256 us
  waiting for transfers between devices  161 us (63%)
  matrix products  32.5 us (13%)
  local copies, waits for them, and re-layouts  25.3 us (10%)
  starting transfers between devices  20.1 us (8%)
  between operations  14.9 us (6%)
    all_gather x1, waiting for transfers between devices, per_device(): pivot_panel = lax.all_gather(lower_panel, 'helper', axis=0, tiled=True)  82.6 us
    all_gather x1, waiting for transfers between devices, per_device(): window_rows = lax.all_gather(factor[:SR], 'helper', axis=0, tiled=True)  66.3 us
    dot_general x15, matrix products, solve_rows(): lax.dot_general(earlier, pivot_panel[column_start:column_start + block_wi...  28.8 us
    unnamed x41, local copies, waits for them, and re-layouts  18 us
    all_to_all x1, waiting for transfers between devices, per_device(): lax.all_to_all(send_rows.reshape(helpers, capacity, contribution.shape[1]...  11.5 us
    all_to_all x1, starting transfers between devices, per_device(): lax.all_to_all(send_rows.reshape(helpers, capacity, contribution.shape[1]...  10.2 us
    all_to_all x1, starting transfers between devices, per_device(): lax.all_to_all(send_local.reshape(helpers, capacity), 'helper', split_axi...  9.91 us
  transfers between devices with their start and end apart: 4, of which 3 were waited for; matrix products, arithmetic and copies ran while one was open for 11% of the time, Pallas kernels for 0%

commit v1 on v0

v1 whole, which is shorter than its diff:
```python
import functools

import jax
import jax.numpy as jnp
from jax import lax
from jax.experimental import pallas as pl
from jax.experimental.pallas import tpu as pltpu
from jax.sharding import PartitionSpec as P

UNIT = 128
SR = 4
PROWS = 128
BS = 128
NB = 16
NPIV = 2048
ROWS = 256
SLAB = 512
HELPERS = 128
CAP = 2
SLOTS = HELPERS * CAP
WIDE = SLAB + 128
ALL = SLAB + ROWS
F32 = jnp.float32
BF16 = jnp.bfloat16
NT = (((1,), (1,)), ((), ()))
TN = (((0,), (0,)), ((), ()))


def dot(a, b, dims=(((1,), (0,)), ((), ()))):
    return lax.dot_general(a, b, dims, preferred_element_type=F32)


def front_kernel(
    count_ref, panel_hbm, window_hbm, rows_ref, block_ref, inv_ref, slot_ref,
    factor_ref, send_ref, lt, xw, solved, wfac, sems,
):
    copies = [pltpu.make_async_copy(window_hbm, xw, sems.at[0])]
    steps = NB // 2
    per_step = [[] for _ in range(steps)]
    for s in range(steps):
        for j in range(2 * s + 1):
            top = 256 * s if j < 2 * s else 256 * s + BS
            rows = pl.ds(top, 256 * (s + 1) - top)
            per_step[s].append(
                pltpu.make_async_copy(
                    panel_hbm.at[rows, pl.ds(BS * j, BS)], lt.at[j, rows, :], sems.at[1 + s]
                )
            )
    for c in copies:
        c.start()
    for group in per_step:
        for c in group:
            c.start()

    live_count = UNIT * count_ref[0]
    live = lax.broadcasted_iota(jnp.int32, (ROWS, 1), 0) < live_count

    for c in copies:
        c.wait()
    for s in range(steps):
        for c in per_step[s]:
            c.wait()
        lo = 256 * s
        k0, k1 = 2 * s, 2 * s + 1
        x0 = jnp.concatenate([xw[k0], rows_ref[:, lo : lo + BS]], axis=0).astype(F32)
        x1 = jnp.concatenate([xw[k1], rows_ref[:, lo + BS : lo + 256]], axis=0).astype(F32)
        if s > 0:
            panel = jnp.concatenate([lt[j, lo : lo + 256, :] for j in range(k0)], axis=1)
            update = dot(solved[:, :lo], panel, NT)
            x0 = x0 - update[:, :BS]
            x1 = x1 - update[:, BS:]
        s0 = x0.astype(BF16)
        x1 = x1 - dot(s0, lt[k0, lo + BS : lo + 256, :], NT)
        s1 = x1.astype(BF16)
        solved[:, lo : lo + BS] = s0
        solved[:, lo + BS : lo + 256] = s1
        for part, base in ((s0, lo), (s1, lo + BS)):
            f = dot(part, inv_ref[base // BS]).astype(BF16)
            wfac[:, base : base + BS] = f[:SLAB]
            factor_ref[:, base : base + BS] = jnp.where(live, f[SLAB:], jnp.zeros((), BF16))

    product = dot(solved[SLAB:, :], wfac[...], NT)
    contribution = (block_ref[...].astype(F32) - product).astype(BF16)

    slot = slot_ref[...]
    owner_row = jnp.broadcast_to(lax.shift_right_logical(slot, 7).astype(F32), (ROWS, ROWS))
    owner_col = owner_row.T
    local_row = jnp.broadcast_to((slot & 127).astype(F32) + 1.0, (BS, ROWS))
    local_col = local_row.T.astype(BF16)
    i0 = lax.broadcasted_iota(jnp.int32, (ROWS, ROWS), 0)
    i1 = lax.broadcasted_iota(jnp.int32, (ROWS, ROWS), 1)
    earlier = jnp.where((owner_row == owner_col) & (i0 < i1) & (i0 < live_count), 1.0, 0.0)
    rank = jnp.sum(earlier, axis=0, keepdims=True)
    target = owner_row * CAP + rank
    chosen = jnp.where((target == i0.astype(F32)) & (i1 < live_count), 1.0, 0.0).astype(BF16)
    payload = jnp.concatenate([contribution, local_col], axis=1)
    send_ref[...] = dot(chosen, payload).astype(BF16)


def front_call(panel, window, rows, block, inverse, count, slot):
    vmem = pl.BlockSpec(memory_space=pltpu.VMEM)
    hbm = pl.BlockSpec(memory_space=pl.ANY)
    return pl.pallas_call(
        front_kernel,
        out_shape=(
            jax.ShapeDtypeStruct((ROWS, NPIV), BF16),
            jax.ShapeDtypeStruct((SLOTS, WIDE), BF16),
        ),
        in_specs=[pl.BlockSpec(memory_space=pltpu.SMEM), hbm, hbm, vmem, vmem, vmem, vmem],
        out_specs=(vmem, vmem),
        scratch_shapes=[
            pltpu.VMEM((NB, NPIV, BS), BF16),
            pltpu.VMEM((NB, SLAB, BS), BF16),
            pltpu.VMEM((ALL, NPIV), BF16),
            pltpu.VMEM((SLAB, NPIV), BF16),
            pltpu.SemaphoreType.DMA((1 + NB // 2,)),
        ],
        compiler_params=pltpu.CompilerParams(vmem_limit_bytes=50 * 1024 * 1024),
        name="front",
    )(count, panel, window, rows, block, inverse, slot)


def assemble_kernel(got_ref, out_ref):
    got = got_ref[...]
    local = got[:, SLAB:].astype(F32)
    wanted = lax.broadcasted_iota(jnp.int32, (SLOTS, PROWS), 1).astype(F32) + 1.0
    chooser = jnp.where(local == wanted, 1.0, 0.0).astype(BF16)
    out_ref[...] = dot(chooser, got[:, :SLAB], TN)


def assemble_call(got):
    vmem = pl.BlockSpec(memory_space=pltpu.VMEM)
    return pl.pallas_call(
        assemble_kernel,
        out_shape=jax.ShapeDtypeStruct((PROWS, SLAB), F32),
        in_specs=[vmem],
        out_specs=vmem,
        name="assemble",
    )(got)


def per_device(lower_panel, pivot_inverse, lower_rows, window_block, block_count, parent_slot):
    mine = jnp.concatenate([lower_panel, lower_rows[:SR]], axis=0)
    every = lax.all_gather(mine, "helper", axis=0)
    panel = every[:, :16].reshape(NPIV, NPIV)
    window = every[:, 16:].reshape(SLAB, NB, BS).transpose(1, 0, 2)
    factor, send = front_call(
        panel, window, lower_rows, window_block, pivot_inverse, block_count, parent_slot.reshape(1, ROWS)
    )
    got = lax.all_to_all(
        send.reshape(HELPERS, CAP, WIDE), "helper", split_axis=0, concat_axis=0, tiled=True
    )
    return factor, assemble_call(got.reshape(SLOTS, WIDE))


def solution(mesh):
    return jax.shard_map(
        per_device,
        mesh=mesh,
        in_specs=(
            P(("front", "helper"), None),
            P("front", None, None),
            P(("front", "helper"), None),
            P(("front", "helper"), None),
            P(("front", "helper")),
            P(("front", "helper")),
        ),
        out_specs=(P(("front", "helper"), None), P(("front", "helper"), None)),
        check_vma=False,
    )
```

time: 257 us -> 175 us (0.68)
  waiting for transfers between devices: 161 us -> 98 us
  matrix products: 32.5 us -> 0 us
  blocking collectives: 0 us -> 26.2 us
  starting transfers between devices: 20.1 us -> 0.04 us
  Pallas kernels: 0 us -> 14.3 us
  local copies, waits for them, and re-layouts: 25.3 us -> 19.8 us
    all_gather x2 -> x1, waiting for transfers between devices: 149 us -> 98 us  [per_device(): every = lax.all_gather(mine, 'helper', axis=0)]
    dot_general x18 -> x0, matrix products: 32.5 us -> none  [the longest x15 28.8 us: solve_rows(): lax.dot_general(earlier, pivot_panel[column_start:column_start + block_wi...]
    all_to_all x0 -> x1, blocking collectives: none -> 26.2 us  [per_device(): lax.all_to_all(send.reshape(HELPERS, CAP, WIDE), 'helper', split_axis=0,...]
    all_to_all x2 -> x0, starting transfers between devices: 20.1 us -> none  [the longest x1 10.2 us: per_device(): lax.all_to_all(send_rows.reshape(helpers, capacity, contribution.shape[1]...]
    unnamed x41 -> x8, local copies, waits for them, and re-layouts: 18 us -> 0.01 us
    pallas_call x0 -> x2, Pallas kernels: none -> 14.3 us  [the longest x1 12.4 us: front_call(): pl.pallas_call(front_kernel, out_shape=(jax.ShapeDtypeStruct((ROWS, NPIV)...]
    slice x1 -> x3, local copies, waits for them, and re-layouts: 1.37 us -> 13.8 us  [the longest x1 8.4 us: per_device(): panel = every[:, :16].reshape(NPIV, NPIV)]
    all_to_all x2 -> x0, waiting for transfers between devices: 11.5 us -> none  [the longest x1 11.5 us: per_device(): lax.all_to_all(send_rows.reshape(helpers, capacity, contribution.shape[1]...]
  transfers between devices with their start and end apart: 4 -> 1, of which waited for: 3 -> 1; matrix products, arithmetic and copies ran while one was open for 11% -> 0% of each run, Pallas kernels for 0% -> 0%
where the time goes in v1:
time: 175 us
  waiting for transfers between devices  98 us (56%)
  blocking collectives  26.2 us (15%)
  local copies, waits for them, and re-layouts  19.8 us (11%)
  between operations  14.7 us (8%)
  Pallas kernels  14.3 us (8%)
    all_gather x1, waiting for transfers between devices, per_device(): every = lax.all_gather(mine, 'helper', axis=0)  98 us
    all_to_all x1, blocking collectives, per_device(): lax.all_to_all(send.reshape(HELPERS, CAP, WIDE), 'helper', split_axis=0,...  26.2 us
    pallas_call x1, Pallas kernels, front_call(): pl.pallas_call(front_kernel, out_shape=(jax.ShapeDtypeStruct((ROWS, NPIV)...  12.4 us
    slice x1, local copies, waits for them, and re-layouts, per_device(): panel = every[:, :16].reshape(NPIV, NPIV)  8.4 us
    reshape x2, local copies, waits for them, and re-layouts, per_device(): window = every[:, 16:].reshape(SLAB, NB, BS).transpose(1, 0, 2)  5.02 us
    slice x1, local copies, waits for them, and re-layouts, per_device(): window = every[:, 16:].reshape(SLAB, NB, BS).transpose(1, 0, 2)  4.64 us
  transfers between devices with their start and end apart: 1, of which 1 were waited for; matrix products, arithmetic and copies ran while one was open for 0% of the time, Pallas kernels for 0%

profile of v1, /device:TPU:6, one launch (start us, length us, event | category | flops | bytes accessed | tf_op | source)
XLA Modules:
  0.0 174.5 jit_solution(13156289847468712811)
XLA Ops:
  7.2 0.0 all-gather.4.cloned.1.call-start
  7.2 0.8 slice.9
  8.0 1.5 maximum_bitcast_fusion
  9.5 0.0 all-gather.4.cloned.1.call-update
  10.1 98.0 %all-gather.4.cloned.1.call-done = bf16[128,20,2048]{2,1,0:T(8,128)(2,1)} async-done(((bf16[1,20,2048]{2,1,0:T(8,128)(2,1)}), bf16[128,20,2048]{2,1,0:T(8,128)(2,1)}) %all-gather.4.cloned.1.call-update) | async-done | bytes 10485776 | tf_op jit(solution)/shard_map/all_gather | solution.py:144
  108.1 4.6 %slice.13 = bf16[128,4,2048]{2,1,0:T(4,128)(2,1)} slice(bf16[128,20,2048]{2,1,0:T(8,128)(2,1)} %all-gather.4.cloned.1.call-done), slice={[0:128], [16:20], [0:2048]} | slice | bytes 4194304 | tf_op jit(solution)/shard_map/slice | solution.py:146
  112.8 3.2 %reshape.20 = bf16[512,16,128]{2,1,0:T(8,128)(2,1)S(1)} reshape(bf16[128,4,2048]{2,1,0:T(4,128)(2,1)} %slice.13) | data formatting | bytes 4194304 | tf_op jit(solution)/shard_map/reshape | solution.py:146
  115.9 1.9 %copy.11 = bf16[512,16,128]{2,0,1:T(8,128)(2,1)} copy(bf16[512,16,128]{2,1,0:T(8,128)(2,1)S(1)} %reshape.20) | data formatting | bytes 4194304 | tf_op jit(solution)/shard_map/reshape | solution.py:146
  117.8 0.0 copy-start
  117.8 0.0 copy-start.1
  117.8 0.0 copy-start.2
  117.8 0.0 copy-start.3
  117.8 8.4 %slice.12 = bf16[128,16,2048]{2,1,0:T(8,128)(2,1)} slice(bf16[128,20,2048]{2,1,0:T(8,128)(2,1)} %all-gather.4.cloned.1.call-done), slice={[0:128], [0:16], [0:2048]} | slice | bytes 16777216 | tf_op jit(solution)/shard_map/slice | solution.py:145
  126.2 0.0 copy-done
  126.2 0.0 copy-done.1
  126.2 0.0 copy-done.2
  126.2 0.0 copy-done.3
  126.2 12.4 %front.1 = (bf16[256,2048]{1,0:T(8,128)(2,1)}, bf16[256,640]{1,0:T(8,128)(2,1)S(1)}) custom-call(s32[1]{0:T(128)S(6)} %copy.12.count_ref, bf16[2048,2048]{1,0:T(8,128)(2,1)} %bitcast.8, bf16[16,512,128]{2,1,0:T(8,128)(2,1)} %bitcast.9, bf16[256,2048]{1,0:T(8,128)(2,1)S(1)} %copy-done, bf16[256,512]{1,0:T(8,128)(2,1)S(1)} %copy-done.2, ...), custom_call_target="tpu_custom_call" | custom-call | tf_op jit(solution)/shard_map/front/pallas_call | solution.py:103
  138.7 0.1 reshape.22
  138.8 26.2 %all_to_all.5 = bf16[128,2,640]{2,1,0:T(2,128)(2,1)S(1)} all-to-all(bf16[128,2,640]{2,1,0:T(2,128)(2,1)S(1)} %reshape.22), channel_id=1, replica_groups=mesh['front'=4,'helper'=128] {'helper'}, dimensions={0} | all-to-all | bytes 655360 | tf_op jit(solution)/shard_map/all_to_all | solution.py:150
  165.0 0.8 reshape.23.got_ref
  165.8 1.9 %assemble.1 = f32[128,512]{1,0:T(8,128)} custom-call(bf16[256,640]{1,0:T(8,128)(2,1)} %reshape.23.got_ref), custom_call_target="tpu_custom_call" | custom-call | tf_op jit(solution)/shard_map/assemble/pallas_call | solution.py:133
Async XLA Ops:
  7.2 101.0 %all-gather.4.cloned.1.call-start = ((), (), s32[]{:S(2)}) async-start(), calls=%async_computation.1 | async-start | bytes 12681216 | tf_op jit(solution)/shard_map/all_gather | solution.py:144
  117.8 8.4 %copy-start = (bf16[256,2048]{1,0:T(8,128)(2,1)S(1)}, bf16[256,2048]{1,0:T(8,128)(2,1)}, u32[]{:S(2)}) copy-start(bf16[256,2048]{1,0:T(8,128)(2,1)} %rows_ref.1) | copy-start | bytes 3145732
  117.8 8.4 %copy-start.1 = (bf16[16,128,128]{2,1,0:T(8,128)(2,1)S(1)}, bf16[16,128,128]{2,1,0:T(8,128)(2,1)}, u32[]{:S(2)}) copy-start(bf16[16,128,128]{2,1,0:T(8,128)(2,1)} %inv_ref.1) | copy-start | bytes 1572868
  117.8 8.4 %copy-start.2 = (bf16[256,512]{1,0:T(8,128)(2,1)S(1)}, bf16[256,512]{1,0:T(8,128)(2,1)}, u32[]{:S(2)}) copy-start(bf16[256,512]{1,0:T(8,128)(2,1)} %block_ref.1) | copy-start | bytes 786436
  117.8 8.4 %copy-start.3 = (s32[256]{0:T(256)S(1)}, s32[256]{0:T(256)}, u32[]{:S(2)}) copy-start(s32[256]{0:T(256)} %param.11) | copy-start | bytes 3076
Sparse Core Ops, SparseCore 0:
  11.7 96.3 all-gather.3

commit v2 on v1

--- a/solution.py
+++ b/solution.py
@@ -24,53 +24,181 @@
 BF16 = jnp.bfloat16
 NT = (((1,), (1,)), ((), ()))
 TN = (((0,), (0,)), ((), ()))
+LINE = 8
+PAIRS = 4
+SENT = NB - 1 + SR
+PIECES = PAIRS * NB + 2 * NB
+FROM = (0, 2, -2, 1, 3, -1, -3, 4)
+
+
+def helper(y, z, core):
+    return 2 * LINE * y + 2 * z + core
+
+
+def line_groups():
+    return [[helper(y, z, 0) for y in range(LINE)] for z in range(LINE)] + [
+        [helper(g if z % 2 == 0 else 7 - g, z, 1) for z in range(LINE)] for g in range(LINE)
+    ]
+
+
+def from_offset(step):
+    pairs = []
+    for y in range(LINE):
+        for z in range(LINE):
+            pairs.append((helper(y, (z + step) % LINE, 0), helper(y, z, 0)))
+            pairs.append((helper((y + step) % LINE, z, 1), helper(y, z, 1)))
+    return pairs
+
+
+def place():
+    me = lax.axis_index("helper")
+    return lax.div(me, 16), lax.rem(lax.div(me, 2), 8), lax.rem(me, 2)
 
 
 def dot(a, b, dims=(((1,), (0,)), ((), ()))):
     return lax.dot_general(a, b, dims, preferred_element_type=F32)
 
 
-def front_kernel(
-    count_ref, panel_hbm, window_hbm, rows_ref, block_ref, inv_ref, slot_ref,
-    factor_ref, send_ref, lt, xw, solved, wfac, sems,
-):
-    copies = [pltpu.make_async_copy(window_hbm, xw, sems.at[0])]
-    steps = NB // 2
-    per_step = [[] for _ in range(steps)]
-    for s in range(steps):
-        for j in range(2 * s + 1):
-            top = 256 * s if j < 2 * s else 256 * s + BS
-            rows = pl.ds(top, 256 * (s + 1) - top)
-            per_step[s].append(
+def spread_kernel(panel_ref, rows_ref, out_ref, window):
+    for j in range(NB):
+        window[SR * j : SR * (j + 1), :] = rows_ref[:, BS * j : BS * (j + 1)].astype(F32)[:SR]
+    leading = window[...].astype(BF16).reshape(SR, 16, BS)
+    for d in range(LINE):
+        for j in range(NB - 1):
+            out_ref[d, j] = panel_ref[:, BS * j : BS * (j + 1)]
+        out_ref[d, NB - 1 :] = leading
+
+
+def spread_call(panel, rows):
+    return pl.pallas_call(
+        spread_kernel,
+        grid=(1,),
+        out_shape=jax.ShapeDtypeStruct((LINE, SENT, 16, BS), BF16),
+        in_specs=[pl.BlockSpec((16, NPIV), lambda i: (0, 0))] * 2,
+        out_specs=pl.BlockSpec((LINE, SENT, 16, BS), lambda i: (0, 0, 0, 0)),
+        scratch_shapes=[pltpu.VMEM((SR * NB, BS), F32)],
+        name="spread",
+    )(panel, rows)
+
+
+def pack_kernel(line_ref, out_ref, window):
+    y, z, core = place()
+    label = jnp.where(lax.rem(z, 2) == 0, y, 7 - y)
+    low = jnp.minimum(label, 7 - label)
+    for p in range(PAIRS):
+        upper = jnp.where(core == 0, jnp.where(z >= 4, 1, 0), 1 if p >= 2 else 0)
+        first = jnp.where(core == 0, p, low)
+        count = 14 - 2 * first + upper
+        swap = jnp.where(label <= 3, 0, 1)
+        large = jnp.where(core == 0, 7 - p, 2 * p + 1 - swap)
+        small = jnp.where(core == 0, p, 2 * p + swap)
+        for s in range(NB):
+            member = jnp.where(s < count, large, small)
+            piece = jnp.where(s < count, s, s - count)
+            out_ref[NB * p + s] = line_ref[member, piece]
+    for d in range(LINE):
+        leading = line_ref[d, NB - 1 :].astype(F32)
+        for j in range(NB):
+            window[j, SR * d : SR * (d + 1), :] = leading[j // 4, SR * (j % 4) : SR * (j % 4 + 1), :]
+    out_ref[PAIRS * NB :] = window[...].astype(BF16).reshape(2 * NB, 16, BS)
+
+
+def pack_call(line):
+    vmem = pl.BlockSpec(memory_space=pltpu.VMEM)
+    return pl.pallas_call(
+        pack_kernel,
+        out_shape=jax.ShapeDtypeStruct((PIECES, 16, BS), BF16),
+        in_specs=[vmem],
+        out_specs=vmem,
+        scratch_shapes=[pltpu.VMEM((NB, SR * LINE, BS), F32)],
+        name="pack",
+    )(line)
+
+
+def block_copies(source, core, y, z, lt, xw, sem):
+    copies = []
+    label_sign = lax.rem(z, 2) == 0
+    for q, step in enumerate(FROM):
+        base = PIECES * q
+        if core == 0:
+            member = lax.rem(z + step + LINE, LINE)
+            window_row = 32 * member
+        else:
+            other = lax.rem(y + step + LINE, LINE)
+            member = jnp.where(label_sign, other, 7 - other)
+            window_row = 32 * member + SLAB // 2
+        copies.append(
+            pltpu.make_async_copy(
+                source.at[pl.ds(base + PAIRS * NB, 2 * NB)], xw.at[lax.div(window_row, 32)], sem
+            )
+        )
+        for p in range(PAIRS):
+            if core == 0:
+                upper = jnp.where(member >= 4, 1, 0)
+                count = 14 - 2 * p + upper
+                large = helper(7 - p, member, 0)
+                small = helper(p, member, 0)
+            else:
+                upper = 1 if p >= 2 else 0
+                low = jnp.minimum(member, 7 - member)
+                count = 14 - 2 * low + upper
+                z_large = jnp.where(member <= 3, 2 * p + 1, 2 * p)
+                large = helper(7 - low, z_large, 1)
+                small = helper(low, 4 * p + 1 - z_large, 1)
+            start = base + NB * p
+            copies.append(
                 pltpu.make_async_copy(
-                    panel_hbm.at[rows, pl.ds(BS * j, BS)], lt.at[j, rows, :], sems.at[1 + s]
+                    source.at[pl.ds(start, NB)], lt.at[:, large], sem
                 )
             )
-    for c in copies:
-        c.start()
-    for group in per_step:
-        for c in group:
-            c.start()
+            copies.append(
+                pltpu.make_async_copy(
+                    source.at[pl.ds(start + count, NB // 2)], lt.at[pl.ds(0, NB // 2), small], sem
+                )
+            )
+    return copies
+
+
+def front_kernel(
+    count_ref, mine_hbm, other_hbm, rows_ref, block_ref, inv_ref, slot_ref,
+    factor_ref, send_ref, lt, xw, solved, wfac, sem,
+):
+    y, z, core = place()
+
+    def copies(here):
+        refs = (mine_hbm, other_hbm) if here == 0 else (other_hbm, mine_hbm)
+        return block_copies(refs[0], 0, y, z, lt, xw, sem) + block_copies(refs[1], 1, y, z, lt, xw, sem)
+
+    for here in (0, 1):
+        @pl.when(core == here)
+        def _():
+            for c in copies(here):
+                c.start()
+
+    for c in copies(0):
+        c.wait()
 
     live_count = UNIT * count_ref[0]
     live = lax.broadcasted_iota(jnp.int32, (ROWS, 1), 0) < live_count
 
-    for c in copies:
-        c.wait()
-    for s in range(steps):
-        for c in per_step[s]:
-            c.wait()
+    def window_piece(k):
+        return xw[:, 2 * k : 2 * k + 2].reshape(SLAB, BS)
+
+    def panel_piece(j, top, count):
+        return lt[j, top // 16 : (top + count) // 16].reshape(count, BS)
+
+    for s in range(NB // 2):
         lo = 256 * s
         k0, k1 = 2 * s, 2 * s + 1
-        x0 = jnp.concatenate([xw[k0], rows_ref[:, lo : lo + BS]], axis=0).astype(F32)
-        x1 = jnp.concatenate([xw[k1], rows_ref[:, lo + BS : lo + 256]], axis=0).astype(F32)
+        x0 = jnp.concatenate([window_piece(k0), rows_ref[:, lo : lo + BS]], axis=0).astype(F32)
+        x1 = jnp.concatenate([window_piece(k1), rows_ref[:, lo + BS : lo + 256]], axis=0).astype(F32)
         if s > 0:
-            panel = jnp.concatenate([lt[j, lo : lo + 256, :] for j in range(k0)], axis=1)
+            panel = jnp.concatenate([panel_piece(j, lo, 256) for j in range(k0)], axis=1)
             update = dot(solved[:, :lo], panel, NT)
             x0 = x0 - update[:, :BS]
             x1 = x1 - update[:, BS:]
         s0 = x0.astype(BF16)
-        x1 = x1 - dot(s0, lt[k0, lo + BS : lo + 256, :], NT)
+        x1 = x1 - dot(s0, panel_piece(k0, lo + BS, BS), NT)
         s1 = x1.astype(BF16)
         solved[:, lo : lo + BS] = s0
         solved[:, lo + BS : lo + 256] = s1
@@ -79,8 +207,20 @@
             wfac[:, base : base + BS] = f[:SLAB]
             factor_ref[:, base : base + BS] = jnp.where(live, f[SLAB:], jnp.zeros((), BF16))
 
+    held = lax.broadcasted_iota(jnp.int32, (1, SLAB), 1)
+    group = lax.shift_right_logical(held, 5) & 7
+    turn = lax.shift_right_logical(held, 2) & 7
+    first_half = held < SLAB // 2
+    held_y = jnp.where(first_half, turn, jnp.where((turn & 1) == 0, group, 7 - group))
+    held_z = jnp.where(first_half, group, turn)
+    column = 64 * held_y + 8 * held_z + jnp.where(first_half, 0, 4) + (held & 3)
+    order = jnp.where(
+        lax.broadcasted_iota(jnp.int32, (SLAB, SLAB), 0) == column, 1.0, 0.0
+    ).astype(BF16)
+
     product = dot(solved[SLAB:, :], wfac[...], NT)
-    contribution = (block_ref[...].astype(F32) - product).astype(BF16)
+    held_contribution = (dot(block_ref[...], order) - product).astype(BF16)
+    contribution = dot(held_contribution, order, NT).astype(BF16)
 
     slot = slot_ref[...]
     owner_row = jnp.broadcast_to(lax.shift_right_logical(slot, 7).astype(F32), (ROWS, ROWS))
@@ -97,7 +237,7 @@
     send_ref[...] = dot(chosen, payload).astype(BF16)
 
 
-def front_call(panel, window, rows, block, inverse, count, slot):
+def front_call(mine, other, rows, block, inverse, count, slot):
     vmem = pl.BlockSpec(memory_space=pltpu.VMEM)
     hbm = pl.BlockSpec(memory_space=pl.ANY)
     return pl.pallas_call(
@@ -109,15 +249,15 @@
         in_specs=[pl.BlockSpec(memory_space=pltpu.SMEM), hbm, hbm, vmem, vmem, vmem, vmem],
         out_specs=(vmem, vmem),
         scratch_shapes=[
-            pltpu.VMEM((NB, NPIV, BS), BF16),
-            pltpu.VMEM((NB, SLAB, BS), BF16),
+            pltpu.VMEM((NB, HELPERS, 16, BS), BF16),
+            pltpu.VMEM((2 * LINE, 2 * NB, 16, BS), BF16),
             pltpu.VMEM((ALL, NPIV), BF16),
             pltpu.VMEM((SLAB, NPIV), BF16),
-            pltpu.SemaphoreType.DMA((1 + NB // 2,)),
+            pltpu.SemaphoreType.DMA,
         ],
         compiler_params=pltpu.CompilerParams(vmem_limit_bytes=50 * 1024 * 1024),
         name="front",
-    )(count, panel, window, rows, block, inverse, slot)
+    )(count, mine, other, rows, block, inverse, slot)
 
 
 def assemble_kernel(got_ref, out_ref):
@@ -140,12 +280,23 @@
 
 
 def per_device(lower_panel, pivot_inverse, lower_rows, window_block, block_count, parent_slot):
-    mine = jnp.concatenate([lower_panel, lower_rows[:SR]], axis=0)
-    every = lax.all_gather(mine, "helper", axis=0)
-    panel = every[:, :16].reshape(NPIV, NPIV)
-    window = every[:, 16:].reshape(SLAB, NB, BS).transpose(1, 0, 2)
+    def receive(block, step):
+        return lax.ppermute(block, "helper", from_offset(step))
+
+    line = lax.all_to_all(
+        spread_call(lower_panel, lower_rows), "helper", 0, 0, tiled=True, axis_index_groups=line_groups()
+    )
+    own = pack_call(line)
+    half = PIECES // 2
+    after = receive(own, 2)
+    before = receive(own, -2)
+    above = receive(jnp.concatenate([own, after]), 1)
+    below = receive(jnp.concatenate([own, before]), -1)
+    far = [receive(after[:half], 2), receive(before[half:], -2)]
+    mine = jnp.concatenate([own, after, before, above, below] + far)
+    other = lax.ppermute(mine, "helper", [(h, h ^ 1) for h in range(HELPERS)])
     factor, send = front_call(
-        panel, window, lower_rows, window_block, pivot_inverse, block_count, parent_slot.reshape(1, ROWS)
+        mine, other, lower_rows, window_block, pivot_inverse, block_count, parent_slot.reshape(1, ROWS)
     )
     got = lax.all_to_all(
         send.reshape(HELPERS, CAP, WIDE), "helper", split_axis=0, concat_axis=0, tiled=True

time: 175 us -> 129 us (0.74)
  waiting for transfers between devices: 98 us -> 21.8 us
  starting transfers between devices: 0.04 us -> 29 us
  blocking collectives: 26.2 us -> 52 us
  local copies, waits for them, and re-layouts: 19.8 us -> 4.25 us
  between operations: 14.7 us -> 1.49 us
  Pallas kernels: 14.3 us -> 18.9 us
    all_gather x1 -> x0, waiting for transfers between devices: 98 us -> none  [per_device(): every = lax.all_gather(mine, 'helper', axis=0)]
    ppermute x0 -> x7, starting transfers between devices: none -> 29 us  [the longest x6 27.1 us: receive(): return lax.ppermute(block, 'helper', from_offset(step))]
    all_to_all x0 -> x1, blocking collectives: none -> 24.7 us  [per_device(): lax.all_to_all(spread_call(lower_panel, lower_rows), 'helper', 0, 0, tile...]
    ppermute x0 -> x7, waiting for transfers between devices: none -> 21.8 us  [the longest x6 16.8 us: receive(): return lax.ppermute(block, 'helper', from_offset(step))]
    slice x3 -> x2, local copies, waits for them, and re-layouts: 13.8 us -> 0.03 us  [per_device(): far = [receive(after[:half], 2), receive(before[half:], -2)]]
    reshape x2 -> x0, local copies, waits for them, and re-layouts: 5.02 us -> none  [per_device(): window = every[:, 16:].reshape(SLAB, NB, BS).transpose(1, 0, 2)]
    pallas_call x0 -> x2, Pallas kernels: none -> 3.77 us  [the longest x1 2 us: pack_call(): pl.pallas_call(pack_kernel, out_shape=jax.ShapeDtypeStruct((PIECES, 16, B...]
    unnamed x8 -> x18, local copies, waits for them, and re-layouts: 0.01 us -> 3.23 us
  transfers between devices with their start and end apart: 1 -> 7, of which waited for: 1 -> 4; matrix products, arithmetic and copies ran while one was open for 0% -> 1% of each run, Pallas kernels for 0% -> 0%
where the time goes in v2:
time: 129 us; the launch traced here: 128 us
  blocking collectives  52 us (40%)
  starting transfers between devices  29 us (22%)
  waiting for transfers between devices  21.8 us (17%)
  Pallas kernels  18.9 us (15%)
  local copies, waits for them, and re-layouts  4.25 us (3%)
  between operations  1.49 us (1%)
    all_to_all x1, blocking collectives, per_device(): lax.all_to_all(send.reshape(HELPERS, CAP, WIDE), 'helper', split_axis=0,...  27.2 us
    ppermute x6, starting transfers between devices, receive(): return lax.ppermute(block, 'helper', from_offset(step))  27.1 us
    all_to_all x1, blocking collectives, per_device(): lax.all_to_all(spread_call(lower_panel, lower_rows), 'helper', 0, 0, tile...  24.7 us
    ppermute x6, waiting for transfers between devices, receive(): return lax.ppermute(block, 'helper', from_offset(step))  16.8 us
    pallas_call x1, Pallas kernels, front_call(): pl.pallas_call(front_kernel, out_shape=(jax.ShapeDtypeStruct((ROWS, NPIV)...  13.2 us
    ppermute x1, waiting for transfers between devices, per_device(): other = lax.ppermute(mine, 'helper', [(h, h ^ 1) for h in range(HELPERS)])  4.97 us
    unnamed x18, local copies, waits for them, and re-layouts  3.23 us
  transfers between devices with their start and end apart: 7, of which 4 were waited for; matrix products, arithmetic and copies ran while one was open for 1% of the time, Pallas kernels for 0%

profile of v2, /device:TPU:6, one launch (start us, length us, event | category | flops | bytes accessed | tf_op | source)
XLA Modules:
  0.0 128.4 jit_solution(8208602316694566747)
XLA Ops:
  0.6 1.8 %spread.1 = bf16[8,19,16,128]{3,2,1,0:T(8,128)(2,1)} custom-call(bf16[16,2048]{1,0:T(8,128)(2,1)} %panel_ref.1, bf16[256,2048]{1,0:T(8,128)(2,1)} %rows_ref.3), custom_call_target="tpu_custom_call" | custom-call | tf_op jit(solution)/shard_map/spread/pallas_call | solution.py:73
  2.4 24.7 %all_to_all.10.line_ref = bf16[8,19,16,128]{3,2,1,0:T(8,128)(2,1)} all-to-all(bf16[8,19,16,128]{3,2,1,0:T(8,128)(2,1)} %spread.1), channel_id=1, replica_groups={{0,16,32,48,64,80,96,112},{2,18,34,50,66,82,98,114},{4,20,36,52,68,84,1..., dimensions={0} | all-to-all | bytes 1245184 | tf_op jit(solution)/shard_map/all_to_all | solution.py:286
  27.1 2.0 %pack.1 = bf16[96,16,128]{2,1,0:T(8,128)(2,1)} custom-call(bf16[8,19,16,128]{3,2,1,0:T(8,128)(2,1)} %all_to_all.10.line_ref), custom_call_target="tpu_custom_call" | custom-call | tf_op jit(solution)/shard_map/pack/pallas_call | solution.py:108
  29.1 8.9 %collective-permute-start = (bf16[96,16,128]{2,1,0:T(8,128)(2,1)}, bf16[96,16,128]{2,1,0:T(8,128)(2,1)S(1)}, u32[]{:S(2)}, u32[]{:S(2)}) collective-permute-start(bf16[96,16,128]{2,1,0:T(8,128)(2,1)} %pack.1), channel_id=1, source_target_pairs={{4,0},{33,1},{6,2},{35,3},{8,4},{37,5},{10,6},{39,7},{12,8},{41,9}... | collective-permute-start | bytes 1179656 | tf_op jit(solution)/shard_map/ppermute | solution.py:284
  38.0 1.9 %collective-permute-start.1 = (bf16[96,16,128]{2,1,0:T(8,128)(2,1)}, bf16[96,16,128]{2,1,0:T(8,128)(2,1)S(1)}, u32[]{:S(2)}, u32[]{:S(2)}) collective-permute-start(bf16[96,16,128]{2,1,0:T(8,128)(2,1)} %pack.1), channel_id=1, source_target_pairs={{12,0},{97,1},{14,2},{99,3},{0,4},{101,5},{2,6},{103,7},{4,8},{105... | collective-permute-start | bytes 1179656 | tf_op jit(solution)/shard_map/ppermute | solution.py:284
  39.9 4.7 %collective-permute-done = bf16[96,16,128]{2,1,0:T(8,128)(2,1)S(1)} collective-permute-done((bf16[96,16,128]{2,1,0:T(8,128)(2,1)}, bf16[96,16,128]{2,1,0:T(8,128)(2,1)S(1)}, u32[]{:S(2)}, u32[]{:S(2)}) %collective-permute-start) | collective-permute-done | bytes 393248 | tf_op jit(solution)/shard_map/ppermute | solution.py:284
  44.6 5.5 %collective-permute-done.1 = bf16[96,16,128]{2,1,0:T(8,128)(2,1)S(1)} collective-permute-done((bf16[96,16,128]{2,1,0:T(8,128)(2,1)}, bf16[96,16,128]{2,1,0:T(8,128)(2,1)S(1)}, u32[]{:S(2)}, u32[]{:S(2)}) %collective-permute-start.1) | collective-permute-done | bytes 393248 | tf_op jit(solution)/shard_map/ppermute | solution.py:284
  50.1 1.1 pad_maximum_fusion
  51.2 7.1 %collective-permute-start.2 = (bf16[192,16,128]{2,1,0:T(8,128)(2,1)S(1)}, bf16[192,16,128]{2,1,0:T(8,128)(2,1)S(1)}, u32[]{:S(2)}, u32[]{:S(2)}) collective-permute-start(bf16[192,16,128]{2,1,0:T(8,128)(2,1)S(1)} %get-tuple-element.7), channel_id=1, source_target_pairs={{2,0},{17,1},{4,2},{19,3},{6,4},{21,5},{8,6},{23,7},{10,8},{25,9},... | collective-permute-start | bytes 2359304 | tf_op jit(solution)/shard_map/ppermute | solution.py:284
  58.4 2.3 %collective-permute-start.3 = (bf16[192,16,128]{2,1,0:T(8,128)(2,1)S(1)}, bf16[192,16,128]{2,1,0:T(8,128)(2,1)S(1)}, u32[]{:S(2)}, u32[]{:S(2)}) collective-permute-start(bf16[192,16,128]{2,1,0:T(8,128)(2,1)S(1)} %get-tuple-element.6), channel_id=1, source_target_pairs={{14,0},{113,1},{0,2},{115,3},{2,4},{117,5},{4,6},{119,7},{6,8},{12... | collective-permute-start | bytes 2359304 | tf_op jit(solution)/shard_map/ppermute | solution.py:284
  60.7 1.0 constant_dynamic-update-slice_fusion.6
  61.7 0.0 copy-start
  61.7 0.0 copy-start.1
  61.7 0.0 copy-start.2
  61.7 0.0 copy-start.3
  61.8 3.1 %collective-permute-start.4 = (bf16[48,16,128]{2,1,0:T(8,128)(2,1)S(1)}, bf16[48,16,128]{2,1,0:T(8,128)(2,1)S(1)}, u32[]{:S(2)}, u32[]{:S(2)}) collective-permute-start(bf16[48,16,128]{2,1,0:T(8,128)(2,1)S(1)} %slice.8), channel_id=1, source_target_pairs={{4,0},{33,1},{6,2},{35,3},{8,4},{37,5},{10,6},{39,7},{12,8},{41,9}... | collective-permute-start | bytes 589832 | tf_op jit(solution)/shard_map/ppermute | solution.py:284
  64.9 3.7 %collective-permute-start.5 = (bf16[48,16,128]{2,1,0:T(8,128)(2,1)S(1)}, bf16[48,16,128]{2,1,0:T(8,128)(2,1)S(1)}, u32[]{:S(2)}, u32[]{:S(2)}) collective-permute-start(bf16[48,16,128]{2,1,0:T(8,128)(2,1)S(1)} %slice.9), channel_id=1, source_target_pairs={{12,0},{97,1},{14,2},{99,3},{0,4},{101,5},{2,6},{103,7},{4,8},{105... | collective-permute-start | bytes 589832 | tf_op jit(solution)/shard_map/ppermute | solution.py:284
  68.7 0.1 constant_dynamic-update-slice_fusion.5
  68.7 0.1 constant_dynamic-update-slice_fusion.4
  68.8 0.0 collective-permute-done.2
  68.8 0.2 constant_dynamic-update-slice_fusion.3
  69.0 6.6 %collective-permute-done.3 = bf16[192,16,128]{2,1,0:T(8,128)(2,1)S(1)} collective-permute-done((bf16[192,16,128]{2,1,0:T(8,128)(2,1)S(1)}, bf16[192,16,128]{2,1,0:T(8,128)(2,1)S(1)}, u32[]{:S(2)}, u32[]{:S(2)}) %collective-permute-start.3) | collective-permute-done | bytes 786464 | tf_op jit(solution)/shard_map/ppermute | solution.py:284
  75.6 0.2 constant_dynamic-update-slice_fusion.2
  75.8 0.0 collective-permute-done.4
  75.8 0.0 collective-permute-done.5
  75.9 0.0 copy-start.4
  75.9 1.9 %collective-permute-start.6 = (bf16[768,16,128]{2,1,0:T(8,128)(2,1)S(1)}, bf16[768,16,128]{2,1,0:T(8,128)(2,1)S(1)}, u32[]{:S(2)}, u32[]{:S(2)}) collective-permute-start(bf16[768,16,128]{2,1,0:T(8,128)(2,1)S(1)} %constant_dynamic-update-slice_fusion.mine_hbm), channel_id=1, source_target_pairs={{0,1},{1,0},{2,3},{3,2},{4,5},{5,4},{6,7},{7,6},{8,9},{9,8},{10,11... | collective-permute-start | bytes 9437192 | tf_op jit(solution)/shard_map/ppermute | solution.py:297
  78.5 5.0 %collective-permute-done.6.other_hbm = bf16[768,16,128]{2,1,0:T(8,128)(2,1)S(1)} collective-permute-done((bf16[768,16,128]{2,1,0:T(8,128)(2,1)S(1)}, bf16[768,16,128]{2,1,0:T(8,128)(2,1)S(1)}, u32[]{:S(2)}, u32[]{:S(2)}) %collective-permute-start.6) | collective-permute-done | bytes 3145760 | tf_op jit(solution)/shard_map/ppermute | solution.py:297
  83.4 0.0 copy-start.5
  83.4 0.0 copy-done.4
  83.4 1.7 %copy-done.5 = bf16[768,16,128]{2,1,0:T(8,128)(2,1)} copy-done((bf16[768,16,128]{2,1,0:T(8,128)(2,1)}, bf16[768,16,128]{2,1,0:T(8,128)(2,1)S(1)}, u32[]{:S(2)}) %copy-start.5) | copy-done | bytes 3145752
  85.1 0.0 copy-done
  85.1 0.0 copy-done.1
  85.1 0.0 copy-done.2
  85.1 0.0 copy-done.3
  85.1 13.2 %front.1 = (bf16[256,2048]{1,0:T(8,128)(2,1)}, bf16[256,640]{1,0:T(8,128)(2,1)S(1)}) custom-call(s32[1]{0:T(128)S(6)} %copy.14.count_ref, bf16[768,16,128]{2,1,0:T(8,128)(2,1)} %copy-done.4, bf16[768,16,128]{2,1,0:T(8,128)(2,1)} %copy-done.5, bf16[256,2048]{1,0:T(8,128)(2,1)S(1)} %copy-done, bf16[256,512]{1,0:T(8,128)(2,1)S(1)} %copy-done.2, ...), custom_call_target="tpu_custom_call" | custom-call | tf_op jit(solution)/shard_map/front/pallas_call | solution.py:243
  98.3 0.1 reshape.14
  98.4 27.2 %all_to_all.11 = bf16[128,2,640]{2,1,0:T(2,128)(2,1)S(1)} all-to-all(bf16[128,2,640]{2,1,0:T(2,128)(2,1)S(1)} %reshape.14), channel_id=1, replica_groups=mesh['front'=4,'helper'=128] {'helper'}, dimensions={0} | all-to-all | bytes 655360 | tf_op jit(solution)/shard_map/all_to_all | solution.py:301
  125.7 0.8 reshape.15.got_ref
  126.5 1.9 %assemble.1 = f32[128,512]{1,0:T(8,128)} custom-call(bf16[256,640]{1,0:T(8,128)(2,1)} %reshape.15.got_ref), custom_call_target="tpu_custom_call" | custom-call | tf_op jit(solution)/shard_map/assemble/pallas_call | solution.py:273
  (4 shorter events, 0.1 us)
Async XLA Ops:
  29.1 15.5 %collective-permute-start = (bf16[96,16,128]{2,1,0:T(8,128)(2,1)}, bf16[96,16,128]{2,1,0:T(8,128)(2,1)S(1)}, u32[]{:S(2)}, u32[]{:S(2)}) collective-permute-start(bf16[96,16,128]{2,1,0:T(8,128)(2,1)} %pack.1), channel_id=1, source_target_pairs={{4,0},{33,1},{6,2},{35,3},{8,4},{37,5},{10,6},{39,7},{12,8},{41,9}... | collective-permute-start | bytes 1179656 | tf_op jit(solution)/shard_map/ppermute | solution.py:284
  38.0 12.1 %collective-permute-start.1 = (bf16[96,16,128]{2,1,0:T(8,128)(2,1)}, bf16[96,16,128]{2,1,0:T(8,128)(2,1)S(1)}, u32[]{:S(2)}, u32[]{:S(2)}) collective-permute-start(bf16[96,16,128]{2,1,0:T(8,128)(2,1)} %pack.1), channel_id=1, source_target_pairs={{12,0},{97,1},{14,2},{99,3},{0,4},{101,5},{2,6},{103,7},{4,8},{105... | collective-permute-start | bytes 1179656 | tf_op jit(solution)/shard_map/ppermute | solution.py:284
  51.2 17.6 %collective-permute-start.2 = (bf16[192,16,128]{2,1,0:T(8,128)(2,1)S(1)}, bf16[192,16,128]{2,1,0:T(8,128)(2,1)S(1)}, u32[]{:S(2)}, u32[]{:S(2)}) collective-permute-start(bf16[192,16,128]{2,1,0:T(8,128)(2,1)S(1)} %get-tuple-element.7), channel_id=1, source_target_pairs={{2,0},{17,1},{4,2},{19,3},{6,4},{21,5},{8,6},{23,7},{10,8},{25,9},... | collective-permute-start | bytes 2359304 | tf_op jit(solution)/shard_map/ppermute | solution.py:284
  58.4 17.2 %collective-permute-start.3 = (bf16[192,16,128]{2,1,0:T(8,128)(2,1)S(1)}, bf16[192,16,128]{2,1,0:T(8,128)(2,1)S(1)}, u32[]{:S(2)}, u32[]{:S(2)}) collective-permute-start(bf16[192,16,128]{2,1,0:T(8,128)(2,1)S(1)} %get-tuple-element.6), channel_id=1, source_target_pairs={{14,0},{113,1},{0,2},{115,3},{2,4},{117,5},{4,6},{119,7},{6,8},{12... | collective-permute-start | bytes 2359304 | tf_op jit(solution)/shard_map/ppermute | solution.py:284
  61.7 23.4 %copy-start = (bf16[256,2048]{1,0:T(8,128)(2,1)S(1)}, bf16[256,2048]{1,0:T(8,128)(2,1)}, u32[]{:S(2)}) copy-start(bf16[256,2048]{1,0:T(8,128)(2,1)} %rows_ref.3) | copy-start | bytes 3145732
  61.7 23.4 %copy-start.1 = (bf16[16,128,128]{2,1,0:T(8,128)(2,1)S(1)}, bf16[16,128,128]{2,1,0:T(8,128)(2,1)}, u32[]{:S(2)}) copy-start(bf16[16,128,128]{2,1,0:T(8,128)(2,1)} %inv_ref.1) | copy-start | bytes 1572868
  61.7 23.4 %copy-start.2 = (bf16[256,512]{1,0:T(8,128)(2,1)S(1)}, bf16[256,512]{1,0:T(8,128)(2,1)}, u32[]{:S(2)}) copy-start(bf16[256,512]{1,0:T(8,128)(2,1)} %block_ref.1) | copy-start | bytes 786436
  61.7 23.4 %copy-start.3 = (s32[256]{0:T(256)S(1)}, s32[256]{0:T(256)}, u32[]{:S(2)}) copy-start(s32[256]{0:T(256)} %param.11) | copy-start | bytes 3076
  61.8 14.0 %collective-permute-start.4 = (bf16[48,16,128]{2,1,0:T(8,128)(2,1)S(1)}, bf16[48,16,128]{2,1,0:T(8,128)(2,1)S(1)}, u32[]{:S(2)}, u32[]{:S(2)}) collective-permute-start(bf16[48,16,128]{2,1,0:T(8,128)(2,1)S(1)} %slice.8), channel_id=1, source_target_pairs={{4,0},{33,1},{6,2},{35,3},{8,4},{37,5},{10,6},{39,7},{12,8},{41,9}... | collective-permute-start | bytes 589832 | tf_op jit(solution)/shard_map/ppermute | solution.py:284
  64.9 10.9 %collective-permute-start.5 = (bf16[48,16,128]{2,1,0:T(8,128)(2,1)S(1)}, bf16[48,16,128]{2,1,0:T(8,128)(2,1)S(1)}, u32[]{:S(2)}, u32[]{:S(2)}) collective-permute-start(bf16[48,16,128]{2,1,0:T(8,128)(2,1)S(1)} %slice.9), channel_id=1, source_target_pairs={{12,0},{97,1},{14,2},{99,3},{0,4},{101,5},{2,6},{103,7},{4,8},{105... | collective-permute-start | bytes 589832 | tf_op jit(solution)/shard_map/ppermute | solution.py:284
  75.9 7.6 %copy-start.4 = (bf16[768,16,128]{2,1,0:T(8,128)(2,1)}, bf16[768,16,128]{2,1,0:T(8,128)(2,1)S(1)}, u32[]{:S(2)}) copy-start(bf16[768,16,128]{2,1,0:T(8,128)(2,1)S(1)} %constant_dynamic-update-slice_fusion.mine_hbm) | copy-start | bytes 9437188
  75.9 7.6 %collective-permute-start.6 = (bf16[768,16,128]{2,1,0:T(8,128)(2,1)S(1)}, bf16[768,16,128]{2,1,0:T(8,128)(2,1)S(1)}, u32[]{:S(2)}, u32[]{:S(2)}) collective-permute-start(bf16[768,16,128]{2,1,0:T(8,128)(2,1)S(1)} %constant_dynamic-update-slice_fusion.mine_hbm), channel_id=1, source_target_pairs={{0,1},{1,0},{2,3},{3,2},{4,5},{5,4},{6,7},{7,6},{8,9},{9,8},{10,11... | collective-permute-start | bytes 9437192 | tf_op jit(solution)/shard_map/ppermute | solution.py:297
  83.4 1.7 %copy-start.5 = (bf16[768,16,128]{2,1,0:T(8,128)(2,1)}, bf16[768,16,128]{2,1,0:T(8,128)(2,1)S(1)}, u32[]{:S(2)}) copy-start(bf16[768,16,128]{2,1,0:T(8,128)(2,1)S(1)} %collective-permute-done.6.other_hbm) | copy-start | bytes 9437188

commit v3 on v2

--- a/solution.py
+++ b/solution.py
@@ -59,7 +59,13 @@
     return lax.dot_general(a, b, dims, preferred_element_type=F32)
 
 
-def spread_kernel(panel_ref, rows_ref, out_ref, window):
+def spread_kernel(panel_hbm, rows_hbm, out_ref, panel_ref, rows_ref, window, sems):
+    panel_copy = pltpu.make_async_copy(panel_hbm, panel_ref, sems.at[0])
+    rows_copy = pltpu.make_async_copy(rows_hbm.at[pl.ds(0, 16)], rows_ref, sems.at[1])
+    panel_copy.start()
+    rows_copy.start()
+    panel_copy.wait()
+    rows_copy.wait()
     for j in range(NB):
         window[SR * j : SR * (j + 1), :] = rows_ref[:, BS * j : BS * (j + 1)].astype(F32)[:SR]
     leading = window[...].astype(BF16).reshape(SR, 16, BS)
@@ -70,13 +76,19 @@
 
 
 def spread_call(panel, rows):
+    hbm = pl.BlockSpec(memory_space=pltpu.HBM)
     return pl.pallas_call(
         spread_kernel,
-        grid=(1,),
         out_shape=jax.ShapeDtypeStruct((LINE, SENT, 16, BS), BF16),
-        in_specs=[pl.BlockSpec((16, NPIV), lambda i: (0, 0))] * 2,
-        out_specs=pl.BlockSpec((LINE, SENT, 16, BS), lambda i: (0, 0, 0, 0)),
-        scratch_shapes=[pltpu.VMEM((SR * NB, BS), F32)],
+        in_specs=[hbm, hbm],
+        out_specs=pl.BlockSpec(memory_space=pltpu.VMEM),
+        scratch_shapes=[
+            pltpu.VMEM((16, NPIV), BF16),
+            pltpu.VMEM((16, NPIV), BF16),
+            pltpu.VMEM((SR * NB, BS), F32),
+            pltpu.SemaphoreType.DMA((2,)),
+        ],
+        compiler_params=pltpu.CompilerParams(vmem_limit_bytes=8 * 1024 * 1024),
         name="spread",
     )(panel, rows)
 
@@ -111,72 +123,55 @@
         in_specs=[vmem],
         out_specs=vmem,
         scratch_shapes=[pltpu.VMEM((NB, SR * LINE, BS), F32)],
+        compiler_params=pltpu.CompilerParams(vmem_limit_bytes=8 * 1024 * 1024),
         name="pack",
     )(line)
 
 
-def block_copies(source, core, y, z, lt, xw, sem):
-    copies = []
-    label_sign = lax.rem(z, 2) == 0
-    for q, step in enumerate(FROM):
-        base = PIECES * q
-        if core == 0:
-            member = lax.rem(z + step + LINE, LINE)
-            window_row = 32 * member
-        else:
-            other = lax.rem(y + step + LINE, LINE)
-            member = jnp.where(label_sign, other, 7 - other)
-            window_row = 32 * member + SLAB // 2
-        copies.append(
-            pltpu.make_async_copy(
-                source.at[pl.ds(base + PAIRS * NB, 2 * NB)], xw.at[lax.div(window_row, 32)], sem
-            )
-        )
-        for p in range(PAIRS):
+def held_at(step):
+    place_of = jnp.int32(0)
+    for q, offset in enumerate(FROM):
+        place_of = jnp.where(step == (offset + LINE) % LINE, q, place_of)
+    return PIECES * place_of
+
+
+def put_tiles(first, second, y, z, lt, xw):
+    for core, source in ((0, first), (1, second)):
+        for member in range(LINE):
             if core == 0:
-                upper = jnp.where(member >= 4, 1, 0)
-                count = 14 - 2 * p + upper
-                large = helper(7 - p, member, 0)
-                small = helper(p, member, 0)
+                base = held_at(lax.rem(member - z + LINE, LINE))
             else:
-                upper = 1 if p >= 2 else 0
-                low = jnp.minimum(member, 7 - member)
+                at = jnp.where(lax.rem(z, 2) == 0, member, 7 - member)
+                base = held_at(lax.rem(at - y + LINE, LINE))
+            xw[core * LINE + member] = source[pl.ds(base + PAIRS * NB, 2 * NB)]
+            for p in range(PAIRS):
+                if core == 0:
+                    low, upper = p, member // 4
+                    large, small = helper(7 - p, member, 0), helper(p, member, 0)
+                else:
+                    low, upper = min(member, 7 - member), p // 2
+                    z_large = 2 * p + 1 if member <= 3 else 2 * p
+                    large, small = helper(7 - low, z_large, 1), helper(low, 4 * p + 1 - z_large, 1)
                 count = 14 - 2 * low + upper
-                z_large = jnp.where(member <= 3, 2 * p + 1, 2 * p)
-                large = helper(7 - low, z_large, 1)
-                small = helper(low, 4 * p + 1 - z_large, 1)
-            start = base + NB * p
-            copies.append(
-                pltpu.make_async_copy(
-                    source.at[pl.ds(start, NB)], lt.at[:, large], sem
-                )
-            )
-            copies.append(
-                pltpu.make_async_copy(
-                    source.at[pl.ds(start + count, NB // 2)], lt.at[pl.ds(0, NB // 2), small], sem
-                )
-            )
-    return copies
+                lt[:count, large] = source[pl.ds(base + NB * p, count)]
+                rest = 2 * low + upper
+                if rest:
+                    lt[:rest, small] = source[pl.ds(base + NB * p + count, rest)]
 
 
 def front_kernel(
-    count_ref, mine_hbm, other_hbm, rows_ref, block_ref, inv_ref, slot_ref,
-    factor_ref, send_ref, lt, xw, solved, wfac, sem,
+    count_ref, mine_ref, other_ref, rows_ref, block_ref, inv_ref, slot_ref,
+    factor_ref, send_ref, lt, xw, solved, wfac,
 ):
     y, z, core = place()
 
-    def copies(here):
-        refs = (mine_hbm, other_hbm) if here == 0 else (other_hbm, mine_hbm)
-        return block_copies(refs[0], 0, y, z, lt, xw, sem) + block_copies(refs[1], 1, y, z, lt, xw, sem)
-
-    for here in (0, 1):
-        @pl.when(core == here)
-        def _():
-            for c in copies(here):
-                c.start()
-
-    for c in copies(0):
-        c.wait()
+    @pl.when(core == 0)
+    def _():
+        put_tiles(mine_ref, other_ref, y, z, lt, xw)
+
+    @pl.when(core == 1)
+    def _():
+        put_tiles(other_ref, mine_ref, y, z, lt, xw)
 
     live_count = UNIT * count_ref[0]
     live = lax.broadcasted_iota(jnp.int32, (ROWS, 1), 0) < live_count
@@ -187,25 +182,37 @@
     def panel_piece(j, top, count):
         return lt[j, top // 16 : (top + count) // 16].reshape(count, BS)
 
+    def start_block(k):
+        return jnp.concatenate([window_piece(k), rows_ref[:, BS * k : BS * (k + 1)]], axis=0).astype(F32)
+
+    def scale(part, k):
+        f = dot(part, inv_ref[k]).astype(BF16)
+        wfac[:, BS * k : BS * (k + 1)] = f[:SLAB]
+        factor_ref[:, BS * k : BS * (k + 1)] = jnp.where(live, f[SLAB:], jnp.zeros((), BF16))
+
+    def pair(s):
+        return jnp.concatenate([start_block(2 * s), start_block(2 * s + 1)], axis=1)
+
+    pending = pair(0)
+    last = None
     for s in range(NB // 2):
         lo = 256 * s
         k0, k1 = 2 * s, 2 * s + 1
-        x0 = jnp.concatenate([window_piece(k0), rows_ref[:, lo : lo + BS]], axis=0).astype(F32)
-        x1 = jnp.concatenate([window_piece(k1), rows_ref[:, lo + BS : lo + 256]], axis=0).astype(F32)
+        x = pending
         if s > 0:
-            panel = jnp.concatenate([panel_piece(j, lo, 256) for j in range(k0)], axis=1)
-            update = dot(solved[:, :lo], panel, NT)
-            x0 = x0 - update[:, :BS]
-            x1 = x1 - update[:, BS:]
-        s0 = x0.astype(BF16)
-        x1 = x1 - dot(s0, panel_piece(k0, lo + BS, BS), NT)
-        s1 = x1.astype(BF16)
-        solved[:, lo : lo + BS] = s0
-        solved[:, lo + BS : lo + 256] = s1
-        for part, base in ((s0, lo), (s1, lo + BS)):
-            f = dot(part, inv_ref[base // BS]).astype(BF16)
-            wfac[:, base : base + BS] = f[:SLAB]
-            factor_ref[:, base : base + BS] = jnp.where(live, f[SLAB:], jnp.zeros((), BF16))
+            panel = jnp.concatenate([panel_piece(j, lo, 256) for j in (k0 - 2, k0 - 1)], axis=1)
+            x = x - dot(last, panel, NT)
+        s0 = x[:, :BS].astype(BF16)
+        if s + 1 < NB // 2:
+            pending = pair(s + 1)
+            if s > 0:
+                panel = jnp.concatenate([panel_piece(j, lo + 256, 256) for j in range(k0)], axis=1)
+                pending = pending - dot(solved[:, :lo], panel, NT)
+        s1 = (x[:, BS:] - dot(s0, panel_piece(k0, lo + BS, BS), NT)).astype(BF16)
+        last = jnp.concatenate([s0, s1], axis=1)
+        solved[:, lo : lo + 256] = last
+        scale(s0, k0)
+        scale(s1, k1)
 
     held = lax.broadcasted_iota(jnp.int32, (1, SLAB), 1)
     group = lax.shift_right_logical(held, 5) & 7
@@ -239,23 +246,21 @@
 
 def front_call(mine, other, rows, block, inverse, count, slot):
     vmem = pl.BlockSpec(memory_space=pltpu.VMEM)
-    hbm = pl.BlockSpec(memory_space=pl.ANY)
     return pl.pallas_call(
         front_kernel,
         out_shape=(
             jax.ShapeDtypeStruct((ROWS, NPIV), BF16),
             jax.ShapeDtypeStruct((SLOTS, WIDE), BF16),
         ),
-        in_specs=[pl.BlockSpec(memory_space=pltpu.SMEM), hbm, hbm, vmem, vmem, vmem, vmem],
+        in_specs=[pl.BlockSpec(memory_space=pltpu.SMEM)] + [vmem] * 6,
         out_specs=(vmem, vmem),
         scratch_shapes=[
             pltpu.VMEM((NB, HELPERS, 16, BS), BF16),
             pltpu.VMEM((2 * LINE, 2 * NB, 16, BS), BF16),
             pltpu.VMEM((ALL, NPIV), BF16),
             pltpu.VMEM((SLAB, NPIV), BF16),
-            pltpu.SemaphoreType.DMA,
         ],
-        compiler_params=pltpu.CompilerParams(vmem_limit_bytes=50 * 1024 * 1024),
+        compiler_params=pltpu.CompilerParams(vmem_limit_bytes=32 * 1024 * 1024),
         name="front",
     )(count, mine, other, rows, block, inverse, slot)
 
@@ -275,6 +280,7 @@
         out_shape=jax.ShapeDtypeStruct((PROWS, SLAB), F32),
         in_specs=[vmem],
         out_specs=vmem,
+        compiler_params=pltpu.CompilerParams(vmem_limit_bytes=8 * 1024 * 1024),
         name="assemble",
     )(got)
 

time: 129 us -> 115 us (0.89)
  Pallas kernels: 18.9 us -> 7.95 us
  local copies, waits for them, and re-layouts: 4.25 us -> 2.93 us
    pallas_call x1, Pallas kernels: 13.2 us -> 6.6 us  [front_call(): pl.pallas_call(front_kernel, out_shape=(jax.ShapeDtypeStruct((ROWS, NPIV)...]
    pallas_call x1, Pallas kernels: 2 us -> 0.2 us  [pack_call(): pl.pallas_call(pack_kernel, out_shape=jax.ShapeDtypeStruct((PIECES, 16, B...]
    pallas_call x1, Pallas kernels: 1.77 us -> 0.23 us  [spread_call(): pl.pallas_call(spread_kernel, out_shape=jax.ShapeDtypeStruct((LINE, SENT,...]
  transfers between devices with their start and end apart: 7 -> 7, of which waited for: 4 -> 5; matrix products, arithmetic and copies ran while one was open for 1% -> 0% of each run, Pallas kernels for 0% -> 0%
where the time goes in v3:
time: 115 us
  blocking collectives  50.9 us (44%)
  starting transfers between devices  29.2 us (25%)
  waiting for transfers between devices  22.3 us (19%)
  Pallas kernels  7.95 us (7%)
  local copies, waits for them, and re-layouts  2.93 us (3%)
  between operations  1.5 us (1%)
    ppermute x6, starting transfers between devices, receive(): return lax.ppermute(block, 'helper', from_offset(step))  27.1 us
    all_to_all x1, blocking collectives, per_device(): lax.all_to_all(send.reshape(HELPERS, CAP, WIDE), 'helper', split_axis=0,...  26.5 us
    all_to_all x1, blocking collectives, per_device(): lax.all_to_all(spread_call(lower_panel, lower_rows), 'helper', 0, 0, tile...  24.4 us
    ppermute x6, waiting for transfers between devices, receive(): return lax.ppermute(block, 'helper', from_offset(step))  17.6 us
    pallas_call x1, Pallas kernels, front_call(): pl.pallas_call(front_kernel, out_shape=(jax.ShapeDtypeStruct((ROWS, NPIV)...  6.6 us
    ppermute x1, waiting for transfers between devices, per_device(): other = lax.ppermute(mine, 'helper', [(h, h ^ 1) for h in range(HELPERS)])  4.73 us
    unnamed x18, local copies, waits for them, and re-layouts  2.62 us
  transfers between devices with their start and end apart: 7, of which 5 were waited for; matrix products, arithmetic and copies ran while one was open for 0% of the time, Pallas kernels for 0%

profile of v3, /device:TPU:6, one launch (start us, length us, event | category | flops | bytes accessed | tf_op | source)
XLA Modules:
  0.0 114.9 jit_solution(16037949886000011351)
XLA Ops:
  0.6 0.0 copy-start
  0.6 1.2 %copy-done = bf16[256,2048]{1,0:T(8,128)(2,1)S(1)} copy-done((bf16[256,2048]{1,0:T(8,128)(2,1)S(1)}, bf16[256,2048]{1,0:T(8,128)(2,1)}, u32[]{:S(2)}) %copy-start) | copy-done | bytes 1048600
  1.9 0.0 copy-start.4
  1.9 0.8 copy-done.4
  2.7 0.2 spread.1
  2.9 24.4 %all_to_all.10.line_ref = bf16[8,19,16,128]{3,2,1,0:T(8,128)(2,1)S(1)} all-to-all(bf16[8,19,16,128]{3,2,1,0:T(8,128)(2,1)S(1)} %spread.1), channel_id=1, replica_groups={{0,16,32,48,64,80,96,112},{2,18,34,50,66,82,98,114},{4,20,36,52,68,84,1..., dimensions={0} | all-to-all | bytes 1245184 | tf_op jit(solution)/shard_map/all_to_all | solution.py:292
  27.4 0.2 pack.1
  27.6 8.9 %collective-permute-start = (bf16[96,16,128]{2,1,0:T(8,128)(2,1)S(1)}, bf16[96,16,128]{2,1,0:T(8,128)(2,1)S(1)}, u32[]{:S(2)}, u32[]{:S(2)}) collective-permute-start(bf16[96,16,128]{2,1,0:T(8,128)(2,1)S(1)} %pack.1), channel_id=1, source_target_pairs={{4,0},{33,1},{6,2},{35,3},{8,4},{37,5},{10,6},{39,7},{12,8},{41,9}... | collective-permute-start | bytes 1179656 | tf_op jit(solution)/shard_map/ppermute | solution.py:290
  36.4 1.9 %collective-permute-start.1 = (bf16[96,16,128]{2,1,0:T(8,128)(2,1)S(1)}, bf16[96,16,128]{2,1,0:T(8,128)(2,1)S(1)}, u32[]{:S(2)}, u32[]{:S(2)}) collective-permute-start(bf16[96,16,128]{2,1,0:T(8,128)(2,1)S(1)} %pack.1), channel_id=1, source_target_pairs={{12,0},{97,1},{14,2},{99,3},{0,4},{101,5},{2,6},{103,7},{4,8},{105... | collective-permute-start | bytes 1179656 | tf_op jit(solution)/shard_map/ppermute | solution.py:290
  38.4 7.6 %collective-permute-done = bf16[96,16,128]{2,1,0:T(8,128)(2,1)S(1)} collective-permute-done((bf16[96,16,128]{2,1,0:T(8,128)(2,1)S(1)}, bf16[96,16,128]{2,1,0:T(8,128)(2,1)S(1)}, u32[]{:S(2)}, u32[]{:S(2)}) %collective-permute-start) | collective-permute-done | bytes 393248 | tf_op jit(solution)/shard_map/ppermute | solution.py:290
  46.0 2.4 %collective-permute-done.1 = bf16[96,16,128]{2,1,0:T(8,128)(2,1)S(1)} collective-permute-done((bf16[96,16,128]{2,1,0:T(8,128)(2,1)S(1)}, bf16[96,16,128]{2,1,0:T(8,128)(2,1)S(1)}, u32[]{:S(2)}, u32[]{:S(2)}) %collective-permute-start.1) | collective-permute-done | bytes 393248 | tf_op jit(solution)/shard_map/ppermute | solution.py:290
  48.4 0.1 pad_maximum_fusion
  48.5 7.1 %collective-permute-start.2 = (bf16[192,16,128]{2,1,0:T(8,128)(2,1)S(1)}, bf16[192,16,128]{2,1,0:T(8,128)(2,1)S(1)}, u32[]{:S(2)}, u32[]{:S(2)}) collective-permute-start(bf16[192,16,128]{2,1,0:T(8,128)(2,1)S(1)} %get-tuple-element.7), channel_id=1, source_target_pairs={{2,0},{17,1},{4,2},{19,3},{6,4},{21,5},{8,6},{23,7},{10,8},{25,9},... | collective-permute-start | bytes 2359304 | tf_op jit(solution)/shard_map/ppermute | solution.py:290
  55.6 2.3 %collective-permute-start.3 = (bf16[192,16,128]{2,1,0:T(8,128)(2,1)S(1)}, bf16[192,16,128]{2,1,0:T(8,128)(2,1)S(1)}, u32[]{:S(2)}, u32[]{:S(2)}) collective-permute-start(bf16[192,16,128]{2,1,0:T(8,128)(2,1)S(1)} %get-tuple-element.6), channel_id=1, source_target_pairs={{14,0},{113,1},{0,2},{115,3},{2,4},{117,5},{4,6},{119,7},{6,8},{12... | collective-permute-start | bytes 2359304 | tf_op jit(solution)/shard_map/ppermute | solution.py:290
  57.9 0.0 copy-start.1
  58.0 0.0 copy-start.2
  58.0 0.0 copy-start.3
  58.0 0.0 copy-start.5
  58.0 3.1 %collective-permute-start.4 = (bf16[48,16,128]{2,1,0:T(8,128)(2,1)S(1)}, bf16[48,16,128]{2,1,0:T(8,128)(2,1)S(1)}, u32[]{:S(2)}, u32[]{:S(2)}) collective-permute-start(bf16[48,16,128]{2,1,0:T(8,128)(2,1)S(1)} %slice.8), channel_id=1, source_target_pairs={{4,0},{33,1},{6,2},{35,3},{8,4},{37,5},{10,6},{39,7},{12,8},{41,9}... | collective-permute-start | bytes 589832 | tf_op jit(solution)/shard_map/ppermute | solution.py:290
  61.2 3.7 %collective-permute-start.5 = (bf16[48,16,128]{2,1,0:T(8,128)(2,1)S(1)}, bf16[48,16,128]{2,1,0:T(8,128)(2,1)S(1)}, u32[]{:S(2)}, u32[]{:S(2)}) collective-permute-start(bf16[48,16,128]{2,1,0:T(8,128)(2,1)S(1)} %slice.9), channel_id=1, source_target_pairs={{12,0},{97,1},{14,2},{99,3},{0,4},{101,5},{2,6},{103,7},{4,8},{105... | collective-permute-start | bytes 589832 | tf_op jit(solution)/shard_map/ppermute | solution.py:290
  64.9 0.1 constant_dynamic-update-slice_fusion.5
  65.0 0.1 constant_dynamic-update-slice_fusion.4
  65.0 0.9 collective-permute-done.2
  65.9 0.2 constant_dynamic-update-slice_fusion.3
  66.1 6.7 %collective-permute-done.3 = bf16[192,16,128]{2,1,0:T(8,128)(2,1)S(1)} collective-permute-done((bf16[192,16,128]{2,1,0:T(8,128)(2,1)S(1)}, bf16[192,16,128]{2,1,0:T(8,128)(2,1)S(1)}, u32[]{:S(2)}, u32[]{:S(2)}) %collective-permute-start.3) | collective-permute-done | bytes 786464 | tf_op jit(solution)/shard_map/ppermute | solution.py:290
  72.8 0.2 constant_dynamic-update-slice_fusion.2
  73.0 0.0 collective-permute-done.4
  73.0 0.0 collective-permute-done.5
  73.1 2.2 %collective-permute-start.6 = (bf16[768,16,128]{2,1,0:T(8,128)(2,1)S(1)}, bf16[768,16,128]{2,1,0:T(8,128)(2,1)S(1)}, u32[]{:S(2)}, u32[]{:S(2)}) collective-permute-start(bf16[768,16,128]{2,1,0:T(8,128)(2,1)S(1)} %constant_dynamic-update-slice_fusion.mine_ref), channel_id=1, source_target_pairs={{0,1},{1,0},{2,3},{3,2},{4,5},{5,4},{6,7},{7,6},{8,9},{9,8},{10,11... | collective-permute-start | bytes 9437192 | tf_op jit(solution)/shard_map/ppermute | solution.py:303
  75.9 4.7 %collective-permute-done.6.other_ref = bf16[768,16,128]{2,1,0:T(8,128)(2,1)S(1)} collective-permute-done((bf16[768,16,128]{2,1,0:T(8,128)(2,1)S(1)}, bf16[768,16,128]{2,1,0:T(8,128)(2,1)S(1)}, u32[]{:S(2)}, u32[]{:S(2)}) %collective-permute-start.6) | collective-permute-done | bytes 3145760 | tf_op jit(solution)/shard_map/ppermute | solution.py:303
  80.6 0.0 copy-done.1
  80.6 0.0 copy-done.2
  80.7 0.0 copy-done.3
  80.7 0.0 copy-done.5
  80.7 6.6 %front.1 = (bf16[256,2048]{1,0:T(8,128)(2,1)}, bf16[256,640]{1,0:T(8,128)(2,1)S(1)}) custom-call(s32[1]{0:T(128)S(6)} %copy.14.count_ref, bf16[768,16,128]{2,1,0:T(8,128)(2,1)S(1)} %constant_dynamic-update-slice_fusion.mine_ref, bf16[768,16,128]{2,1,0:T(8,128)(2,1)S(1)} %collective-permute-done.6.other_ref, bf16[256,2048]{1,0:T(8,128)(2,1)S(1)} %copy-done.1, ...), custom_call_target="tpu_custom_call" | custom-call | tf_op jit(solution)/shard_map/front/pallas_call | solution.py:249
  87.3 0.1 reshape.14
  87.4 26.5 %all_to_all.11 = bf16[128,2,640]{2,1,0:T(2,128)(2,1)S(1)} all-to-all(bf16[128,2,640]{2,1,0:T(2,128)(2,1)S(1)} %reshape.14), channel_id=1, replica_groups=mesh['front'=4,'helper'=128] {'helper'}, dimensions={0} | all-to-all | bytes 655360 | tf_op jit(solution)/shard_map/all_to_all | solution.py:307
  113.9 0.1 reshape.15.got_ref
  114.0 0.9 assemble.1
  (5 shorter events, 0.1 us)
Async XLA Ops:
  0.6 1.2 %copy-start = (bf16[256,2048]{1,0:T(8,128)(2,1)S(1)}, bf16[256,2048]{1,0:T(8,128)(2,1)}, u32[]{:S(2)}) copy-start(bf16[256,2048]{1,0:T(8,128)(2,1)} %rows_ref.1) | copy-start | bytes 3145732
  1.9 0.8 copy-start.4
  27.6 18.4 %collective-permute-start = (bf16[96,16,128]{2,1,0:T(8,128)(2,1)S(1)}, bf16[96,16,128]{2,1,0:T(8,128)(2,1)S(1)}, u32[]{:S(2)}, u32[]{:S(2)}) collective-permute-start(bf16[96,16,128]{2,1,0:T(8,128)(2,1)S(1)} %pack.1), channel_id=1, source_target_pairs={{4,0},{33,1},{6,2},{35,3},{8,4},{37,5},{10,6},{39,7},{12,8},{41,9}... | collective-permute-start | bytes 1179656 | tf_op jit(solution)/shard_map/ppermute | solution.py:290
  36.4 11.9 %collective-permute-start.1 = (bf16[96,16,128]{2,1,0:T(8,128)(2,1)S(1)}, bf16[96,16,128]{2,1,0:T(8,128)(2,1)S(1)}, u32[]{:S(2)}, u32[]{:S(2)}) collective-permute-start(bf16[96,16,128]{2,1,0:T(8,128)(2,1)S(1)} %pack.1), channel_id=1, source_target_pairs={{12,0},{97,1},{14,2},{99,3},{0,4},{101,5},{2,6},{103,7},{4,8},{105... | collective-permute-start | bytes 1179656 | tf_op jit(solution)/shard_map/ppermute | solution.py:290
  48.5 17.4 %collective-permute-start.2 = (bf16[192,16,128]{2,1,0:T(8,128)(2,1)S(1)}, bf16[192,16,128]{2,1,0:T(8,128)(2,1)S(1)}, u32[]{:S(2)}, u32[]{:S(2)}) collective-permute-start(bf16[192,16,128]{2,1,0:T(8,128)(2,1)S(1)} %get-tuple-element.7), channel_id=1, source_target_pairs={{2,0},{17,1},{4,2},{19,3},{6,4},{21,5},{8,6},{23,7},{10,8},{25,9},... | collective-permute-start | bytes 2359304 | tf_op jit(solution)/shard_map/ppermute | solution.py:290
  55.6 17.2 %collective-permute-start.3 = (bf16[192,16,128]{2,1,0:T(8,128)(2,1)S(1)}, bf16[192,16,128]{2,1,0:T(8,128)(2,1)S(1)}, u32[]{:S(2)}, u32[]{:S(2)}) collective-permute-start(bf16[192,16,128]{2,1,0:T(8,128)(2,1)S(1)} %get-tuple-element.6), channel_id=1, source_target_pairs={{14,0},{113,1},{0,2},{115,3},{2,4},{117,5},{4,6},{119,7},{6,8},{12... | collective-permute-start | bytes 2359304 | tf_op jit(solution)/shard_map/ppermute | solution.py:290
  57.9 22.7 %copy-start.1 = (bf16[256,2048]{1,0:T(8,128)(2,1)S(1)}, bf16[256,2048]{1,0:T(8,128)(2,1)}, u32[]{:S(2)}) copy-start(bf16[256,2048]{1,0:T(8,128)(2,1)} %rows_ref.1) | copy-start | bytes 3145732
  58.0 22.7 %copy-start.2 = (bf16[16,128,128]{2,1,0:T(8,128)(2,1)S(1)}, bf16[16,128,128]{2,1,0:T(8,128)(2,1)}, u32[]{:S(2)}) copy-start(bf16[16,128,128]{2,1,0:T(8,128)(2,1)} %inv_ref.1) | copy-start | bytes 1572868
  58.0 22.7 %copy-start.3 = (bf16[256,512]{1,0:T(8,128)(2,1)S(1)}, bf16[256,512]{1,0:T(8,128)(2,1)}, u32[]{:S(2)}) copy-start(bf16[256,512]{1,0:T(8,128)(2,1)} %block_ref.1) | copy-start | bytes 786436
  58.0 22.7 %copy-start.5 = (s32[256]{0:T(256)S(1)}, s32[256]{0:T(256)}, u32[]{:S(2)}) copy-start(s32[256]{0:T(256)} %param.11) | copy-start | bytes 3076
  58.0 15.0 %collective-permute-start.4 = (bf16[48,16,128]{2,1,0:T(8,128)(2,1)S(1)}, bf16[48,16,128]{2,1,0:T(8,128)(2,1)S(1)}, u32[]{:S(2)}, u32[]{:S(2)}) collective-permute-start(bf16[48,16,128]{2,1,0:T(8,128)(2,1)S(1)} %slice.8), channel_id=1, source_target_pairs={{4,0},{33,1},{6,2},{35,3},{8,4},{37,5},{10,6},{39,7},{12,8},{41,9}... | collective-permute-start | bytes 589832 | tf_op jit(solution)/shard_map/ppermute | solution.py:290
  61.2 11.9 %collective-permute-start.5 = (bf16[48,16,128]{2,1,0:T(8,128)(2,1)S(1)}, bf16[48,16,128]{2,1,0:T(8,128)(2,1)S(1)}, u32[]{:S(2)}, u32[]{:S(2)}) collective-permute-start(bf16[48,16,128]{2,1,0:T(8,128)(2,1)S(1)} %slice.9), channel_id=1, source_target_pairs={{12,0},{97,1},{14,2},{99,3},{0,4},{101,5},{2,6},{103,7},{4,8},{105... | collective-permute-start | bytes 589832 | tf_op jit(solution)/shard_map/ppermute | solution.py:290
  73.1 7.6 %collective-permute-start.6 = (bf16[768,16,128]{2,1,0:T(8,128)(2,1)S(1)}, bf16[768,16,128]{2,1,0:T(8,128)(2,1)S(1)}, u32[]{:S(2)}, u32[]{:S(2)}) collective-permute-start(bf16[768,16,128]{2,1,0:T(8,128)(2,1)S(1)} %constant_dynamic-update-slice_fusion.mine_ref), channel_id=1, source_target_pairs={{0,1},{1,0},{2,3},{3,2},{4,5},{5,4},{6,7},{7,6},{8,9},{9,8},{10,11... | collective-permute-start | bytes 9437192 | tf_op jit(solution)/shard_map/ppermute | solution.py:303

commit v4 on v3

--- a/solution.py
+++ b/solution.py
@@ -28,7 +28,7 @@
 PAIRS = 4
 SENT = NB - 1 + SR
 PIECES = PAIRS * NB + 2 * NB
-FROM = (0, 2, -2, 1, 3, -1, -3, 4)
+FROM = (0, 1, -1, 2, -2, 3, -3, 4)
 
 
 def helper(y, z, core):
@@ -59,38 +59,27 @@
     return lax.dot_general(a, b, dims, preferred_element_type=F32)
 
 
-def spread_kernel(panel_hbm, rows_hbm, out_ref, panel_ref, rows_ref, window, sems):
-    panel_copy = pltpu.make_async_copy(panel_hbm, panel_ref, sems.at[0])
-    rows_copy = pltpu.make_async_copy(rows_hbm.at[pl.ds(0, 16)], rows_ref, sems.at[1])
-    panel_copy.start()
-    rows_copy.start()
-    panel_copy.wait()
-    rows_copy.wait()
+def spread_kernel(held_ref, out_ref, window):
     for j in range(NB):
-        window[SR * j : SR * (j + 1), :] = rows_ref[:, BS * j : BS * (j + 1)].astype(F32)[:SR]
+        window[SR * j : SR * (j + 1), :] = held_ref[16:, BS * j : BS * (j + 1)].astype(F32)[:SR]
     leading = window[...].astype(BF16).reshape(SR, 16, BS)
     for d in range(LINE):
         for j in range(NB - 1):
-            out_ref[d, j] = panel_ref[:, BS * j : BS * (j + 1)]
+            out_ref[d, j] = held_ref[:16, BS * j : BS * (j + 1)]
         out_ref[d, NB - 1 :] = leading
 
 
-def spread_call(panel, rows):
-    hbm = pl.BlockSpec(memory_space=pltpu.HBM)
+def spread_call(held):
+    vmem = pl.BlockSpec(memory_space=pltpu.VMEM)
     return pl.pallas_call(
         spread_kernel,
         out_shape=jax.ShapeDtypeStruct((LINE, SENT, 16, BS), BF16),
-        in_specs=[hbm, hbm],
-        out_specs=pl.BlockSpec(memory_space=pltpu.VMEM),
-        scratch_shapes=[
-            pltpu.VMEM((16, NPIV), BF16),
-            pltpu.VMEM((16, NPIV), BF16),
-            pltpu.VMEM((SR * NB, BS), F32),
-            pltpu.SemaphoreType.DMA((2,)),
-        ],
+        in_specs=[vmem],
+        out_specs=vmem,
+        scratch_shapes=[pltpu.VMEM((SR * NB, BS), F32)],
         compiler_params=pltpu.CompilerParams(vmem_limit_bytes=8 * 1024 * 1024),
         name="spread",
-    )(panel, rows)
+    )(held)
 
 
 def pack_kernel(line_ref, out_ref, window):
@@ -159,8 +148,54 @@
                     lt[:rest, small] = source[pl.ds(base + NB * p + count, rest)]
 
 
+def prepare_kernel(count_ref, slot_ref, block_ref, held_ref, order_ref, chosen_ref, local_ref):
+    live_count = UNIT * count_ref[0]
+    held = lax.broadcasted_iota(jnp.int32, (1, SLAB), 1)
+    group = lax.shift_right_logical(held, 5) & 7
+    turn = lax.shift_right_logical(held, 2) & 7
+    first_half = held < SLAB // 2
+    held_y = jnp.where(first_half, turn, jnp.where((turn & 1) == 0, group, 7 - group))
+    held_z = jnp.where(first_half, group, turn)
+    column = 64 * held_y + 8 * held_z + jnp.where(first_half, 0, 4) + (held & 3)
+    order = jnp.where(
+        lax.broadcasted_iota(jnp.int32, (SLAB, SLAB), 0) == column, 1.0, 0.0
+    ).astype(BF16)
+
+    slot = slot_ref[...]
+    owner_row = jnp.broadcast_to(lax.shift_right_logical(slot, 7).astype(F32), (ROWS, ROWS))
+    owner_col = owner_row.T
+    local_row = jnp.broadcast_to((slot & 127).astype(F32) + 1.0, (BS, ROWS))
+    local_ref[...] = local_row.T.astype(BF16)
+    i0 = lax.broadcasted_iota(jnp.int32, (ROWS, ROWS), 0)
+    i1 = lax.broadcasted_iota(jnp.int32, (ROWS, ROWS), 1)
+    earlier = jnp.where((owner_row == owner_col) & (i0 < i1) & (i0 < live_count), 1.0, 0.0)
+    rank = jnp.sum(earlier, axis=0, keepdims=True)
+    target = owner_row * CAP + rank
+    chosen_ref[...] = jnp.where((target == i0.astype(F32)) & (i1 < live_count), 1.0, 0.0).astype(BF16)
+    held_ref[...] = dot(block_ref[...], order)
+    order_ref[...] = order
+
+
+def prepare_call(count, slot, block):
+    vmem = pl.BlockSpec(memory_space=pltpu.VMEM)
+    return pl.pallas_call(
+        prepare_kernel,
+        out_shape=(
+            jax.ShapeDtypeStruct((ROWS, SLAB), F32),
+            jax.ShapeDtypeStruct((SLAB, SLAB), BF16),
+            jax.ShapeDtypeStruct((SLOTS, ROWS), BF16),
+            jax.ShapeDtypeStruct((ROWS, BS), BF16),
+        ),
+        in_specs=[pl.BlockSpec(memory_space=pltpu.SMEM), vmem, vmem],
+        out_specs=(vmem,) * 4,
+        compiler_params=pltpu.CompilerParams(vmem_limit_bytes=8 * 1024 * 1024),
+        cost_estimate=pl.CostEstimate(flops=2 * ROWS * SLAB * SLAB, bytes_accessed=1 << 20, transcendentals=0),
+        name="prepare",
+    )(count, slot, block)
+
+
 def front_kernel(
-    count_ref, mine_ref, other_ref, rows_ref, block_ref, inv_ref, slot_ref,
+    count_ref, mine_ref, other_ref, rows_ref, inv_ref, block_ref, order_ref, chosen_ref, local_ref,
     factor_ref, send_ref, lt, xw, solved, wfac,
 ):
     y, z, core = place()
@@ -214,37 +249,15 @@
         scale(s0, k0)
         scale(s1, k1)
 
-    held = lax.broadcasted_iota(jnp.int32, (1, SLAB), 1)
-    group = lax.shift_right_logical(held, 5) & 7
-    turn = lax.shift_right_logical(held, 2) & 7
-    first_half = held < SLAB // 2
-    held_y = jnp.where(first_half, turn, jnp.where((turn & 1) == 0, group, 7 - group))
-    held_z = jnp.where(first_half, group, turn)
-    column = 64 * held_y + 8 * held_z + jnp.where(first_half, 0, 4) + (held & 3)
-    order = jnp.where(
-        lax.broadcasted_iota(jnp.int32, (SLAB, SLAB), 0) == column, 1.0, 0.0
-    ).astype(BF16)
-
     product = dot(solved[SLAB:, :], wfac[...], NT)
-    held_contribution = (dot(block_ref[...], order) - product).astype(BF16)
-    contribution = dot(held_contribution, order, NT).astype(BF16)
-
-    slot = slot_ref[...]
-    owner_row = jnp.broadcast_to(lax.shift_right_logical(slot, 7).astype(F32), (ROWS, ROWS))
-    owner_col = owner_row.T
-    local_row = jnp.broadcast_to((slot & 127).astype(F32) + 1.0, (BS, ROWS))
-    local_col = local_row.T.astype(BF16)
-    i0 = lax.broadcasted_iota(jnp.int32, (ROWS, ROWS), 0)
-    i1 = lax.broadcasted_iota(jnp.int32, (ROWS, ROWS), 1)
-    earlier = jnp.where((owner_row == owner_col) & (i0 < i1) & (i0 < live_count), 1.0, 0.0)
-    rank = jnp.sum(earlier, axis=0, keepdims=True)
-    target = owner_row * CAP + rank
-    chosen = jnp.where((target == i0.astype(F32)) & (i1 < live_count), 1.0, 0.0).astype(BF16)
-    payload = jnp.concatenate([contribution, local_col], axis=1)
-    send_ref[...] = dot(chosen, payload).astype(BF16)
-
-
-def front_call(mine, other, rows, block, inverse, count, slot):
+    held_contribution = (block_ref[...] - product).astype(BF16)
+    contribution = dot(held_contribution, order_ref[...], NT).astype(BF16)
+
+    payload = jnp.concatenate([contribution, local_ref[...]], axis=1)
+    send_ref[...] = dot(chosen_ref[...], payload).astype(BF16)
+
+
+def front_call(mine, other, rows, inverse, count, prepared):
     vmem = pl.BlockSpec(memory_space=pltpu.VMEM)
     return pl.pallas_call(
         front_kernel,
@@ -252,7 +265,7 @@
             jax.ShapeDtypeStruct((ROWS, NPIV), BF16),
             jax.ShapeDtypeStruct((SLOTS, WIDE), BF16),
         ),
-        in_specs=[pl.BlockSpec(memory_space=pltpu.SMEM)] + [vmem] * 6,
+        in_specs=[pl.BlockSpec(memory_space=pltpu.SMEM)] + [vmem] * 8,
         out_specs=(vmem, vmem),
         scratch_shapes=[
             pltpu.VMEM((NB, HELPERS, 16, BS), BF16),
@@ -262,7 +275,7 @@
         ],
         compiler_params=pltpu.CompilerParams(vmem_limit_bytes=32 * 1024 * 1024),
         name="front",
-    )(count, mine, other, rows, block, inverse, slot)
+    )(count, mine, other, rows, inverse, *prepared)
 
 
 def assemble_kernel(got_ref, out_ref):
@@ -290,19 +303,20 @@
         return lax.ppermute(block, "helper", from_offset(step))
 
     line = lax.all_to_all(
-        spread_call(lower_panel, lower_rows), "helper", 0, 0, tiled=True, axis_index_groups=line_groups()
+        spread_call(jnp.concatenate([lower_panel, lower_rows[:16]])), "helper", 0, 0, tiled=True, axis_index_groups=line_groups()
     )
     own = pack_call(line)
     half = PIECES // 2
-    after = receive(own, 2)
-    before = receive(own, -2)
-    above = receive(jnp.concatenate([own, after]), 1)
-    below = receive(jnp.concatenate([own, before]), -1)
-    far = [receive(after[:half], 2), receive(before[half:], -2)]
-    mine = jnp.concatenate([own, after, before, above, below] + far)
+    up, down = receive(own, 1), receive(own, -1)
+    up2, down2 = receive(own, 2), receive(own, -2)
+    mine = jnp.concatenate(
+        [own, up, down, up2, down2]
+        + [receive(up2, 1), receive(down2, -1), receive(up2[:half], 2), receive(down2[half:], -2)]
+    )
     other = lax.ppermute(mine, "helper", [(h, h ^ 1) for h in range(HELPERS)])
     factor, send = front_call(
-        mine, other, lower_rows, window_block, pivot_inverse, block_count, parent_slot.reshape(1, ROWS)
+        mine, other, lower_rows, pivot_inverse, block_count,
+        prepare_call(block_count, parent_slot.reshape(1, ROWS), window_block),
     )
     got = lax.all_to_all(
         send.reshape(HELPERS, CAP, WIDE), "helper", split_axis=0, concat_axis=0, tiled=True

time: 115 us -> 111 us (0.965)
  waiting for transfers between devices: 22.3 us -> 13.3 us
  starting transfers between devices: 29.2 us -> 37 us
  blocking collectives: 50.9 us -> 48.7 us
  local copies, waits for them, and re-layouts: 2.93 us -> 1.55 us
    ppermute x6 -> x8, waiting for transfers between devices: 17.6 us -> 8.66 us  [receive(): return lax.ppermute(block, 'helper', from_offset(step))]
    ppermute x6 -> x8, starting transfers between devices: 27.1 us -> 35.1 us  [receive(): return lax.ppermute(block, 'helper', from_offset(step))]
    unnamed x18 -> x16, local copies, waits for them, and re-layouts: 2.62 us -> 0.4 us
    all_to_all x1, blocking collectives: 26.5 us -> 24.3 us  [per_device(): lax.all_to_all(send.reshape(HELPERS, CAP, WIDE), 'helper', split_axis=0,...]
  transfers between devices with their start and end apart: 7 -> 9, of which waited for: 5 -> 3; matrix products, arithmetic and copies ran while one was open for 0% -> 0% of each run, Pallas kernels for 0% -> 0%
where the time goes in v4:
time: 111 us
  blocking collectives  48.7 us (44%)
  starting transfers between devices  37 us (33%)
  waiting for transfers between devices  13.3 us (12%)
  Pallas kernels  7.96 us (7%)
  between operations  1.57 us (1%)
  local copies, waits for them, and re-layouts  1.55 us (1%)
    ppermute x8, starting transfers between devices, receive(): return lax.ppermute(block, 'helper', from_offset(step))  35.1 us
    all_to_all x1, blocking collectives, per_device(): lax.all_to_all(spread_call(jnp.concatenate([lower_panel, lower_rows[:16]]...  24.4 us
    all_to_all x1, blocking collectives, per_device(): lax.all_to_all(send.reshape(HELPERS, CAP, WIDE), 'helper', split_axis=0,...  24.3 us
    ppermute x8, waiting for transfers between devices, receive(): return lax.ppermute(block, 'helper', from_offset(step))  8.66 us
    pallas_call x1, Pallas kernels, front_call(): pl.pallas_call(front_kernel, out_shape=(jax.ShapeDtypeStruct((ROWS, NPIV)...  6.44 us
    ppermute x1, waiting for transfers between devices, per_device(): other = lax.ppermute(mine, 'helper', [(h, h ^ 1) for h in range(HELPERS)])  4.62 us
  transfers between devices with their start and end apart: 9, of which 3 were waited for; matrix products, arithmetic and copies ran while one was open for 0% of the time, Pallas kernels for 0%

profile of v4, /device:TPU:6, one launch (start us, length us, event | category | flops | bytes accessed | tf_op | source)
XLA Modules:
  0.0 111.0 jit_solution(18104653128960194787)
XLA Ops:
  0.6 0.8 slice.9
  1.5 0.8 pad_maximum_fusion.held_ref
  2.3 0.1 spread.1
  2.4 24.4 %all_to_all.10.line_ref = bf16[8,19,16,128]{3,2,1,0:T(8,128)(2,1)S(1)} all-to-all(bf16[8,19,16,128]{3,2,1,0:T(8,128)(2,1)S(1)} %spread.1), channel_id=1, replica_groups={{0,16,32,48,64,80,96,112},{2,18,34,50,66,82,98,114},{4,20,36,52,68,84,1..., dimensions={0} | all-to-all | bytes 1245184 | tf_op jit(solution)/shard_map/all_to_all | solution.py:305
  26.8 0.2 pack.1
  27.0 8.9 %collective-permute-start.2 = (bf16[96,16,128]{2,1,0:T(8,128)(2,1)S(1)}, bf16[96,16,128]{2,1,0:T(8,128)(2,1)S(1)}, u32[]{:S(2)}, u32[]{:S(2)}) collective-permute-start(bf16[96,16,128]{2,1,0:T(8,128)(2,1)S(1)} %pack.1), channel_id=1, source_target_pairs={{4,0},{33,1},{6,2},{35,3},{8,4},{37,5},{10,6},{39,7},{12,8},{41,9}... | collective-permute-start | bytes 1179656 | tf_op jit(solution)/shard_map/ppermute | solution.py:303
  35.9 1.9 %collective-permute-start.3 = (bf16[96,16,128]{2,1,0:T(8,128)(2,1)S(1)}, bf16[96,16,128]{2,1,0:T(8,128)(2,1)S(1)}, u32[]{:S(2)}, u32[]{:S(2)}) collective-permute-start(bf16[96,16,128]{2,1,0:T(8,128)(2,1)S(1)} %pack.1), channel_id=1, source_target_pairs={{12,0},{97,1},{14,2},{99,3},{0,4},{101,5},{2,6},{103,7},{4,8},{105... | collective-permute-start | bytes 1179656 | tf_op jit(solution)/shard_map/ppermute | solution.py:303
  37.8 7.3 %collective-permute-start = (bf16[96,16,128]{2,1,0:T(8,128)(2,1)S(1)}, bf16[96,16,128]{2,1,0:T(8,128)(2,1)S(1)}, u32[]{:S(2)}, u32[]{:S(2)}) collective-permute-start(bf16[96,16,128]{2,1,0:T(8,128)(2,1)S(1)} %pack.1), channel_id=1, source_target_pairs={{2,0},{17,1},{4,2},{19,3},{6,4},{21,5},{8,6},{23,7},{10,8},{25,9},... | collective-permute-start | bytes 1179656 | tf_op jit(solution)/shard_map/ppermute | solution.py:303
  45.1 1.9 %collective-permute-start.1 = (bf16[96,16,128]{2,1,0:T(8,128)(2,1)S(1)}, bf16[96,16,128]{2,1,0:T(8,128)(2,1)S(1)}, u32[]{:S(2)}, u32[]{:S(2)}) collective-permute-start(bf16[96,16,128]{2,1,0:T(8,128)(2,1)S(1)} %pack.1), channel_id=1, source_target_pairs={{14,0},{113,1},{0,2},{115,3},{2,4},{117,5},{4,6},{119,7},{6,8},{12... | collective-permute-start | bytes 1179656 | tf_op jit(solution)/shard_map/ppermute | solution.py:303
  47.1 0.0 copy-start.2
  47.1 0.0 copy-start.3
  47.1 0.0 collective-permute-done.2
  47.1 0.0 copy-start
  47.1 0.0 copy-start.1
  47.1 5.1 %collective-permute-start.6 = (bf16[48,16,128]{2,1,0:T(8,128)(2,1)S(1)}, bf16[48,16,128]{2,1,0:T(8,128)(2,1)S(1)}, u32[]{:S(2)}, u32[]{:S(2)}) collective-permute-start(bf16[48,16,128]{2,1,0:T(8,128)(2,1)S(1)} %slice.12), channel_id=1, source_target_pairs={{4,0},{33,1},{6,2},{35,3},{8,4},{37,5},{10,6},{39,7},{12,8},{41,9}... | collective-permute-start | bytes 589832 | tf_op jit(solution)/shard_map/ppermute | solution.py:303
  52.2 0.0 collective-permute-done.3
  52.3 1.9 %collective-permute-start.7 = (bf16[48,16,128]{2,1,0:T(8,128)(2,1)S(1)}, bf16[48,16,128]{2,1,0:T(8,128)(2,1)S(1)}, u32[]{:S(2)}, u32[]{:S(2)}) collective-permute-start(bf16[48,16,128]{2,1,0:T(8,128)(2,1)S(1)} %slice.13), channel_id=1, source_target_pairs={{12,0},{97,1},{14,2},{99,3},{0,4},{101,5},{2,6},{103,7},{4,8},{105... | collective-permute-start | bytes 589832 | tf_op jit(solution)/shard_map/ppermute | solution.py:303
  54.2 6.2 %collective-permute-start.4 = (bf16[96,16,128]{2,1,0:T(8,128)(2,1)S(1)}, bf16[96,16,128]{2,1,0:T(8,128)(2,1)S(1)}, u32[]{:S(2)}, u32[]{:S(2)}) collective-permute-start(bf16[96,16,128]{2,1,0:T(8,128)(2,1)S(1)} %collective-permute-done.2), channel_id=1, source_target_pairs={{2,0},{17,1},{4,2},{19,3},{6,4},{21,5},{8,6},{23,7},{10,8},{25,9},... | collective-permute-start | bytes 1179656 | tf_op jit(solution)/shard_map/ppermute | solution.py:303
  60.4 0.0 collective-permute-done
  60.4 1.9 %collective-permute-start.5 = (bf16[96,16,128]{2,1,0:T(8,128)(2,1)S(1)}, bf16[96,16,128]{2,1,0:T(8,128)(2,1)S(1)}, u32[]{:S(2)}, u32[]{:S(2)}) collective-permute-start(bf16[96,16,128]{2,1,0:T(8,128)(2,1)S(1)} %collective-permute-done.3), channel_id=1, source_target_pairs={{14,0},{113,1},{0,2},{115,3},{2,4},{117,5},{4,6},{119,7},{6,8},{12... | collective-permute-start | bytes 1179656 | tf_op jit(solution)/shard_map/ppermute | solution.py:303
  62.4 0.1 constant_dynamic-update-slice_fusion.7
  62.4 0.0 collective-permute-done.1
  62.4 0.1 constant_dynamic-update-slice_fusion.6
  62.5 0.1 constant_dynamic-update-slice_fusion.5
  62.6 0.1 constant_dynamic-update-slice_fusion.4
  62.6 3.1 %collective-permute-done.4 = bf16[96,16,128]{2,1,0:T(8,128)(2,1)S(1)} collective-permute-done((bf16[96,16,128]{2,1,0:T(8,128)(2,1)S(1)}, bf16[96,16,128]{2,1,0:T(8,128)(2,1)S(1)}, u32[]{:S(2)}, u32[]{:S(2)}) %collective-permute-start.4) | collective-permute-done | bytes 393248 | tf_op jit(solution)/shard_map/ppermute | solution.py:303
  65.7 0.1 constant_dynamic-update-slice_fusion.3
  65.7 5.6 %collective-permute-done.5 = bf16[96,16,128]{2,1,0:T(8,128)(2,1)S(1)} collective-permute-done((bf16[96,16,128]{2,1,0:T(8,128)(2,1)S(1)}, bf16[96,16,128]{2,1,0:T(8,128)(2,1)S(1)}, u32[]{:S(2)}, u32[]{:S(2)}) %collective-permute-start.5) | collective-permute-done | bytes 393248 | tf_op jit(solution)/shard_map/ppermute | solution.py:303
  71.3 0.1 constant_dynamic-update-slice_fusion.2
  71.4 0.0 collective-permute-done.6
  71.4 0.0 collective-permute-done.7
  71.5 1.9 %collective-permute-start.8 = (bf16[768,16,128]{2,1,0:T(8,128)(2,1)S(1)}, bf16[768,16,128]{2,1,0:T(8,128)(2,1)S(1)}, u32[]{:S(2)}, u32[]{:S(2)}) collective-permute-start(bf16[768,16,128]{2,1,0:T(8,128)(2,1)S(1)} %constant_dynamic-update-slice_fusion.mine_ref), channel_id=1, source_target_pairs={{0,1},{1,0},{2,3},{3,2},{4,5},{5,4},{6,7},{7,6},{8,9},{9,8},{10,11... | collective-permute-start | bytes 9437192 | tf_op jit(solution)/shard_map/ppermute | solution.py:316
  74.0 0.0 copy-done.2
  74.0 0.0 copy-done.3
  74.1 0.3 prepare.1
  74.4 4.6 %collective-permute-done.8.other_ref = bf16[768,16,128]{2,1,0:T(8,128)(2,1)S(1)} collective-permute-done((bf16[768,16,128]{2,1,0:T(8,128)(2,1)S(1)}, bf16[768,16,128]{2,1,0:T(8,128)(2,1)S(1)}, u32[]{:S(2)}, u32[]{:S(2)}) %collective-permute-start.8) | collective-permute-done | bytes 3145760 | tf_op jit(solution)/shard_map/ppermute | solution.py:316
  79.0 0.0 copy-done
  79.0 0.0 copy-done.1
  79.0 6.4 %front.1 = (bf16[256,2048]{1,0:T(8,128)(2,1)}, bf16[256,640]{1,0:T(8,128)(2,1)S(1)}) custom-call(s32[1]{0:T(128)S(6)} %copy.16.count_ref, bf16[768,16,128]{2,1,0:T(8,128)(2,1)S(1)} %constant_dynamic-update-slice_fusion.mine_ref, bf16[768,16,128]{2,1,0:T(8,128)(2,1)S(1)} %collective-permute-done.8.other_ref, bf16[256,2048]{1,0:T(8,128)(2,1)S(1)} %copy-done, ...), custom_call_target="tpu_custom_call" | custom-call | tf_op jit(solution)/shard_map/front/pallas_call | solution.py:262
  85.5 0.1 reshape.14
  85.6 24.3 %all_to_all.11 = bf16[128,2,640]{2,1,0:T(2,128)(2,1)S(1)} all-to-all(bf16[128,2,640]{2,1,0:T(2,128)(2,1)S(1)} %reshape.14), channel_id=1, replica_groups=mesh['front'=4,'helper'=128] {'helper'}, dimensions={0} | all-to-all | bytes 655360 | tf_op jit(solution)/shard_map/all_to_all | solution.py:321
  109.9 0.1 reshape.15.got_ref
  110.0 0.9 assemble.1
  (5 shorter events, 0.1 us)
Async XLA Ops:
  27.0 20.1 %collective-permute-start.2 = (bf16[96,16,128]{2,1,0:T(8,128)(2,1)S(1)}, bf16[96,16,128]{2,1,0:T(8,128)(2,1)S(1)}, u32[]{:S(2)}, u32[]{:S(2)}) collective-permute-start(bf16[96,16,128]{2,1,0:T(8,128)(2,1)S(1)} %pack.1), channel_id=1, source_target_pairs={{4,0},{33,1},{6,2},{35,3},{8,4},{37,5},{10,6},{39,7},{12,8},{41,9}... | collective-permute-start | bytes 1179656 | tf_op jit(solution)/shard_map/ppermute | solution.py:303
  35.9 16.3 %collective-permute-start.3 = (bf16[96,16,128]{2,1,0:T(8,128)(2,1)S(1)}, bf16[96,16,128]{2,1,0:T(8,128)(2,1)S(1)}, u32[]{:S(2)}, u32[]{:S(2)}) collective-permute-start(bf16[96,16,128]{2,1,0:T(8,128)(2,1)S(1)} %pack.1), channel_id=1, source_target_pairs={{12,0},{97,1},{14,2},{99,3},{0,4},{101,5},{2,6},{103,7},{4,8},{105... | collective-permute-start | bytes 1179656 | tf_op jit(solution)/shard_map/ppermute | solution.py:303
  37.8 22.6 %collective-permute-start = (bf16[96,16,128]{2,1,0:T(8,128)(2,1)S(1)}, bf16[96,16,128]{2,1,0:T(8,128)(2,1)S(1)}, u32[]{:S(2)}, u32[]{:S(2)}) collective-permute-start(bf16[96,16,128]{2,1,0:T(8,128)(2,1)S(1)} %pack.1), channel_id=1, source_target_pairs={{2,0},{17,1},{4,2},{19,3},{6,4},{21,5},{8,6},{23,7},{10,8},{25,9},... | collective-permute-start | bytes 1179656 | tf_op jit(solution)/shard_map/ppermute | solution.py:303
  45.1 17.3 %collective-permute-start.1 = (bf16[96,16,128]{2,1,0:T(8,128)(2,1)S(1)}, bf16[96,16,128]{2,1,0:T(8,128)(2,1)S(1)}, u32[]{:S(2)}, u32[]{:S(2)}) collective-permute-start(bf16[96,16,128]{2,1,0:T(8,128)(2,1)S(1)} %pack.1), channel_id=1, source_target_pairs={{14,0},{113,1},{0,2},{115,3},{2,4},{117,5},{4,6},{119,7},{6,8},{12... | collective-permute-start | bytes 1179656 | tf_op jit(solution)/shard_map/ppermute | solution.py:303
  47.1 27.0 %copy-start.2 = (bf16[256,512]{1,0:T(8,128)(2,1)S(1)}, bf16[256,512]{1,0:T(8,128)(2,1)}, u32[]{:S(2)}) copy-start(bf16[256,512]{1,0:T(8,128)(2,1)} %block_ref.1) | copy-start | bytes 786436
  47.1 27.0 %copy-start.3 = (s32[256]{0:T(256)S(1)}, s32[256]{0:T(256)}, u32[]{:S(2)}) copy-start(s32[256]{0:T(256)} %param.11) | copy-start | bytes 3076
  47.1 31.9 %copy-start = (bf16[256,2048]{1,0:T(8,128)(2,1)S(1)}, bf16[256,2048]{1,0:T(8,128)(2,1)}, u32[]{:S(2)}) copy-start(bf16[256,2048]{1,0:T(8,128)(2,1)} %rows_ref.1) | copy-start | bytes 3145732
  47.1 31.9 %copy-start.1 = (bf16[16,128,128]{2,1,0:T(8,128)(2,1)S(1)}, bf16[16,128,128]{2,1,0:T(8,128)(2,1)}, u32[]{:S(2)}) copy-start(bf16[16,128,128]{2,1,0:T(8,128)(2,1)} %inv_ref.1) | copy-start | bytes 1572868
  47.1 24.2 %collective-permute-start.6 = (bf16[48,16,128]{2,1,0:T(8,128)(2,1)S(1)}, bf16[48,16,128]{2,1,0:T(8,128)(2,1)S(1)}, u32[]{:S(2)}, u32[]{:S(2)}) collective-permute-start(bf16[48,16,128]{2,1,0:T(8,128)(2,1)S(1)} %slice.12), channel_id=1, source_target_pairs={{4,0},{33,1},{6,2},{35,3},{8,4},{37,5},{10,6},{39,7},{12,8},{41,9}... | collective-permute-start | bytes 589832 | tf_op jit(solution)/shard_map/ppermute | solution.py:303
  52.3 19.2 %collective-permute-start.7 = (bf16[48,16,128]{2,1,0:T(8,128)(2,1)S(1)}, bf16[48,16,128]{2,1,0:T(8,128)(2,1)S(1)}, u32[]{:S(2)}, u32[]{:S(2)}) collective-permute-start(bf16[48,16,128]{2,1,0:T(8,128)(2,1)S(1)} %slice.13), channel_id=1, source_target_pairs={{12,0},{97,1},{14,2},{99,3},{0,4},{101,5},{2,6},{103,7},{4,8},{105... | collective-permute-start | bytes 589832 | tf_op jit(solution)/shard_map/ppermute | solution.py:303
  54.2 11.5 %collective-permute-start.4 = (bf16[96,16,128]{2,1,0:T(8,128)(2,1)S(1)}, bf16[96,16,128]{2,1,0:T(8,128)(2,1)S(1)}, u32[]{:S(2)}, u32[]{:S(2)}) collective-permute-start(bf16[96,16,128]{2,1,0:T(8,128)(2,1)S(1)} %collective-permute-done.2), channel_id=1, source_target_pairs={{2,0},{17,1},{4,2},{19,3},{6,4},{21,5},{8,6},{23,7},{10,8},{25,9},... | collective-permute-start | bytes 1179656 | tf_op jit(solution)/shard_map/ppermute | solution.py:303
  60.4 10.9 %collective-permute-start.5 = (bf16[96,16,128]{2,1,0:T(8,128)(2,1)S(1)}, bf16[96,16,128]{2,1,0:T(8,128)(2,1)S(1)}, u32[]{:S(2)}, u32[]{:S(2)}) collective-permute-start(bf16[96,16,128]{2,1,0:T(8,128)(2,1)S(1)} %collective-permute-done.3), channel_id=1, source_target_pairs={{14,0},{113,1},{0,2},{115,3},{2,4},{117,5},{4,6},{119,7},{6,8},{12... | collective-permute-start | bytes 1179656 | tf_op jit(solution)/shard_map/ppermute | solution.py:303
  71.5 7.6 %collective-permute-start.8 = (bf16[768,16,128]{2,1,0:T(8,128)(2,1)S(1)}, bf16[768,16,128]{2,1,0:T(8,128)(2,1)S(1)}, u32[]{:S(2)}, u32[]{:S(2)}) collective-permute-start(bf16[768,16,128]{2,1,0:T(8,128)(2,1)S(1)} %constant_dynamic-update-slice_fusion.mine_ref), channel_id=1, source_target_pairs={{0,1},{1,0},{2,3},{3,2},{4,5},{5,4},{6,7},{7,6},{8,9},{9,8},{10,11... | collective-permute-start | bytes 9437192 | tf_op jit(solution)/shard_map/ppermute | solution.py:316

commit v5 on v4

--- a/solution.py
+++ b/solution.py
@@ -228,26 +228,42 @@
     def pair(s):
         return jnp.concatenate([start_block(2 * s), start_block(2 * s + 1)], axis=1)
 
-    pending = pair(0)
-    last = None
+    groups = ((0, 512), (512, 768))
+
+    def start_rows(k, g):
+        r0, r1 = groups[g]
+        parts = []
+        if r0 < SLAB:
+            parts.append(window_piece(k)[r0 : min(r1, SLAB)])
+        if r1 > SLAB:
+            parts.append(rows_ref[max(r0, SLAB) - SLAB : r1 - SLAB, BS * k : BS * (k + 1)])
+        return jnp.concatenate(parts, axis=0).astype(F32)
+
+    def pair2(s, g):
+        return jnp.concatenate([start_rows(2 * s, g), start_rows(2 * s + 1, g)], axis=1)
+
+    pend = [pair2(0, g) for g in range(len(groups))]
+    lasts = [None] * len(groups)
     for s in range(NB // 2):
         lo = 256 * s
         k0, k1 = 2 * s, 2 * s + 1
-        x = pending
+        xs = list(pend)
         if s > 0:
             panel = jnp.concatenate([panel_piece(j, lo, 256) for j in (k0 - 2, k0 - 1)], axis=1)
-            x = x - dot(last, panel, NT)
-        s0 = x[:, :BS].astype(BF16)
+            xs = [xs[g] - dot(lasts[g], panel, NT) for g in range(len(groups))]
+        s0s = [x[:, :BS].astype(BF16) for x in xs]
         if s + 1 < NB // 2:
-            pending = pair(s + 1)
+            pend = [pair2(s + 1, g) for g in range(len(groups))]
             if s > 0:
                 panel = jnp.concatenate([panel_piece(j, lo + 256, 256) for j in range(k0)], axis=1)
-                pending = pending - dot(solved[:, :lo], panel, NT)
-        s1 = (x[:, BS:] - dot(s0, panel_piece(k0, lo + BS, BS), NT)).astype(BF16)
-        last = jnp.concatenate([s0, s1], axis=1)
-        solved[:, lo : lo + 256] = last
-        scale(s0, k0)
-        scale(s1, k1)
+                pend = [pend[g] - dot(solved[r0:r1, :lo], panel, NT) for g, (r0, r1) in enumerate(groups)]
+        diag = panel_piece(k0, lo + BS, BS)
+        s1s = [(xs[g][:, BS:] - dot(s0s[g], diag, NT)).astype(BF16) for g in range(len(groups))]
+        lasts = [jnp.concatenate([s0s[g], s1s[g]], axis=1) for g in range(len(groups))]
+        for g, (r0, r1) in enumerate(groups):
+            solved[r0:r1, lo : lo + 256] = lasts[g]
+        scale(jnp.concatenate(s0s, axis=0), k0)
+        scale(jnp.concatenate(s1s, axis=0), k1)
 
     product = dot(solved[SLAB:, :], wfac[...], NT)
     held_contribution = (block_ref[...] - product).astype(BF16)

time: 111 us -> 111 us (level)
  no operation moved by 1% of the time
where the time goes in v5:
time: 111 us
  blocking collectives  48.7 us (44%)
  starting transfers between devices  37 us (33%)
  waiting for transfers between devices  13.3 us (12%)
  Pallas kernels  7.58 us (7%)
  between operations  1.56 us (1%)
  local copies, waits for them, and re-layouts  1.55 us (1%)
    ppermute x8, starting transfers between devices, receive(): return lax.ppermute(block, 'helper', from_offset(step))  35.1 us
    all_to_all x1, blocking collectives, per_device(): lax.all_to_all(spread_call(jnp.concatenate([lower_panel, lower_rows[:16]]...  24.4 us
    all_to_all x1, blocking collectives, per_device(): lax.all_to_all(send.reshape(HELPERS, CAP, WIDE), 'helper', split_axis=0,...  24.3 us
    ppermute x8, waiting for transfers between devices, receive(): return lax.ppermute(block, 'helper', from_offset(step))  8.66 us
    pallas_call x1, Pallas kernels, front_call(): pl.pallas_call(front_kernel, out_shape=(jax.ShapeDtypeStruct((ROWS, NPIV)...  6.05 us
    ppermute x1, waiting for transfers between devices, per_device(): other = lax.ppermute(mine, 'helper', [(h, h ^ 1) for h in range(HELPERS)])  4.62 us
  transfers between devices with their start and end apart: 9, of which 3 were waited for; matrix products, arithmetic and copies ran while one was open for 0% of the time, Pallas kernels for 0%

profile of v5, /device:TPU:6, one launch (start us, length us, event | category | flops | bytes accessed | tf_op | source)
XLA Modules:
  0.0 110.6 jit_solution(14858576469741756806)
XLA Ops:
  0.6 0.8 slice.9
  1.5 0.8 pad_maximum_fusion.held_ref
  2.3 0.1 spread.1
  2.4 24.4 %all_to_all.10.line_ref = bf16[8,19,16,128]{3,2,1,0:T(8,128)(2,1)S(1)} all-to-all(bf16[8,19,16,128]{3,2,1,0:T(8,128)(2,1)S(1)} %spread.1), channel_id=1, replica_groups={{0,16,32,48,64,80,96,112},{2,18,34,50,66,82,98,114},{4,20,36,52,68,84,1..., dimensions={0} | all-to-all | bytes 1245184 | tf_op jit(solution)/shard_map/all_to_all | solution.py:321
  26.8 0.2 pack.1
  27.0 8.9 %collective-permute-start.2 = (bf16[96,16,128]{2,1,0:T(8,128)(2,1)S(1)}, bf16[96,16,128]{2,1,0:T(8,128)(2,1)S(1)}, u32[]{:S(2)}, u32[]{:S(2)}) collective-permute-start(bf16[96,16,128]{2,1,0:T(8,128)(2,1)S(1)} %pack.1), channel_id=1, source_target_pairs={{4,0},{33,1},{6,2},{35,3},{8,4},{37,5},{10,6},{39,7},{12,8},{41,9}... | collective-permute-start | bytes 1179656 | tf_op jit(solution)/shard_map/ppermute | solution.py:319
  35.9 1.9 %collective-permute-start.3 = (bf16[96,16,128]{2,1,0:T(8,128)(2,1)S(1)}, bf16[96,16,128]{2,1,0:T(8,128)(2,1)S(1)}, u32[]{:S(2)}, u32[]{:S(2)}) collective-permute-start(bf16[96,16,128]{2,1,0:T(8,128)(2,1)S(1)} %pack.1), channel_id=1, source_target_pairs={{12,0},{97,1},{14,2},{99,3},{0,4},{101,5},{2,6},{103,7},{4,8},{105... | collective-permute-start | bytes 1179656 | tf_op jit(solution)/shard_map/ppermute | solution.py:319
  37.8 7.3 %collective-permute-start = (bf16[96,16,128]{2,1,0:T(8,128)(2,1)S(1)}, bf16[96,16,128]{2,1,0:T(8,128)(2,1)S(1)}, u32[]{:S(2)}, u32[]{:S(2)}) collective-permute-start(bf16[96,16,128]{2,1,0:T(8,128)(2,1)S(1)} %pack.1), channel_id=1, source_target_pairs={{2,0},{17,1},{4,2},{19,3},{6,4},{21,5},{8,6},{23,7},{10,8},{25,9},... | collective-permute-start | bytes 1179656 | tf_op jit(solution)/shard_map/ppermute | solution.py:319
  45.1 1.9 %collective-permute-start.1 = (bf16[96,16,128]{2,1,0:T(8,128)(2,1)S(1)}, bf16[96,16,128]{2,1,0:T(8,128)(2,1)S(1)}, u32[]{:S(2)}, u32[]{:S(2)}) collective-permute-start(bf16[96,16,128]{2,1,0:T(8,128)(2,1)S(1)} %pack.1), channel_id=1, source_target_pairs={{14,0},{113,1},{0,2},{115,3},{2,4},{117,5},{4,6},{119,7},{6,8},{12... | collective-permute-start | bytes 1179656 | tf_op jit(solution)/shard_map/ppermute | solution.py:319
  47.1 0.0 copy-start.2
  47.1 0.0 copy-start.3
  47.1 0.0 collective-permute-done.2
  47.1 0.0 copy-start
  47.1 0.0 copy-start.1
  47.1 5.1 %collective-permute-start.6 = (bf16[48,16,128]{2,1,0:T(8,128)(2,1)S(1)}, bf16[48,16,128]{2,1,0:T(8,128)(2,1)S(1)}, u32[]{:S(2)}, u32[]{:S(2)}) collective-permute-start(bf16[48,16,128]{2,1,0:T(8,128)(2,1)S(1)} %slice.12), channel_id=1, source_target_pairs={{4,0},{33,1},{6,2},{35,3},{8,4},{37,5},{10,6},{39,7},{12,8},{41,9}... | collective-permute-start | bytes 589832 | tf_op jit(solution)/shard_map/ppermute | solution.py:319
  52.2 0.0 collective-permute-done.3
  52.3 1.9 %collective-permute-start.7 = (bf16[48,16,128]{2,1,0:T(8,128)(2,1)S(1)}, bf16[48,16,128]{2,1,0:T(8,128)(2,1)S(1)}, u32[]{:S(2)}, u32[]{:S(2)}) collective-permute-start(bf16[48,16,128]{2,1,0:T(8,128)(2,1)S(1)} %slice.13), channel_id=1, source_target_pairs={{12,0},{97,1},{14,2},{99,3},{0,4},{101,5},{2,6},{103,7},{4,8},{105... | collective-permute-start | bytes 589832 | tf_op jit(solution)/shard_map/ppermute | solution.py:319
  54.2 6.2 %collective-permute-start.4 = (bf16[96,16,128]{2,1,0:T(8,128)(2,1)S(1)}, bf16[96,16,128]{2,1,0:T(8,128)(2,1)S(1)}, u32[]{:S(2)}, u32[]{:S(2)}) collective-permute-start(bf16[96,16,128]{2,1,0:T(8,128)(2,1)S(1)} %collective-permute-done.2), channel_id=1, source_target_pairs={{2,0},{17,1},{4,2},{19,3},{6,4},{21,5},{8,6},{23,7},{10,8},{25,9},... | collective-permute-start | bytes 1179656 | tf_op jit(solution)/shard_map/ppermute | solution.py:319
  60.4 0.0 collective-permute-done
  60.4 1.9 %collective-permute-start.5 = (bf16[96,16,128]{2,1,0:T(8,128)(2,1)S(1)}, bf16[96,16,128]{2,1,0:T(8,128)(2,1)S(1)}, u32[]{:S(2)}, u32[]{:S(2)}) collective-permute-start(bf16[96,16,128]{2,1,0:T(8,128)(2,1)S(1)} %collective-permute-done.3), channel_id=1, source_target_pairs={{14,0},{113,1},{0,2},{115,3},{2,4},{117,5},{4,6},{119,7},{6,8},{12... | collective-permute-start | bytes 1179656 | tf_op jit(solution)/shard_map/ppermute | solution.py:319
  62.4 0.1 constant_dynamic-update-slice_fusion.7
  62.4 0.0 collective-permute-done.1
  62.4 0.1 constant_dynamic-update-slice_fusion.6
  62.5 0.1 constant_dynamic-update-slice_fusion.5
  62.6 0.1 constant_dynamic-update-slice_fusion.4
  62.6 3.1 %collective-permute-done.4 = bf16[96,16,128]{2,1,0:T(8,128)(2,1)S(1)} collective-permute-done((bf16[96,16,128]{2,1,0:T(8,128)(2,1)S(1)}, bf16[96,16,128]{2,1,0:T(8,128)(2,1)S(1)}, u32[]{:S(2)}, u32[]{:S(2)}) %collective-permute-start.4) | collective-permute-done | bytes 393248 | tf_op jit(solution)/shard_map/ppermute | solution.py:319
  65.7 0.1 constant_dynamic-update-slice_fusion.3
  65.7 5.6 %collective-permute-done.5 = bf16[96,16,128]{2,1,0:T(8,128)(2,1)S(1)} collective-permute-done((bf16[96,16,128]{2,1,0:T(8,128)(2,1)S(1)}, bf16[96,16,128]{2,1,0:T(8,128)(2,1)S(1)}, u32[]{:S(2)}, u32[]{:S(2)}) %collective-permute-start.5) | collective-permute-done | bytes 393248 | tf_op jit(solution)/shard_map/ppermute | solution.py:319
  71.3 0.1 constant_dynamic-update-slice_fusion.2
  71.4 0.0 collective-permute-done.6
  71.4 0.0 collective-permute-done.7
  71.5 1.9 %collective-permute-start.8 = (bf16[768,16,128]{2,1,0:T(8,128)(2,1)S(1)}, bf16[768,16,128]{2,1,0:T(8,128)(2,1)S(1)}, u32[]{:S(2)}, u32[]{:S(2)}) collective-permute-start(bf16[768,16,128]{2,1,0:T(8,128)(2,1)S(1)} %constant_dynamic-update-slice_fusion.mine_ref), channel_id=1, source_target_pairs={{0,1},{1,0},{2,3},{3,2},{4,5},{5,4},{6,7},{7,6},{8,9},{9,8},{10,11... | collective-permute-start | bytes 9437192 | tf_op jit(solution)/shard_map/ppermute | solution.py:332
  74.0 0.0 copy-done.2
  74.0 0.0 copy-done.3
  74.1 0.3 prepare.1
  74.4 4.6 %collective-permute-done.8.other_ref = bf16[768,16,128]{2,1,0:T(8,128)(2,1)S(1)} collective-permute-done((bf16[768,16,128]{2,1,0:T(8,128)(2,1)S(1)}, bf16[768,16,128]{2,1,0:T(8,128)(2,1)S(1)}, u32[]{:S(2)}, u32[]{:S(2)}) %collective-permute-start.8) | collective-permute-done | bytes 3145760 | tf_op jit(solution)/shard_map/ppermute | solution.py:332
  79.0 0.0 copy-done
  79.0 0.0 copy-done.1
  79.0 6.0 %front.1 = (bf16[256,2048]{1,0:T(8,128)(2,1)}, bf16[256,640]{1,0:T(8,128)(2,1)S(1)}) custom-call(s32[1]{0:T(128)S(6)} %copy.16.count_ref, bf16[768,16,128]{2,1,0:T(8,128)(2,1)S(1)} %constant_dynamic-update-slice_fusion.mine_ref, bf16[768,16,128]{2,1,0:T(8,128)(2,1)S(1)} %collective-permute-done.8.other_ref, bf16[256,2048]{1,0:T(8,128)(2,1)S(1)} %copy-done, ...), custom_call_target="tpu_custom_call" | custom-call | tf_op jit(solution)/shard_map/front/pallas_call | solution.py:278
  85.1 0.1 reshape.14
  85.2 24.3 %all_to_all.11 = bf16[128,2,640]{2,1,0:T(2,128)(2,1)S(1)} all-to-all(bf16[128,2,640]{2,1,0:T(2,128)(2,1)S(1)} %reshape.14), channel_id=1, replica_groups=mesh['front'=4,'helper'=128] {'helper'}, dimensions={0} | all-to-all | bytes 655360 | tf_op jit(solution)/shard_map/all_to_all | solution.py:337
  109.5 0.1 reshape.15.got_ref
  109.6 0.9 assemble.1
  (5 shorter events, 0.1 us)
Async XLA Ops:
  27.0 20.1 %collective-permute-start.2 = (bf16[96,16,128]{2,1,0:T(8,128)(2,1)S(1)}, bf16[96,16,128]{2,1,0:T(8,128)(2,1)S(1)}, u32[]{:S(2)}, u32[]{:S(2)}) collective-permute-start(bf16[96,16,128]{2,1,0:T(8,128)(2,1)S(1)} %pack.1), channel_id=1, source_target_pairs={{4,0},{33,1},{6,2},{35,3},{8,4},{37,5},{10,6},{39,7},{12,8},{41,9}... | collective-permute-start | bytes 1179656 | tf_op jit(solution)/shard_map/ppermute | solution.py:319
  35.9 16.3 %collective-permute-start.3 = (bf16[96,16,128]{2,1,0:T(8,128)(2,1)S(1)}, bf16[96,16,128]{2,1,0:T(8,128)(2,1)S(1)}, u32[]{:S(2)}, u32[]{:S(2)}) collective-permute-start(bf16[96,16,128]{2,1,0:T(8,128)(2,1)S(1)} %pack.1), channel_id=1, source_target_pairs={{12,0},{97,1},{14,2},{99,3},{0,4},{101,5},{2,6},{103,7},{4,8},{105... | collective-permute-start | bytes 1179656 | tf_op jit(solution)/shard_map/ppermute | solution.py:319
  37.8 22.6 %collective-permute-start = (bf16[96,16,128]{2,1,0:T(8,128)(2,1)S(1)}, bf16[96,16,128]{2,1,0:T(8,128)(2,1)S(1)}, u32[]{:S(2)}, u32[]{:S(2)}) collective-permute-start(bf16[96,16,128]{2,1,0:T(8,128)(2,1)S(1)} %pack.1), channel_id=1, source_target_pairs={{2,0},{17,1},{4,2},{19,3},{6,4},{21,5},{8,6},{23,7},{10,8},{25,9},... | collective-permute-start | bytes 1179656 | tf_op jit(solution)/shard_map/ppermute | solution.py:319
  45.1 17.3 %collective-permute-start.1 = (bf16[96,16,128]{2,1,0:T(8,128)(2,1)S(1)}, bf16[96,16,128]{2,1,0:T(8,128)(2,1)S(1)}, u32[]{:S(2)}, u32[]{:S(2)}) collective-permute-start(bf16[96,16,128]{2,1,0:T(8,128)(2,1)S(1)} %pack.1), channel_id=1, source_target_pairs={{14,0},{113,1},{0,2},{115,3},{2,4},{117,5},{4,6},{119,7},{6,8},{12... | collective-permute-start | bytes 1179656 | tf_op jit(solution)/shard_map/ppermute | solution.py:319
  47.1 27.0 %copy-start.2 = (bf16[256,512]{1,0:T(8,128)(2,1)S(1)}, bf16[256,512]{1,0:T(8,128)(2,1)}, u32[]{:S(2)}) copy-start(bf16[256,512]{1,0:T(8,128)(2,1)} %block_ref.1) | copy-start | bytes 786436
  47.1 27.0 %copy-start.3 = (s32[256]{0:T(256)S(1)}, s32[256]{0:T(256)}, u32[]{:S(2)}) copy-start(s32[256]{0:T(256)} %param.11) | copy-start | bytes 3076
  47.1 31.9 %copy-start = (bf16[256,2048]{1,0:T(8,128)(2,1)S(1)}, bf16[256,2048]{1,0:T(8,128)(2,1)}, u32[]{:S(2)}) copy-start(bf16[256,2048]{1,0:T(8,128)(2,1)} %rows_ref.1) | copy-start | bytes 3145732
  47.1 31.9 %copy-start.1 = (bf16[16,128,128]{2,1,0:T(8,128)(2,1)S(1)}, bf16[16,128,128]{2,1,0:T(8,128)(2,1)}, u32[]{:S(2)}) copy-start(bf16[16,128,128]{2,1,0:T(8,128)(2,1)} %inv_ref.1) | copy-start | bytes 1572868
  47.1 24.2 %collective-permute-start.6 = (bf16[48,16,128]{2,1,0:T(8,128)(2,1)S(1)}, bf16[48,16,128]{2,1,0:T(8,128)(2,1)S(1)}, u32[]{:S(2)}, u32[]{:S(2)}) collective-permute-start(bf16[48,16,128]{2,1,0:T(8,128)(2,1)S(1)} %slice.12), channel_id=1, source_target_pairs={{4,0},{33,1},{6,2},{35,3},{8,4},{37,5},{10,6},{39,7},{12,8},{41,9}... | collective-permute-start | bytes 589832 | tf_op jit(solution)/shard_map/ppermute | solution.py:319
  52.3 19.2 %collective-permute-start.7 = (bf16[48,16,128]{2,1,0:T(8,128)(2,1)S(1)}, bf16[48,16,128]{2,1,0:T(8,128)(2,1)S(1)}, u32[]{:S(2)}, u32[]{:S(2)}) collective-permute-start(bf16[48,16,128]{2,1,0:T(8,128)(2,1)S(1)} %slice.13), channel_id=1, source_target_pairs={{12,0},{97,1},{14,2},{99,3},{0,4},{101,5},{2,6},{103,7},{4,8},{105... | collective-permute-start | bytes 589832 | tf_op jit(solution)/shard_map/ppermute | solution.py:319
  54.2 11.5 %collective-permute-start.4 = (bf16[96,16,128]{2,1,0:T(8,128)(2,1)S(1)}, bf16[96,16,128]{2,1,0:T(8,128)(2,1)S(1)}, u32[]{:S(2)}, u32[]{:S(2)}) collective-permute-start(bf16[96,16,128]{2,1,0:T(8,128)(2,1)S(1)} %collective-permute-done.2), channel_id=1, source_target_pairs={{2,0},{17,1},{4,2},{19,3},{6,4},{21,5},{8,6},{23,7},{10,8},{25,9},... | collective-permute-start | bytes 1179656 | tf_op jit(solution)/shard_map/ppermute | solution.py:319
  60.4 10.9 %collective-permute-start.5 = (bf16[96,16,128]{2,1,0:T(8,128)(2,1)S(1)}, bf16[96,16,128]{2,1,0:T(8,128)(2,1)S(1)}, u32[]{:S(2)}, u32[]{:S(2)}) collective-permute-start(bf16[96,16,128]{2,1,0:T(8,128)(2,1)S(1)} %collective-permute-done.3), channel_id=1, source_target_pairs={{14,0},{113,1},{0,2},{115,3},{2,4},{117,5},{4,6},{119,7},{6,8},{12... | collective-permute-start | bytes 1179656 | tf_op jit(solution)/shard_map/ppermute | solution.py:319
  71.5 7.6 %collective-permute-start.8 = (bf16[768,16,128]{2,1,0:T(8,128)(2,1)S(1)}, bf16[768,16,128]{2,1,0:T(8,128)(2,1)S(1)}, u32[]{:S(2)}, u32[]{:S(2)}) collective-permute-start(bf16[768,16,128]{2,1,0:T(8,128)(2,1)S(1)} %constant_dynamic-update-slice_fusion.mine_ref), channel_id=1, source_target_pairs={{0,1},{1,0},{2,3},{3,2},{4,5},{5,4},{6,7},{7,6},{8,9},{9,8},{10,11... | collective-permute-start | bytes 9437192 | tf_op jit(solution)/shard_map/ppermute | solution.py:332

commit v6 on v5

--- a/solution.py
+++ b/solution.py
@@ -266,7 +266,7 @@
         scale(jnp.concatenate(s1s, axis=0), k1)
 
     product = dot(solved[SLAB:, :], wfac[...], NT)
-    held_contribution = (block_ref[...] - product).astype(BF16)
+    held_contribution = jnp.where(live, block_ref[...] - product, 0.0).astype(BF16)
     contribution = dot(held_contribution, order_ref[...], NT).astype(BF16)
 
     payload = jnp.concatenate([contribution, local_ref[...]], axis=1)

time: 111 us -> 111 us (level)
  no operation moved by 1% of the time
where the time goes in v6:
time: 111 us
  blocking collectives  48.7 us (44%)
  starting transfers between devices  37 us (33%)
  waiting for transfers between devices  13.3 us (12%)
  Pallas kernels  7.58 us (7%)
  between operations  1.56 us (1%)
  local copies, waits for them, and re-layouts  1.55 us (1%)
    ppermute x8, starting transfers between devices, receive(): return lax.ppermute(block, 'helper', from_offset(step))  35.1 us
    all_to_all x1, blocking collectives, per_device(): lax.all_to_all(spread_call(jnp.concatenate([lower_panel, lower_rows[:16]]...  24.4 us
    all_to_all x1, blocking collectives, per_device(): lax.all_to_all(send.reshape(HELPERS, CAP, WIDE), 'helper', split_axis=0,...  24.3 us
    ppermute x8, waiting for transfers between devices, receive(): return lax.ppermute(block, 'helper', from_offset(step))  8.66 us
    pallas_call x1, Pallas kernels, front_call(): pl.pallas_call(front_kernel, out_shape=(jax.ShapeDtypeStruct((ROWS, NPIV)...  6.05 us
    ppermute x1, waiting for transfers between devices, per_device(): other = lax.ppermute(mine, 'helper', [(h, h ^ 1) for h in range(HELPERS)])  4.62 us
  transfers between devices with their start and end apart: 9, of which 3 were waited for; matrix products, arithmetic and copies ran while one was open for 0% of the time, Pallas kernels for 0%

profile of v6, /device:TPU:6, one launch (start us, length us, event | category | flops | bytes accessed | tf_op | source)
XLA Modules:
  0.0 110.6 jit_solution(7290833290996457699)
XLA Ops:
  0.6 0.8 slice.9
  1.5 0.8 pad_maximum_fusion.held_ref
  2.3 0.1 spread.1
  2.4 24.4 %all_to_all.10.line_ref = bf16[8,19,16,128]{3,2,1,0:T(8,128)(2,1)S(1)} all-to-all(bf16[8,19,16,128]{3,2,1,0:T(8,128)(2,1)S(1)} %spread.1), channel_id=1, replica_groups={{0,16,32,48,64,80,96,112},{2,18,34,50,66,82,98,114},{4,20,36,52,68,84,1..., dimensions={0} | all-to-all | bytes 1245184 | tf_op jit(solution)/shard_map/all_to_all | solution.py:321
  26.8 0.2 pack.1
  27.0 8.9 %collective-permute-start.2 = (bf16[96,16,128]{2,1,0:T(8,128)(2,1)S(1)}, bf16[96,16,128]{2,1,0:T(8,128)(2,1)S(1)}, u32[]{:S(2)}, u32[]{:S(2)}) collective-permute-start(bf16[96,16,128]{2,1,0:T(8,128)(2,1)S(1)} %pack.1), channel_id=1, source_target_pairs={{4,0},{33,1},{6,2},{35,3},{8,4},{37,5},{10,6},{39,7},{12,8},{41,9}... | collective-permute-start | bytes 1179656 | tf_op jit(solution)/shard_map/ppermute | solution.py:319
  35.9 1.9 %collective-permute-start.3 = (bf16[96,16,128]{2,1,0:T(8,128)(2,1)S(1)}, bf16[96,16,128]{2,1,0:T(8,128)(2,1)S(1)}, u32[]{:S(2)}, u32[]{:S(2)}) collective-permute-start(bf16[96,16,128]{2,1,0:T(8,128)(2,1)S(1)} %pack.1), channel_id=1, source_target_pairs={{12,0},{97,1},{14,2},{99,3},{0,4},{101,5},{2,6},{103,7},{4,8},{105... | collective-permute-start | bytes 1179656 | tf_op jit(solution)/shard_map/ppermute | solution.py:319
  37.8 7.3 %collective-permute-start = (bf16[96,16,128]{2,1,0:T(8,128)(2,1)S(1)}, bf16[96,16,128]{2,1,0:T(8,128)(2,1)S(1)}, u32[]{:S(2)}, u32[]{:S(2)}) collective-permute-start(bf16[96,16,128]{2,1,0:T(8,128)(2,1)S(1)} %pack.1), channel_id=1, source_target_pairs={{2,0},{17,1},{4,2},{19,3},{6,4},{21,5},{8,6},{23,7},{10,8},{25,9},... | collective-permute-start | bytes 1179656 | tf_op jit(solution)/shard_map/ppermute | solution.py:319
  45.1 1.9 %collective-permute-start.1 = (bf16[96,16,128]{2,1,0:T(8,128)(2,1)S(1)}, bf16[96,16,128]{2,1,0:T(8,128)(2,1)S(1)}, u32[]{:S(2)}, u32[]{:S(2)}) collective-permute-start(bf16[96,16,128]{2,1,0:T(8,128)(2,1)S(1)} %pack.1), channel_id=1, source_target_pairs={{14,0},{113,1},{0,2},{115,3},{2,4},{117,5},{4,6},{119,7},{6,8},{12... | collective-permute-start | bytes 1179656 | tf_op jit(solution)/shard_map/ppermute | solution.py:319
  47.1 0.0 copy-start.2
  47.1 0.0 copy-start.3
  47.1 0.0 collective-permute-done.2
  47.1 0.0 copy-start
  47.1 0.0 copy-start.1
  47.1 5.1 %collective-permute-start.6 = (bf16[48,16,128]{2,1,0:T(8,128)(2,1)S(1)}, bf16[48,16,128]{2,1,0:T(8,128)(2,1)S(1)}, u32[]{:S(2)}, u32[]{:S(2)}) collective-permute-start(bf16[48,16,128]{2,1,0:T(8,128)(2,1)S(1)} %slice.12), channel_id=1, source_target_pairs={{4,0},{33,1},{6,2},{35,3},{8,4},{37,5},{10,6},{39,7},{12,8},{41,9}... | collective-permute-start | bytes 589832 | tf_op jit(solution)/shard_map/ppermute | solution.py:319
  52.2 0.0 collective-permute-done.3
  52.3 1.9 %collective-permute-start.7 = (bf16[48,16,128]{2,1,0:T(8,128)(2,1)S(1)}, bf16[48,16,128]{2,1,0:T(8,128)(2,1)S(1)}, u32[]{:S(2)}, u32[]{:S(2)}) collective-permute-start(bf16[48,16,128]{2,1,0:T(8,128)(2,1)S(1)} %slice.13), channel_id=1, source_target_pairs={{12,0},{97,1},{14,2},{99,3},{0,4},{101,5},{2,6},{103,7},{4,8},{105... | collective-permute-start | bytes 589832 | tf_op jit(solution)/shard_map/ppermute | solution.py:319
  54.2 6.2 %collective-permute-start.4 = (bf16[96,16,128]{2,1,0:T(8,128)(2,1)S(1)}, bf16[96,16,128]{2,1,0:T(8,128)(2,1)S(1)}, u32[]{:S(2)}, u32[]{:S(2)}) collective-permute-start(bf16[96,16,128]{2,1,0:T(8,128)(2,1)S(1)} %collective-permute-done.2), channel_id=1, source_target_pairs={{2,0},{17,1},{4,2},{19,3},{6,4},{21,5},{8,6},{23,7},{10,8},{25,9},... | collective-permute-start | bytes 1179656 | tf_op jit(solution)/shard_map/ppermute | solution.py:319
  60.4 0.0 collective-permute-done
  60.4 1.9 %collective-permute-start.5 = (bf16[96,16,128]{2,1,0:T(8,128)(2,1)S(1)}, bf16[96,16,128]{2,1,0:T(8,128)(2,1)S(1)}, u32[]{:S(2)}, u32[]{:S(2)}) collective-permute-start(bf16[96,16,128]{2,1,0:T(8,128)(2,1)S(1)} %collective-permute-done.3), channel_id=1, source_target_pairs={{14,0},{113,1},{0,2},{115,3},{2,4},{117,5},{4,6},{119,7},{6,8},{12... | collective-permute-start | bytes 1179656 | tf_op jit(solution)/shard_map/ppermute | solution.py:319
  62.4 0.1 constant_dynamic-update-slice_fusion.7
  62.4 0.0 collective-permute-done.1
  62.4 0.1 constant_dynamic-update-slice_fusion.6
  62.5 0.1 constant_dynamic-update-slice_fusion.5
  62.6 0.1 constant_dynamic-update-slice_fusion.4
  62.6 3.1 %collective-permute-done.4 = bf16[96,16,128]{2,1,0:T(8,128)(2,1)S(1)} collective-permute-done((bf16[96,16,128]{2,1,0:T(8,128)(2,1)S(1)}, bf16[96,16,128]{2,1,0:T(8,128)(2,1)S(1)}, u32[]{:S(2)}, u32[]{:S(2)}) %collective-permute-start.4) | collective-permute-done | bytes 393248 | tf_op jit(solution)/shard_map/ppermute | solution.py:319
  65.7 0.1 constant_dynamic-update-slice_fusion.3
  65.7 5.6 %collective-permute-done.5 = bf16[96,16,128]{2,1,0:T(8,128)(2,1)S(1)} collective-permute-done((bf16[96,16,128]{2,1,0:T(8,128)(2,1)S(1)}, bf16[96,16,128]{2,1,0:T(8,128)(2,1)S(1)}, u32[]{:S(2)}, u32[]{:S(2)}) %collective-permute-start.5) | collective-permute-done | bytes 393248 | tf_op jit(solution)/shard_map/ppermute | solution.py:319
  71.3 0.1 constant_dynamic-update-slice_fusion.2
  71.4 0.0 collective-permute-done.6
  71.4 0.0 collective-permute-done.7
  71.5 1.9 %collective-permute-start.8 = (bf16[768,16,128]{2,1,0:T(8,128)(2,1)S(1)}, bf16[768,16,128]{2,1,0:T(8,128)(2,1)S(1)}, u32[]{:S(2)}, u32[]{:S(2)}) collective-permute-start(bf16[768,16,128]{2,1,0:T(8,128)(2,1)S(1)} %constant_dynamic-update-slice_fusion.mine_ref), channel_id=1, source_target_pairs={{0,1},{1,0},{2,3},{3,2},{4,5},{5,4},{6,7},{7,6},{8,9},{9,8},{10,11... | collective-permute-start | bytes 9437192 | tf_op jit(solution)/shard_map/ppermute | solution.py:332
  74.0 0.0 copy-done.2
  74.0 0.0 copy-done.3
  74.1 0.3 prepare.1
  74.4 4.6 %collective-permute-done.8.other_ref = bf16[768,16,128]{2,1,0:T(8,128)(2,1)S(1)} collective-permute-done((bf16[768,16,128]{2,1,0:T(8,128)(2,1)S(1)}, bf16[768,16,128]{2,1,0:T(8,128)(2,1)S(1)}, u32[]{:S(2)}, u32[]{:S(2)}) %collective-permute-start.8) | collective-permute-done | bytes 3145760 | tf_op jit(solution)/shard_map/ppermute | solution.py:332
  79.0 0.0 copy-done
  79.0 0.0 copy-done.1
  79.0 6.0 %front.1 = (bf16[256,2048]{1,0:T(8,128)(2,1)}, bf16[256,640]{1,0:T(8,128)(2,1)S(1)}) custom-call(s32[1]{0:T(128)S(6)} %copy.16.count_ref, bf16[768,16,128]{2,1,0:T(8,128)(2,1)S(1)} %constant_dynamic-update-slice_fusion.mine_ref, bf16[768,16,128]{2,1,0:T(8,128)(2,1)S(1)} %collective-permute-done.8.other_ref, bf16[256,2048]{1,0:T(8,128)(2,1)S(1)} %copy-done, ...), custom_call_target="tpu_custom_call" | custom-call | tf_op jit(solution)/shard_map/front/pallas_call | solution.py:278
  85.1 0.1 reshape.14
  85.2 24.3 %all_to_all.11 = bf16[128,2,640]{2,1,0:T(2,128)(2,1)S(1)} all-to-all(bf16[128,2,640]{2,1,0:T(2,128)(2,1)S(1)} %reshape.14), channel_id=1, replica_groups=mesh['front'=4,'helper'=128] {'helper'}, dimensions={0} | all-to-all | bytes 655360 | tf_op jit(solution)/shard_map/all_to_all | solution.py:337
  109.5 0.1 reshape.15.got_ref
  109.6 0.9 assemble.1
  (5 shorter events, 0.1 us)
Async XLA Ops:
  27.0 20.1 %collective-permute-start.2 = (bf16[96,16,128]{2,1,0:T(8,128)(2,1)S(1)}, bf16[96,16,128]{2,1,0:T(8,128)(2,1)S(1)}, u32[]{:S(2)}, u32[]{:S(2)}) collective-permute-start(bf16[96,16,128]{2,1,0:T(8,128)(2,1)S(1)} %pack.1), channel_id=1, source_target_pairs={{4,0},{33,1},{6,2},{35,3},{8,4},{37,5},{10,6},{39,7},{12,8},{41,9}... | collective-permute-start | bytes 1179656 | tf_op jit(solution)/shard_map/ppermute | solution.py:319
  35.9 16.3 %collective-permute-start.3 = (bf16[96,16,128]{2,1,0:T(8,128)(2,1)S(1)}, bf16[96,16,128]{2,1,0:T(8,128)(2,1)S(1)}, u32[]{:S(2)}, u32[]{:S(2)}) collective-permute-start(bf16[96,16,128]{2,1,0:T(8,128)(2,1)S(1)} %pack.1), channel_id=1, source_target_pairs={{12,0},{97,1},{14,2},{99,3},{0,4},{101,5},{2,6},{103,7},{4,8},{105... | collective-permute-start | bytes 1179656 | tf_op jit(solution)/shard_map/ppermute | solution.py:319
  37.8 22.6 %collective-permute-start = (bf16[96,16,128]{2,1,0:T(8,128)(2,1)S(1)}, bf16[96,16,128]{2,1,0:T(8,128)(2,1)S(1)}, u32[]{:S(2)}, u32[]{:S(2)}) collective-permute-start(bf16[96,16,128]{2,1,0:T(8,128)(2,1)S(1)} %pack.1), channel_id=1, source_target_pairs={{2,0},{17,1},{4,2},{19,3},{6,4},{21,5},{8,6},{23,7},{10,8},{25,9},... | collective-permute-start | bytes 1179656 | tf_op jit(solution)/shard_map/ppermute | solution.py:319
  45.1 17.3 %collective-permute-start.1 = (bf16[96,16,128]{2,1,0:T(8,128)(2,1)S(1)}, bf16[96,16,128]{2,1,0:T(8,128)(2,1)S(1)}, u32[]{:S(2)}, u32[]{:S(2)}) collective-permute-start(bf16[96,16,128]{2,1,0:T(8,128)(2,1)S(1)} %pack.1), channel_id=1, source_target_pairs={{14,0},{113,1},{0,2},{115,3},{2,4},{117,5},{4,6},{119,7},{6,8},{12... | collective-permute-start | bytes 1179656 | tf_op jit(solution)/shard_map/ppermute | solution.py:319
  47.1 27.0 %copy-start.2 = (bf16[256,512]{1,0:T(8,128)(2,1)S(1)}, bf16[256,512]{1,0:T(8,128)(2,1)}, u32[]{:S(2)}) copy-start(bf16[256,512]{1,0:T(8,128)(2,1)} %block_ref.1) | copy-start | bytes 786436
  47.1 27.0 %copy-start.3 = (s32[256]{0:T(256)S(1)}, s32[256]{0:T(256)}, u32[]{:S(2)}) copy-start(s32[256]{0:T(256)} %param.11) | copy-start | bytes 3076
  47.1 31.9 %copy-start = (bf16[256,2048]{1,0:T(8,128)(2,1)S(1)}, bf16[256,2048]{1,0:T(8,128)(2,1)}, u32[]{:S(2)}) copy-start(bf16[256,2048]{1,0:T(8,128)(2,1)} %rows_ref.1) | copy-start | bytes 3145732
  47.1 31.9 %copy-start.1 = (bf16[16,128,128]{2,1,0:T(8,128)(2,1)S(1)}, bf16[16,128,128]{2,1,0:T(8,128)(2,1)}, u32[]{:S(2)}) copy-start(bf16[16,128,128]{2,1,0:T(8,128)(2,1)} %inv_ref.1) | copy-start | bytes 1572868
  47.1 24.2 %collective-permute-start.6 = (bf16[48,16,128]{2,1,0:T(8,128)(2,1)S(1)}, bf16[48,16,128]{2,1,0:T(8,128)(2,1)S(1)}, u32[]{:S(2)}, u32[]{:S(2)}) collective-permute-start(bf16[48,16,128]{2,1,0:T(8,128)(2,1)S(1)} %slice.12), channel_id=1, source_target_pairs={{4,0},{33,1},{6,2},{35,3},{8,4},{37,5},{10,6},{39,7},{12,8},{41,9}... | collective-permute-start | bytes 589832 | tf_op jit(solution)/shard_map/ppermute | solution.py:319
  52.3 19.2 %collective-permute-start.7 = (bf16[48,16,128]{2,1,0:T(8,128)(2,1)S(1)}, bf16[48,16,128]{2,1,0:T(8,128)(2,1)S(1)}, u32[]{:S(2)}, u32[]{:S(2)}) collective-permute-start(bf16[48,16,128]{2,1,0:T(8,128)(2,1)S(1)} %slice.13), channel_id=1, source_target_pairs={{12,0},{97,1},{14,2},{99,3},{0,4},{101,5},{2,6},{103,7},{4,8},{105... | collective-permute-start | bytes 589832 | tf_op jit(solution)/shard_map/ppermute | solution.py:319
  54.2 11.5 %collective-permute-start.4 = (bf16[96,16,128]{2,1,0:T(8,128)(2,1)S(1)}, bf16[96,16,128]{2,1,0:T(8,128)(2,1)S(1)}, u32[]{:S(2)}, u32[]{:S(2)}) collective-permute-start(bf16[96,16,128]{2,1,0:T(8,128)(2,1)S(1)} %collective-permute-done.2), channel_id=1, source_target_pairs={{2,0},{17,1},{4,2},{19,3},{6,4},{21,5},{8,6},{23,7},{10,8},{25,9},... | collective-permute-start | bytes 1179656 | tf_op jit(solution)/shard_map/ppermute | solution.py:319
  60.4 10.9 %collective-permute-start.5 = (bf16[96,16,128]{2,1,0:T(8,128)(2,1)S(1)}, bf16[96,16,128]{2,1,0:T(8,128)(2,1)S(1)}, u32[]{:S(2)}, u32[]{:S(2)}) collective-permute-start(bf16[96,16,128]{2,1,0:T(8,128)(2,1)S(1)} %collective-permute-done.3), channel_id=1, source_target_pairs={{14,0},{113,1},{0,2},{115,3},{2,4},{117,5},{4,6},{119,7},{6,8},{12... | collective-permute-start | bytes 1179656 | tf_op jit(solution)/shard_map/ppermute | solution.py:319
  71.5 7.6 %collective-permute-start.8 = (bf16[768,16,128]{2,1,0:T(8,128)(2,1)S(1)}, bf16[768,16,128]{2,1,0:T(8,128)(2,1)S(1)}, u32[]{:S(2)}, u32[]{:S(2)}) collective-permute-start(bf16[768,16,128]{2,1,0:T(8,128)(2,1)S(1)} %constant_dynamic-update-slice_fusion.mine_ref), channel_id=1, source_target_pairs={{0,1},{1,0},{2,3},{3,2},{4,5},{5,4},{6,7},{7,6},{8,9},{9,8},{10,11... | collective-permute-start | bytes 9437192 | tf_op jit(solution)/shard_map/ppermute | solution.py:332

commit v7 on v6

--- a/solution.py
+++ b/solution.py
@@ -59,27 +59,27 @@
     return lax.dot_general(a, b, dims, preferred_element_type=F32)
 
 
-def spread_kernel(held_ref, out_ref, window):
+def spread_kernel(panel_ref, rows_ref, out_ref, window):
     for j in range(NB):
-        window[SR * j : SR * (j + 1), :] = held_ref[16:, BS * j : BS * (j + 1)].astype(F32)[:SR]
+        window[SR * j : SR * (j + 1), :] = rows_ref[:, BS * j : BS * (j + 1)].astype(F32)[:SR]
     leading = window[...].astype(BF16).reshape(SR, 16, BS)
     for d in range(LINE):
         for j in range(NB - 1):
-            out_ref[d, j] = held_ref[:16, BS * j : BS * (j + 1)]
+            out_ref[d, j] = panel_ref[:, BS * j : BS * (j + 1)]
         out_ref[d, NB - 1 :] = leading
 
 
-def spread_call(held):
+def spread_call(panel, rows):
     vmem = pl.BlockSpec(memory_space=pltpu.VMEM)
     return pl.pallas_call(
         spread_kernel,
         out_shape=jax.ShapeDtypeStruct((LINE, SENT, 16, BS), BF16),
-        in_specs=[vmem],
+        in_specs=[vmem, vmem],
         out_specs=vmem,
         scratch_shapes=[pltpu.VMEM((SR * NB, BS), F32)],
-        compiler_params=pltpu.CompilerParams(vmem_limit_bytes=8 * 1024 * 1024),
+        compiler_params=pltpu.CompilerParams(allow_input_fusion=[False, True], vmem_limit_bytes=8 * 1024 * 1024),
         name="spread",
-    )(held)
+    )(panel, rows)
 
 
 def pack_kernel(line_ref, out_ref, window):
@@ -319,7 +319,7 @@
         return lax.ppermute(block, "helper", from_offset(step))
 
     line = lax.all_to_all(
-        spread_call(jnp.concatenate([lower_panel, lower_rows[:16]])), "helper", 0, 0, tiled=True, axis_index_groups=line_groups()
+        spread_call(lower_panel, lower_rows[:16]), "helper", 0, 0, tiled=True, axis_index_groups=line_groups()
     )
     own = pack_call(line)
     half = PIECES // 2

time: 111 us -> 111 us (level)
  no operation moved by 1% of the time
where the time goes in v7:
time: 111 us
  blocking collectives  48.7 us (44%)
  starting transfers between devices  37 us (33%)
  waiting for transfers between devices  13.3 us (12%)
  Pallas kernels  7.58 us (7%)
  local copies, waits for them, and re-layouts  2.39 us (2%)
  between operations  1.55 us (1%)
    ppermute x8, starting transfers between devices, receive(): return lax.ppermute(block, 'helper', from_offset(step))  35.1 us
    all_to_all x1, blocking collectives, per_device(): lax.all_to_all(spread_call(lower_panel, lower_rows[:16]), 'helper', 0, 0,...  24.4 us
    all_to_all x1, blocking collectives, per_device(): lax.all_to_all(send.reshape(HELPERS, CAP, WIDE), 'helper', split_axis=0,...  24.3 us
    ppermute x8, waiting for transfers between devices, receive(): return lax.ppermute(block, 'helper', from_offset(step))  8.66 us
    pallas_call x1, Pallas kernels, front_call(): pl.pallas_call(front_kernel, out_shape=(jax.ShapeDtypeStruct((ROWS, NPIV)...  6.05 us
    ppermute x1, waiting for transfers between devices, per_device(): other = lax.ppermute(mine, 'helper', [(h, h ^ 1) for h in range(HELPERS)])  4.62 us
  transfers between devices with their start and end apart: 9, of which 3 were waited for; matrix products, arithmetic and copies ran while one was open for 0% of the time, Pallas kernels for 0%

profile of v7, /device:TPU:6, one launch (start us, length us, event | category | flops | bytes accessed | tf_op | source)
XLA Modules:
  0.0 110.5 jit_solution(9008104526280133414)
XLA Ops:
  0.6 0.8 slice.9.rows_ref
  1.5 0.0 copy-start.2
  1.5 0.8 copy-done.2
  2.3 0.1 spread.1
  2.4 24.4 %all_to_all.10.line_ref = bf16[8,19,16,128]{3,2,1,0:T(8,128)(2,1)S(1)} all-to-all(bf16[8,19,16,128]{3,2,1,0:T(8,128)(2,1)S(1)} %spread.1), channel_id=1, replica_groups={{0,16,32,48,64,80,96,112},{2,18,34,50,66,82,98,114},{4,20,36,52,68,84,1..., dimensions={0} | all-to-all | bytes 1245184 | tf_op jit(solution)/shard_map/all_to_all | solution.py:321
  26.8 0.2 pack.1
  27.0 8.9 %collective-permute-start.2 = (bf16[96,16,128]{2,1,0:T(8,128)(2,1)S(1)}, bf16[96,16,128]{2,1,0:T(8,128)(2,1)S(1)}, u32[]{:S(2)}, u32[]{:S(2)}) collective-permute-start(bf16[96,16,128]{2,1,0:T(8,128)(2,1)S(1)} %pack.1), channel_id=1, source_target_pairs={{4,0},{33,1},{6,2},{35,3},{8,4},{37,5},{10,6},{39,7},{12,8},{41,9}... | collective-permute-start | bytes 1179656 | tf_op jit(solution)/shard_map/ppermute | solution.py:319
  35.9 1.9 %collective-permute-start.3 = (bf16[96,16,128]{2,1,0:T(8,128)(2,1)S(1)}, bf16[96,16,128]{2,1,0:T(8,128)(2,1)S(1)}, u32[]{:S(2)}, u32[]{:S(2)}) collective-permute-start(bf16[96,16,128]{2,1,0:T(8,128)(2,1)S(1)} %pack.1), channel_id=1, source_target_pairs={{12,0},{97,1},{14,2},{99,3},{0,4},{101,5},{2,6},{103,7},{4,8},{105... | collective-permute-start | bytes 1179656 | tf_op jit(solution)/shard_map/ppermute | solution.py:319
  37.8 7.3 %collective-permute-start = (bf16[96,16,128]{2,1,0:T(8,128)(2,1)S(1)}, bf16[96,16,128]{2,1,0:T(8,128)(2,1)S(1)}, u32[]{:S(2)}, u32[]{:S(2)}) collective-permute-start(bf16[96,16,128]{2,1,0:T(8,128)(2,1)S(1)} %pack.1), channel_id=1, source_target_pairs={{2,0},{17,1},{4,2},{19,3},{6,4},{21,5},{8,6},{23,7},{10,8},{25,9},... | collective-permute-start | bytes 1179656 | tf_op jit(solution)/shard_map/ppermute | solution.py:319
  45.1 1.9 %collective-permute-start.1 = (bf16[96,16,128]{2,1,0:T(8,128)(2,1)S(1)}, bf16[96,16,128]{2,1,0:T(8,128)(2,1)S(1)}, u32[]{:S(2)}, u32[]{:S(2)}) collective-permute-start(bf16[96,16,128]{2,1,0:T(8,128)(2,1)S(1)} %pack.1), channel_id=1, source_target_pairs={{14,0},{113,1},{0,2},{115,3},{2,4},{117,5},{4,6},{119,7},{6,8},{12... | collective-permute-start | bytes 1179656 | tf_op jit(solution)/shard_map/ppermute | solution.py:319
  47.0 0.0 copy-start.3
  47.1 0.0 copy-start.4
  47.1 0.0 collective-permute-done.2
  47.1 0.0 copy-start
  47.1 0.0 copy-start.1
  47.1 5.1 %collective-permute-start.6 = (bf16[48,16,128]{2,1,0:T(8,128)(2,1)S(1)}, bf16[48,16,128]{2,1,0:T(8,128)(2,1)S(1)}, u32[]{:S(2)}, u32[]{:S(2)}) collective-permute-start(bf16[48,16,128]{2,1,0:T(8,128)(2,1)S(1)} %slice.12), channel_id=1, source_target_pairs={{4,0},{33,1},{6,2},{35,3},{8,4},{37,5},{10,6},{39,7},{12,8},{41,9}... | collective-permute-start | bytes 589832 | tf_op jit(solution)/shard_map/ppermute | solution.py:319
  52.2 0.0 collective-permute-done.3
  52.2 1.9 %collective-permute-start.7 = (bf16[48,16,128]{2,1,0:T(8,128)(2,1)S(1)}, bf16[48,16,128]{2,1,0:T(8,128)(2,1)S(1)}, u32[]{:S(2)}, u32[]{:S(2)}) collective-permute-start(bf16[48,16,128]{2,1,0:T(8,128)(2,1)S(1)} %slice.13), channel_id=1, source_target_pairs={{12,0},{97,1},{14,2},{99,3},{0,4},{101,5},{2,6},{103,7},{4,8},{105... | collective-permute-start | bytes 589832 | tf_op jit(solution)/shard_map/ppermute | solution.py:319
  54.2 6.2 %collective-permute-start.4 = (bf16[96,16,128]{2,1,0:T(8,128)(2,1)S(1)}, bf16[96,16,128]{2,1,0:T(8,128)(2,1)S(1)}, u32[]{:S(2)}, u32[]{:S(2)}) collective-permute-start(bf16[96,16,128]{2,1,0:T(8,128)(2,1)S(1)} %collective-permute-done.2), channel_id=1, source_target_pairs={{2,0},{17,1},{4,2},{19,3},{6,4},{21,5},{8,6},{23,7},{10,8},{25,9},... | collective-permute-start | bytes 1179656 | tf_op jit(solution)/shard_map/ppermute | solution.py:319
  60.4 0.0 collective-permute-done
  60.4 1.9 %collective-permute-start.5 = (bf16[96,16,128]{2,1,0:T(8,128)(2,1)S(1)}, bf16[96,16,128]{2,1,0:T(8,128)(2,1)S(1)}, u32[]{:S(2)}, u32[]{:S(2)}) collective-permute-start(bf16[96,16,128]{2,1,0:T(8,128)(2,1)S(1)} %collective-permute-done.3), channel_id=1, source_target_pairs={{14,0},{113,1},{0,2},{115,3},{2,4},{117,5},{4,6},{119,7},{6,8},{12... | collective-permute-start | bytes 1179656 | tf_op jit(solution)/shard_map/ppermute | solution.py:319
  62.3 0.1 constant_dynamic-update-slice_fusion.7
  62.4 0.0 collective-permute-done.1
  62.4 0.1 constant_dynamic-update-slice_fusion.6
  62.5 0.1 constant_dynamic-update-slice_fusion.5
  62.5 0.1 constant_dynamic-update-slice_fusion.4
  62.6 3.1 %collective-permute-done.4 = bf16[96,16,128]{2,1,0:T(8,128)(2,1)S(1)} collective-permute-done((bf16[96,16,128]{2,1,0:T(8,128)(2,1)S(1)}, bf16[96,16,128]{2,1,0:T(8,128)(2,1)S(1)}, u32[]{:S(2)}, u32[]{:S(2)}) %collective-permute-start.4) | collective-permute-done | bytes 393248 | tf_op jit(solution)/shard_map/ppermute | solution.py:319
  65.7 0.1 constant_dynamic-update-slice_fusion.3
  65.7 5.6 %collective-permute-done.5 = bf16[96,16,128]{2,1,0:T(8,128)(2,1)S(1)} collective-permute-done((bf16[96,16,128]{2,1,0:T(8,128)(2,1)S(1)}, bf16[96,16,128]{2,1,0:T(8,128)(2,1)S(1)}, u32[]{:S(2)}, u32[]{:S(2)}) %collective-permute-start.5) | collective-permute-done | bytes 393248 | tf_op jit(solution)/shard_map/ppermute | solution.py:319
  71.3 0.1 constant_dynamic-update-slice_fusion.2
  71.3 0.0 collective-permute-done.6
  71.4 0.0 collective-permute-done.7
  71.4 1.9 %collective-permute-start.8 = (bf16[768,16,128]{2,1,0:T(8,128)(2,1)S(1)}, bf16[768,16,128]{2,1,0:T(8,128)(2,1)S(1)}, u32[]{:S(2)}, u32[]{:S(2)}) collective-permute-start(bf16[768,16,128]{2,1,0:T(8,128)(2,1)S(1)} %constant_dynamic-update-slice_fusion.mine_ref), channel_id=1, source_target_pairs={{0,1},{1,0},{2,3},{3,2},{4,5},{5,4},{6,7},{7,6},{8,9},{9,8},{10,11... | collective-permute-start | bytes 9437192 | tf_op jit(solution)/shard_map/ppermute | solution.py:332
  74.0 0.0 copy-done.3
  74.0 0.0 copy-done.4
  74.0 0.3 prepare.1
  74.4 4.6 %collective-permute-done.8.other_ref = bf16[768,16,128]{2,1,0:T(8,128)(2,1)S(1)} collective-permute-done((bf16[768,16,128]{2,1,0:T(8,128)(2,1)S(1)}, bf16[768,16,128]{2,1,0:T(8,128)(2,1)S(1)}, u32[]{:S(2)}, u32[]{:S(2)}) %collective-permute-start.8) | collective-permute-done | bytes 3145760 | tf_op jit(solution)/shard_map/ppermute | solution.py:332
  79.0 0.0 copy-done
  79.0 0.0 copy-done.1
  79.0 6.0 %front.1 = (bf16[256,2048]{1,0:T(8,128)(2,1)}, bf16[256,640]{1,0:T(8,128)(2,1)S(1)}) custom-call(s32[1]{0:T(128)S(6)} %copy.16.count_ref, bf16[768,16,128]{2,1,0:T(8,128)(2,1)S(1)} %constant_dynamic-update-slice_fusion.mine_ref, bf16[768,16,128]{2,1,0:T(8,128)(2,1)S(1)} %collective-permute-done.8.other_ref, bf16[256,2048]{1,0:T(8,128)(2,1)S(1)} %copy-done, ...), custom_call_target="tpu_custom_call" | custom-call | tf_op jit(solution)/shard_map/front/pallas_call | solution.py:278
  85.1 0.1 reshape.14
  85.2 24.3 %all_to_all.11 = bf16[128,2,640]{2,1,0:T(2,128)(2,1)S(1)} all-to-all(bf16[128,2,640]{2,1,0:T(2,128)(2,1)S(1)} %reshape.14), channel_id=1, replica_groups=mesh['front'=4,'helper'=128] {'helper'}, dimensions={0} | all-to-all | bytes 655360 | tf_op jit(solution)/shard_map/all_to_all | solution.py:337
  109.5 0.1 reshape.15.got_ref
  109.6 0.9 assemble.1
  (5 shorter events, 0.1 us)
Async XLA Ops:
  1.5 0.8 copy-start.2
  27.0 20.1 %collective-permute-start.2 = (bf16[96,16,128]{2,1,0:T(8,128)(2,1)S(1)}, bf16[96,16,128]{2,1,0:T(8,128)(2,1)S(1)}, u32[]{:S(2)}, u32[]{:S(2)}) collective-permute-start(bf16[96,16,128]{2,1,0:T(8,128)(2,1)S(1)} %pack.1), channel_id=1, source_target_pairs={{4,0},{33,1},{6,2},{35,3},{8,4},{37,5},{10,6},{39,7},{12,8},{41,9}... | collective-permute-start | bytes 1179656 | tf_op jit(solution)/shard_map/ppermute | solution.py:319
  35.9 16.3 %collective-permute-start.3 = (bf16[96,16,128]{2,1,0:T(8,128)(2,1)S(1)}, bf16[96,16,128]{2,1,0:T(8,128)(2,1)S(1)}, u32[]{:S(2)}, u32[]{:S(2)}) collective-permute-start(bf16[96,16,128]{2,1,0:T(8,128)(2,1)S(1)} %pack.1), channel_id=1, source_target_pairs={{12,0},{97,1},{14,2},{99,3},{0,4},{101,5},{2,6},{103,7},{4,8},{105... | collective-permute-start | bytes 1179656 | tf_op jit(solution)/shard_map/ppermute | solution.py:319
  37.8 22.6 %collective-permute-start = (bf16[96,16,128]{2,1,0:T(8,128)(2,1)S(1)}, bf16[96,16,128]{2,1,0:T(8,128)(2,1)S(1)}, u32[]{:S(2)}, u32[]{:S(2)}) collective-permute-start(bf16[96,16,128]{2,1,0:T(8,128)(2,1)S(1)} %pack.1), channel_id=1, source_target_pairs={{2,0},{17,1},{4,2},{19,3},{6,4},{21,5},{8,6},{23,7},{10,8},{25,9},... | collective-permute-start | bytes 1179656 | tf_op jit(solution)/shard_map/ppermute | solution.py:319
  45.1 17.3 %collective-permute-start.1 = (bf16[96,16,128]{2,1,0:T(8,128)(2,1)S(1)}, bf16[96,16,128]{2,1,0:T(8,128)(2,1)S(1)}, u32[]{:S(2)}, u32[]{:S(2)}) collective-permute-start(bf16[96,16,128]{2,1,0:T(8,128)(2,1)S(1)} %pack.1), channel_id=1, source_target_pairs={{14,0},{113,1},{0,2},{115,3},{2,4},{117,5},{4,6},{119,7},{6,8},{12... | collective-permute-start | bytes 1179656 | tf_op jit(solution)/shard_map/ppermute | solution.py:319
  47.0 27.0 %copy-start.3 = (bf16[256,512]{1,0:T(8,128)(2,1)S(1)}, bf16[256,512]{1,0:T(8,128)(2,1)}, u32[]{:S(2)}) copy-start(bf16[256,512]{1,0:T(8,128)(2,1)} %block_ref.1) | copy-start | bytes 786436
  47.1 27.0 %copy-start.4 = (s32[256]{0:T(256)S(1)}, s32[256]{0:T(256)}, u32[]{:S(2)}) copy-start(s32[256]{0:T(256)} %param.11) | copy-start | bytes 3076
  47.1 31.9 %copy-start = (bf16[256,2048]{1,0:T(8,128)(2,1)S(1)}, bf16[256,2048]{1,0:T(8,128)(2,1)}, u32[]{:S(2)}) copy-start(bf16[256,2048]{1,0:T(8,128)(2,1)} %rows_ref.1) | copy-start | bytes 3145732
  47.1 31.9 %copy-start.1 = (bf16[16,128,128]{2,1,0:T(8,128)(2,1)S(1)}, bf16[16,128,128]{2,1,0:T(8,128)(2,1)}, u32[]{:S(2)}) copy-start(bf16[16,128,128]{2,1,0:T(8,128)(2,1)} %inv_ref.1) | copy-start | bytes 1572868
  47.1 24.2 %collective-permute-start.6 = (bf16[48,16,128]{2,1,0:T(8,128)(2,1)S(1)}, bf16[48,16,128]{2,1,0:T(8,128)(2,1)S(1)}, u32[]{:S(2)}, u32[]{:S(2)}) collective-permute-start(bf16[48,16,128]{2,1,0:T(8,128)(2,1)S(1)} %slice.12), channel_id=1, source_target_pairs={{4,0},{33,1},{6,2},{35,3},{8,4},{37,5},{10,6},{39,7},{12,8},{41,9}... | collective-permute-start | bytes 589832 | tf_op jit(solution)/shard_map/ppermute | solution.py:319
  52.2 19.2 %collective-permute-start.7 = (bf16[48,16,128]{2,1,0:T(8,128)(2,1)S(1)}, bf16[48,16,128]{2,1,0:T(8,128)(2,1)S(1)}, u32[]{:S(2)}, u32[]{:S(2)}) collective-permute-start(bf16[48,16,128]{2,1,0:T(8,128)(2,1)S(1)} %slice.13), channel_id=1, source_target_pairs={{12,0},{97,1},{14,2},{99,3},{0,4},{101,5},{2,6},{103,7},{4,8},{105... | collective-permute-start | bytes 589832 | tf_op jit(solution)/shard_map/ppermute | solution.py:319
  54.2 11.5 %collective-permute-start.4 = (bf16[96,16,128]{2,1,0:T(8,128)(2,1)S(1)}, bf16[96,16,128]{2,1,0:T(8,128)(2,1)S(1)}, u32[]{:S(2)}, u32[]{:S(2)}) collective-permute-start(bf16[96,16,128]{2,1,0:T(8,128)(2,1)S(1)} %collective-permute-done.2), channel_id=1, source_target_pairs={{2,0},{17,1},{4,2},{19,3},{6,4},{21,5},{8,6},{23,7},{10,8},{25,9},... | collective-permute-start | bytes 1179656 | tf_op jit(solution)/shard_map/ppermute | solution.py:319
  60.4 10.9 %collective-permute-start.5 = (bf16[96,16,128]{2,1,0:T(8,128)(2,1)S(1)}, bf16[96,16,128]{2,1,0:T(8,128)(2,1)S(1)}, u32[]{:S(2)}, u32[]{:S(2)}) collective-permute-start(bf16[96,16,128]{2,1,0:T(8,128)(2,1)S(1)} %collective-permute-done.3), channel_id=1, source_target_pairs={{14,0},{113,1},{0,2},{115,3},{2,4},{117,5},{4,6},{119,7},{6,8},{12... | collective-permute-start | bytes 1179656 | tf_op jit(solution)/shard_map/ppermute | solution.py:319
  71.4 7.6 %collective-permute-start.8 = (bf16[768,16,128]{2,1,0:T(8,128)(2,1)S(1)}, bf16[768,16,128]{2,1,0:T(8,128)(2,1)S(1)}, u32[]{:S(2)}, u32[]{:S(2)}) collective-permute-start(bf16[768,16,128]{2,1,0:T(8,128)(2,1)S(1)} %constant_dynamic-update-slice_fusion.mine_ref), channel_id=1, source_target_pairs={{0,1},{1,0},{2,3},{3,2},{4,5},{5,4},{6,7},{7,6},{8,9},{9,8},{10,11... | collective-permute-start | bytes 9437192 | tf_op jit(solution)/shard_map/ppermute | solution.py:332

commit v8 on v6

--- a/solution.py
+++ b/solution.py
@@ -228,7 +228,7 @@
     def pair(s):
         return jnp.concatenate([start_block(2 * s), start_block(2 * s + 1)], axis=1)
 
-    groups = ((0, 512), (512, 768))
+    groups = ((512, 768), (0, 512))
 
     def start_rows(k, g):
         r0, r1 = groups[g]
@@ -262,8 +262,8 @@
         lasts = [jnp.concatenate([s0s[g], s1s[g]], axis=1) for g in range(len(groups))]
         for g, (r0, r1) in enumerate(groups):
             solved[r0:r1, lo : lo + 256] = lasts[g]
-        scale(jnp.concatenate(s0s, axis=0), k0)
-        scale(jnp.concatenate(s1s, axis=0), k1)
+        scale(jnp.concatenate(s0s[::-1], axis=0), k0)
+        scale(jnp.concatenate(s1s[::-1], axis=0), k1)
 
     product = dot(solved[SLAB:, :], wfac[...], NT)
     held_contribution = jnp.where(live, block_ref[...] - product, 0.0).astype(BF16)

time: 111 us -> 111 us (level)
  no operation moved by 1% of the time
where the time goes in v8:
time: 111 us
  blocking collectives  48.7 us (44%)
  starting transfers between devices  37 us (33%)
  waiting for transfers between devices  13.3 us (12%)
  Pallas kernels  7.64 us (7%)
  between operations  1.56 us (1%)
  local copies, waits for them, and re-layouts  1.55 us (1%)
    ppermute x8, starting transfers between devices, receive(): return lax.ppermute(block, 'helper', from_offset(step))  35.1 us
    all_to_all x1, blocking collectives, per_device(): lax.all_to_all(spread_call(jnp.concatenate([lower_panel, lower_rows[:16]]...  24.4 us
    all_to_all x1, blocking collectives, per_device(): lax.all_to_all(send.reshape(HELPERS, CAP, WIDE), 'helper', split_axis=0,...  24.3 us
    ppermute x8, waiting for transfers between devices, receive(): return lax.ppermute(block, 'helper', from_offset(step))  8.66 us
    pallas_call x1, Pallas kernels, front_call(): pl.pallas_call(front_kernel, out_shape=(jax.ShapeDtypeStruct((ROWS, NPIV)...  6.12 us
    ppermute x1, waiting for transfers between devices, per_device(): other = lax.ppermute(mine, 'helper', [(h, h ^ 1) for h in range(HELPERS)])  4.62 us
  transfers between devices with their start and end apart: 9, of which 3 were waited for; matrix products, arithmetic and copies ran while one was open for 0% of the time, Pallas kernels for 0%

profile of v8, /device:TPU:6, one launch (start us, length us, event | category | flops | bytes accessed | tf_op | source)
XLA Modules:
  0.0 110.6 jit_solution(16207225533124944048)
XLA Ops:
  0.6 0.8 slice.9
  1.5 0.8 pad_maximum_fusion.held_ref
  2.3 0.1 spread.1
  2.4 24.4 %all_to_all.10.line_ref = bf16[8,19,16,128]{3,2,1,0:T(8,128)(2,1)S(1)} all-to-all(bf16[8,19,16,128]{3,2,1,0:T(8,128)(2,1)S(1)} %spread.1), channel_id=1, replica_groups={{0,16,32,48,64,80,96,112},{2,18,34,50,66,82,98,114},{4,20,36,52,68,84,1..., dimensions={0} | all-to-all | bytes 1245184 | tf_op jit(solution)/shard_map/all_to_all | solution.py:321
  26.8 0.2 pack.1
  27.0 8.9 %collective-permute-start.2 = (bf16[96,16,128]{2,1,0:T(8,128)(2,1)S(1)}, bf16[96,16,128]{2,1,0:T(8,128)(2,1)S(1)}, u32[]{:S(2)}, u32[]{:S(2)}) collective-permute-start(bf16[96,16,128]{2,1,0:T(8,128)(2,1)S(1)} %pack.1), channel_id=1, source_target_pairs={{4,0},{33,1},{6,2},{35,3},{8,4},{37,5},{10,6},{39,7},{12,8},{41,9}... | collective-permute-start | bytes 1179656 | tf_op jit(solution)/shard_map/ppermute | solution.py:319
  35.9 1.9 %collective-permute-start.3 = (bf16[96,16,128]{2,1,0:T(8,128)(2,1)S(1)}, bf16[96,16,128]{2,1,0:T(8,128)(2,1)S(1)}, u32[]{:S(2)}, u32[]{:S(2)}) collective-permute-start(bf16[96,16,128]{2,1,0:T(8,128)(2,1)S(1)} %pack.1), channel_id=1, source_target_pairs={{12,0},{97,1},{14,2},{99,3},{0,4},{101,5},{2,6},{103,7},{4,8},{105... | collective-permute-start | bytes 1179656 | tf_op jit(solution)/shard_map/ppermute | solution.py:319
  37.8 7.3 %collective-permute-start = (bf16[96,16,128]{2,1,0:T(8,128)(2,1)S(1)}, bf16[96,16,128]{2,1,0:T(8,128)(2,1)S(1)}, u32[]{:S(2)}, u32[]{:S(2)}) collective-permute-start(bf16[96,16,128]{2,1,0:T(8,128)(2,1)S(1)} %pack.1), channel_id=1, source_target_pairs={{2,0},{17,1},{4,2},{19,3},{6,4},{21,5},{8,6},{23,7},{10,8},{25,9},... | collective-permute-start | bytes 1179656 | tf_op jit(solution)/shard_map/ppermute | solution.py:319
  45.1 1.9 %collective-permute-start.1 = (bf16[96,16,128]{2,1,0:T(8,128)(2,1)S(1)}, bf16[96,16,128]{2,1,0:T(8,128)(2,1)S(1)}, u32[]{:S(2)}, u32[]{:S(2)}) collective-permute-start(bf16[96,16,128]{2,1,0:T(8,128)(2,1)S(1)} %pack.1), channel_id=1, source_target_pairs={{14,0},{113,1},{0,2},{115,3},{2,4},{117,5},{4,6},{119,7},{6,8},{12... | collective-permute-start | bytes 1179656 | tf_op jit(solution)/shard_map/ppermute | solution.py:319
  47.1 0.0 copy-start.2
  47.1 0.0 copy-start.3
  47.1 0.0 collective-permute-done.2
  47.1 0.0 copy-start
  47.1 0.0 copy-start.1
  47.1 5.1 %collective-permute-start.6 = (bf16[48,16,128]{2,1,0:T(8,128)(2,1)S(1)}, bf16[48,16,128]{2,1,0:T(8,128)(2,1)S(1)}, u32[]{:S(2)}, u32[]{:S(2)}) collective-permute-start(bf16[48,16,128]{2,1,0:T(8,128)(2,1)S(1)} %slice.12), channel_id=1, source_target_pairs={{4,0},{33,1},{6,2},{35,3},{8,4},{37,5},{10,6},{39,7},{12,8},{41,9}... | collective-permute-start | bytes 589832 | tf_op jit(solution)/shard_map/ppermute | solution.py:319
  52.2 0.0 collective-permute-done.3
  52.3 1.9 %collective-permute-start.7 = (bf16[48,16,128]{2,1,0:T(8,128)(2,1)S(1)}, bf16[48,16,128]{2,1,0:T(8,128)(2,1)S(1)}, u32[]{:S(2)}, u32[]{:S(2)}) collective-permute-start(bf16[48,16,128]{2,1,0:T(8,128)(2,1)S(1)} %slice.13), channel_id=1, source_target_pairs={{12,0},{97,1},{14,2},{99,3},{0,4},{101,5},{2,6},{103,7},{4,8},{105... | collective-permute-start | bytes 589832 | tf_op jit(solution)/shard_map/ppermute | solution.py:319
  54.2 6.2 %collective-permute-start.4 = (bf16[96,16,128]{2,1,0:T(8,128)(2,1)S(1)}, bf16[96,16,128]{2,1,0:T(8,128)(2,1)S(1)}, u32[]{:S(2)}, u32[]{:S(2)}) collective-permute-start(bf16[96,16,128]{2,1,0:T(8,128)(2,1)S(1)} %collective-permute-done.2), channel_id=1, source_target_pairs={{2,0},{17,1},{4,2},{19,3},{6,4},{21,5},{8,6},{23,7},{10,8},{25,9},... | collective-permute-start | bytes 1179656 | tf_op jit(solution)/shard_map/ppermute | solution.py:319
  60.4 0.0 collective-permute-done
  60.4 1.9 %collective-permute-start.5 = (bf16[96,16,128]{2,1,0:T(8,128)(2,1)S(1)}, bf16[96,16,128]{2,1,0:T(8,128)(2,1)S(1)}, u32[]{:S(2)}, u32[]{:S(2)}) collective-permute-start(bf16[96,16,128]{2,1,0:T(8,128)(2,1)S(1)} %collective-permute-done.3), channel_id=1, source_target_pairs={{14,0},{113,1},{0,2},{115,3},{2,4},{117,5},{4,6},{119,7},{6,8},{12... | collective-permute-start | bytes 1179656 | tf_op jit(solution)/shard_map/ppermute | solution.py:319
  62.4 0.1 constant_dynamic-update-slice_fusion.7
  62.4 0.0 collective-permute-done.1
  62.4 0.1 constant_dynamic-update-slice_fusion.6
  62.5 0.1 constant_dynamic-update-slice_fusion.5
  62.6 0.1 constant_dynamic-update-slice_fusion.4
  62.6 3.1 %collective-permute-done.4 = bf16[96,16,128]{2,1,0:T(8,128)(2,1)S(1)} collective-permute-done((bf16[96,16,128]{2,1,0:T(8,128)(2,1)S(1)}, bf16[96,16,128]{2,1,0:T(8,128)(2,1)S(1)}, u32[]{:S(2)}, u32[]{:S(2)}) %collective-permute-start.4) | collective-permute-done | bytes 393248 | tf_op jit(solution)/shard_map/ppermute | solution.py:319
  65.7 0.1 constant_dynamic-update-slice_fusion.3
  65.7 5.6 %collective-permute-done.5 = bf16[96,16,128]{2,1,0:T(8,128)(2,1)S(1)} collective-permute-done((bf16[96,16,128]{2,1,0:T(8,128)(2,1)S(1)}, bf16[96,16,128]{2,1,0:T(8,128)(2,1)S(1)}, u32[]{:S(2)}, u32[]{:S(2)}) %collective-permute-start.5) | collective-permute-done | bytes 393248 | tf_op jit(solution)/shard_map/ppermute | solution.py:319
  71.3 0.1 constant_dynamic-update-slice_fusion.2
  71.4 0.0 collective-permute-done.6
  71.4 0.0 collective-permute-done.7
  71.5 1.9 %collective-permute-start.8 = (bf16[768,16,128]{2,1,0:T(8,128)(2,1)S(1)}, bf16[768,16,128]{2,1,0:T(8,128)(2,1)S(1)}, u32[]{:S(2)}, u32[]{:S(2)}) collective-permute-start(bf16[768,16,128]{2,1,0:T(8,128)(2,1)S(1)} %constant_dynamic-update-slice_fusion.mine_ref), channel_id=1, source_target_pairs={{0,1},{1,0},{2,3},{3,2},{4,5},{5,4},{6,7},{7,6},{8,9},{9,8},{10,11... | collective-permute-start | bytes 9437192 | tf_op jit(solution)/shard_map/ppermute | solution.py:332
  74.0 0.0 copy-done.2
  74.0 0.0 copy-done.3
  74.1 0.3 prepare.1
  74.4 4.6 %collective-permute-done.8.other_ref = bf16[768,16,128]{2,1,0:T(8,128)(2,1)S(1)} collective-permute-done((bf16[768,16,128]{2,1,0:T(8,128)(2,1)S(1)}, bf16[768,16,128]{2,1,0:T(8,128)(2,1)S(1)}, u32[]{:S(2)}, u32[]{:S(2)}) %collective-permute-start.8) | collective-permute-done | bytes 3145760 | tf_op jit(solution)/shard_map/ppermute | solution.py:332
  79.0 0.0 copy-done
  79.0 0.0 copy-done.1
  79.0 6.1 %front.1 = (bf16[256,2048]{1,0:T(8,128)(2,1)}, bf16[256,640]{1,0:T(8,128)(2,1)S(1)}) custom-call(s32[1]{0:T(128)S(6)} %copy.16.count_ref, bf16[768,16,128]{2,1,0:T(8,128)(2,1)S(1)} %constant_dynamic-update-slice_fusion.mine_ref, bf16[768,16,128]{2,1,0:T(8,128)(2,1)S(1)} %collective-permute-done.8.other_ref, bf16[256,2048]{1,0:T(8,128)(2,1)S(1)} %copy-done, ...), custom_call_target="tpu_custom_call" | custom-call | tf_op jit(solution)/shard_map/front/pallas_call | solution.py:278
  85.1 0.1 reshape.14
  85.3 24.3 %all_to_all.11 = bf16[128,2,640]{2,1,0:T(2,128)(2,1)S(1)} all-to-all(bf16[128,2,640]{2,1,0:T(2,128)(2,1)S(1)} %reshape.14), channel_id=1, replica_groups=mesh['front'=4,'helper'=128] {'helper'}, dimensions={0} | all-to-all | bytes 655360 | tf_op jit(solution)/shard_map/all_to_all | solution.py:337
  109.6 0.1 reshape.15.got_ref
  109.7 0.9 assemble.1
  (5 shorter events, 0.1 us)
Async XLA Ops:
  27.0 20.1 %collective-permute-start.2 = (bf16[96,16,128]{2,1,0:T(8,128)(2,1)S(1)}, bf16[96,16,128]{2,1,0:T(8,128)(2,1)S(1)}, u32[]{:S(2)}, u32[]{:S(2)}) collective-permute-start(bf16[96,16,128]{2,1,0:T(8,128)(2,1)S(1)} %pack.1), channel_id=1, source_target_pairs={{4,0},{33,1},{6,2},{35,3},{8,4},{37,5},{10,6},{39,7},{12,8},{41,9}... | collective-permute-start | bytes 1179656 | tf_op jit(solution)/shard_map/ppermute | solution.py:319
  35.9 16.3 %collective-permute-start.3 = (bf16[96,16,128]{2,1,0:T(8,128)(2,1)S(1)}, bf16[96,16,128]{2,1,0:T(8,128)(2,1)S(1)}, u32[]{:S(2)}, u32[]{:S(2)}) collective-permute-start(bf16[96,16,128]{2,1,0:T(8,128)(2,1)S(1)} %pack.1), channel_id=1, source_target_pairs={{12,0},{97,1},{14,2},{99,3},{0,4},{101,5},{2,6},{103,7},{4,8},{105... | collective-permute-start | bytes 1179656 | tf_op jit(solution)/shard_map/ppermute | solution.py:319
  37.8 22.6 %collective-permute-start = (bf16[96,16,128]{2,1,0:T(8,128)(2,1)S(1)}, bf16[96,16,128]{2,1,0:T(8,128)(2,1)S(1)}, u32[]{:S(2)}, u32[]{:S(2)}) collective-permute-start(bf16[96,16,128]{2,1,0:T(8,128)(2,1)S(1)} %pack.1), channel_id=1, source_target_pairs={{2,0},{17,1},{4,2},{19,3},{6,4},{21,5},{8,6},{23,7},{10,8},{25,9},... | collective-permute-start | bytes 1179656 | tf_op jit(solution)/shard_map/ppermute | solution.py:319
  45.1 17.3 %collective-permute-start.1 = (bf16[96,16,128]{2,1,0:T(8,128)(2,1)S(1)}, bf16[96,16,128]{2,1,0:T(8,128)(2,1)S(1)}, u32[]{:S(2)}, u32[]{:S(2)}) collective-permute-start(bf16[96,16,128]{2,1,0:T(8,128)(2,1)S(1)} %pack.1), channel_id=1, source_target_pairs={{14,0},{113,1},{0,2},{115,3},{2,4},{117,5},{4,6},{119,7},{6,8},{12... | collective-permute-start | bytes 1179656 | tf_op jit(solution)/shard_map/ppermute | solution.py:319
  47.1 27.0 %copy-start.2 = (bf16[256,512]{1,0:T(8,128)(2,1)S(1)}, bf16[256,512]{1,0:T(8,128)(2,1)}, u32[]{:S(2)}) copy-start(bf16[256,512]{1,0:T(8,128)(2,1)} %block_ref.1) | copy-start | bytes 786436
  47.1 27.0 %copy-start.3 = (s32[256]{0:T(256)S(1)}, s32[256]{0:T(256)}, u32[]{:S(2)}) copy-start(s32[256]{0:T(256)} %param.11) | copy-start | bytes 3076
  47.1 31.9 %copy-start = (bf16[256,2048]{1,0:T(8,128)(2,1)S(1)}, bf16[256,2048]{1,0:T(8,128)(2,1)}, u32[]{:S(2)}) copy-start(bf16[256,2048]{1,0:T(8,128)(2,1)} %rows_ref.1) | copy-start | bytes 3145732
  47.1 31.9 %copy-start.1 = (bf16[16,128,128]{2,1,0:T(8,128)(2,1)S(1)}, bf16[16,128,128]{2,1,0:T(8,128)(2,1)}, u32[]{:S(2)}) copy-start(bf16[16,128,128]{2,1,0:T(8,128)(2,1)} %inv_ref.1) | copy-start | bytes 1572868
  47.1 24.2 %collective-permute-start.6 = (bf16[48,16,128]{2,1,0:T(8,128)(2,1)S(1)}, bf16[48,16,128]{2,1,0:T(8,128)(2,1)S(1)}, u32[]{:S(2)}, u32[]{:S(2)}) collective-permute-start(bf16[48,16,128]{2,1,0:T(8,128)(2,1)S(1)} %slice.12), channel_id=1, source_target_pairs={{4,0},{33,1},{6,2},{35,3},{8,4},{37,5},{10,6},{39,7},{12,8},{41,9}... | collective-permute-start | bytes 589832 | tf_op jit(solution)/shard_map/ppermute | solution.py:319
  52.3 19.2 %collective-permute-start.7 = (bf16[48,16,128]{2,1,0:T(8,128)(2,1)S(1)}, bf16[48,16,128]{2,1,0:T(8,128)(2,1)S(1)}, u32[]{:S(2)}, u32[]{:S(2)}) collective-permute-start(bf16[48,16,128]{2,1,0:T(8,128)(2,1)S(1)} %slice.13), channel_id=1, source_target_pairs={{12,0},{97,1},{14,2},{99,3},{0,4},{101,5},{2,6},{103,7},{4,8},{105... | collective-permute-start | bytes 589832 | tf_op jit(solution)/shard_map/ppermute | solution.py:319
  54.2 11.5 %collective-permute-start.4 = (bf16[96,16,128]{2,1,0:T(8,128)(2,1)S(1)}, bf16[96,16,128]{2,1,0:T(8,128)(2,1)S(1)}, u32[]{:S(2)}, u32[]{:S(2)}) collective-permute-start(bf16[96,16,128]{2,1,0:T(8,128)(2,1)S(1)} %collective-permute-done.2), channel_id=1, source_target_pairs={{2,0},{17,1},{4,2},{19,3},{6,4},{21,5},{8,6},{23,7},{10,8},{25,9},... | collective-permute-start | bytes 1179656 | tf_op jit(solution)/shard_map/ppermute | solution.py:319
  60.4 10.9 %collective-permute-start.5 = (bf16[96,16,128]{2,1,0:T(8,128)(2,1)S(1)}, bf16[96,16,128]{2,1,0:T(8,128)(2,1)S(1)}, u32[]{:S(2)}, u32[]{:S(2)}) collective-permute-start(bf16[96,16,128]{2,1,0:T(8,128)(2,1)S(1)} %collective-permute-done.3), channel_id=1, source_target_pairs={{14,0},{113,1},{0,2},{115,3},{2,4},{117,5},{4,6},{119,7},{6,8},{12... | collective-permute-start | bytes 1179656 | tf_op jit(solution)/shard_map/ppermute | solution.py:319
  71.5 7.6 %collective-permute-start.8 = (bf16[768,16,128]{2,1,0:T(8,128)(2,1)S(1)}, bf16[768,16,128]{2,1,0:T(8,128)(2,1)S(1)}, u32[]{:S(2)}, u32[]{:S(2)}) collective-permute-start(bf16[768,16,128]{2,1,0:T(8,128)(2,1)S(1)} %constant_dynamic-update-slice_fusion.mine_ref), channel_id=1, source_target_pairs={{0,1},{1,0},{2,3},{3,2},{4,5},{5,4},{6,7},{7,6},{8,9},{9,8},{10,11... | collective-permute-start | bytes 9437192 | tf_op jit(solution)/shard_map/ppermute | solution.py:332
